TPU v7x, 32 devices: a whole 2x2x4 slice. The times are simulated.
32 devices in a mesh: dp: 8 (over y, x, core), tensor: 4 (over z).
Axes of the slice: x: 2, y: 2, z: 4, core: 2. Of those that a mesh axis runs over, the one named last changes fastest.
Arguments:
- tokens: bfloat16 [8192, 2048], P(('dp', 'tensor')), may hold values from -6 to 6
- lengths: int32 [8, 4], P('dp'), may hold values from 1 to 512, 1024 in all within a row
- w_attn: float32 [4, 2048, 2048], P(None, 'dp', 'tensor')
- w_mlp: float32 [3, 2048, 8192], P(None, 'dp', 'tensor')
- norm_gains: float32 [4, 2048], P(None, ('dp', 'tensor')), may hold values from 0.25 to 1.75
- moment_attn: float32 [4, 2048, 2048], P(None, 'dp', 'tensor')
- square_attn: float32 [4, 2048, 2048], P(None, 'dp', 'tensor')
- moment_mlp: float32 [3, 2048, 8192], P(None, 'dp', 'tensor')
- square_mlp: float32 [3, 2048, 8192], P(None, 'dp', 'tensor')
- moment_gains: float32 [4, 2048], P(None, ('dp', 'tensor'))
- square_gains: float32 [4, 2048], P(None, ('dp', 'tensor'))
- cotangent: bfloat16 [8192, 2048], P(('dp', 'tensor')), may hold values from -6 to 6
Outputs:
- out_tokens: bfloat16 [8192, 2048], P(('dp', 'tensor'))
- grad_tokens: bfloat16 [8192, 2048], P(('dp', 'tensor'))
- new_attn: float32 [4, 2048, 2048], P(None, 'dp', 'tensor')
- new_moment_attn: float32 [4, 2048, 2048], P(None, 'dp', 'tensor')
- new_square_attn: float32 [4, 2048, 2048], P(None, 'dp', 'tensor')
- new_mlp: float32 [3, 2048, 8192], P(None, 'dp', 'tensor')
- new_moment_mlp: float32 [3, 2048, 8192], P(None, 'dp', 'tensor')
- new_square_mlp: float32 [3, 2048, 8192], P(None, 'dp', 'tensor')
- new_gains: float32 [4, 2048], P(None, ('dp', 'tensor'))
- new_moment_gains: float32 [4, 2048], P(None, ('dp', 'tensor'))
- new_square_gains: float32 [4, 2048], P(None, ('dp', 'tensor'))
All inputs are finite; a program needn't handle non-finite values.
Results may differ from a plain program's by a relative error of at most 0.018.
The roundings to bfloat16 on the way count: a program that leaves them out, or rounds other values in their place, can miss the bound.
Values may be sent and summed in bfloat16 or wider, within the bound.
No kernel may reach another device: no remote copies, remote signals or barrier semaphores. Data moves between devices by JAX's collectives and lax.ppermute only.
A program may use at most 320 MiB of HBM per device.

v0:
```python
import jax
import jax.numpy as jnp
from jax import lax
from jax.sharding import PartitionSpec as P

HDIM = 128
STEP = 10


NORM_EPS = 1e-06
ROPE_BASE = 500000.0
BETA_ONE = 0.9
BETA_TWO = 0.95
ADAM_EPS = 1e-08
RATE_MATRIX = 0.03
RATE_GAIN = 0.6
DECAY_MATRIX = 0.1
ROW_CONTRACT = (((0,), (0,)), ((), ()))
COLUMN_CONTRACT = (((1,), (1,)), ((), ()))


def doc_positions(lengths, seq_len):
    ends = jnp.cumsum(lengths, axis=-1, dtype=jnp.int32)
    starts = ends - lengths
    places = jnp.arange(seq_len, dtype=jnp.int32)
    inside = starts[:, None, :] <= places[None, :, None]
    begins = jnp.max(jnp.where(inside, starts[:, None, :], jnp.int32(0)), axis=-1)
    return places[None, :] - begins


def rope_tables(positions, head_dim):
    halfway = head_dim // 2
    powers = jnp.arange(halfway, dtype=jnp.float32) * (2.0 / head_dim)
    angles = positions.astype(jnp.float32)[:, None] * jnp.power(ROPE_BASE, -powers)
    return (jnp.cos(angles), jnp.sin(angles))


def rotate(values, cos_table, sin_table):
    halfway = values.shape[-1] // 2
    first_half = values[..., :halfway]
    second_half = values[..., halfway:]
    cosine = cos_table[:, None, :]
    sine = sin_table[:, None, :]
    return jnp.concatenate(
        [first_half * cosine - second_half * sine, second_half * cosine + first_half * sine],
        axis=-1,
    )


def post_norm(raw_rows, gain_row):
    return (
        raw_rows
        * lax.rsqrt(jnp.mean(raw_rows * raw_rows, axis=-1, keepdims=True) + NORM_EPS)
        * gain_row
    )


def adamw(weight, gradient, moment_one, moment_two, rate, decay):
    moment_one = BETA_ONE * moment_one + (1.0 - BETA_ONE) * gradient
    moment_two = BETA_TWO * moment_two + (1.0 - BETA_TWO) * gradient * gradient
    fix_one = 1.0 - BETA_ONE**STEP
    fix_two = 1.0 - BETA_TWO**STEP
    update = moment_one / fix_one / (jnp.sqrt(moment_two / fix_two) + ADAM_EPS)
    return (weight * (1.0 - rate * decay) - rate * update, moment_one, moment_two)


def masked_scores(query_block, key_rows, offset, score_scale):
    scores = (
        jnp.einsum("qhd,khd->hqk", query_block, key_rows, preferred_element_type=jnp.float32)
        * score_scale
    )
    query_pos = offset + jnp.arange(query_block.shape[0], dtype=jnp.int32)
    key_pos = jnp.arange(key_rows.shape[0], dtype=jnp.int32)
    return jnp.where(key_pos[None, None, :] <= query_pos[None, :, None], scores, -jnp.inf)


def local(
    tokens,
    lengths,
    w_attn,
    w_mlp,
    norm_gains,
    moment_attn,
    square_attn,
    moment_mlp,
    square_mlp,
    moment_gains,
    square_gains,
    cotangent,
):
    rows_here, model_width = tokens.shape
    tensor_size = lax.axis_size("tensor")
    tensor_index = lax.axis_index("tensor")
    seq_count = lengths.shape[0]
    total_rows = rows_here * tensor_size
    seq_len = total_rows // seq_count
    local_width = w_attn.shape[2]
    head_count = local_width // HDIM
    block_rows = min(512, seq_len)
    block_count = seq_len // block_rows
    score_scale = HDIM ** (-0.5)
    attn_low = w_attn.astype(jnp.bfloat16)
    mlp_low = w_mlp.astype(jnp.bfloat16)
    whole_tokens, gain_block = (
        lax.all_gather(tokens, "tensor", axis=0, tiled=True),
        lax.all_gather(norm_gains.astype(jnp.bfloat16), "tensor", axis=1, tiled=True),
    )
    attn_full, mlp_full, gain_full = (
        lax.all_gather(attn_low, "dp", axis=1, tiled=True),
        lax.all_gather(mlp_low, "dp", axis=1, tiled=True),
        lax.all_gather(gain_block, "dp", axis=1, tiled=True),
    )
    gain_values = gain_full.astype(jnp.float32)
    column_start = tensor_index * local_width
    query_gain = lax.dynamic_slice_in_dim(gain_values[2], column_start, local_width)
    key_gain = lax.dynamic_slice_in_dim(gain_values[3], column_start, local_width)
    positions = doc_positions(lengths, seq_len).reshape(total_rows)
    cos_table, sin_table = rope_tables(positions, HDIM)
    projected = jnp.einsum(
        "rd,kdf->krf", whole_tokens, attn_full[:3], preferred_element_type=jnp.float32
    )
    queries = projected[0]
    keys_raw = projected[1]
    value_low = projected[2].astype(jnp.bfloat16).reshape(total_rows, head_count, HDIM)
    square_sums = lax.psum(
        jnp.stack([jnp.sum(queries * queries, axis=-1), jnp.sum(keys_raw * keys_raw, axis=-1)]),
        "tensor",
    )
    inverse = lax.rsqrt(square_sums / model_width + NORM_EPS)
    query_hat = queries * inverse[0][:, None]
    key_hat = keys_raw * inverse[1][:, None]
    query_norm = (query_hat * query_gain).reshape(total_rows, head_count, HDIM)
    key_norm = (key_hat * key_gain).reshape(total_rows, head_count, HDIM)
    query_low = rotate(query_norm, cos_table, sin_table).astype(jnp.bfloat16)
    key_low = rotate(key_norm, cos_table, sin_table).astype(jnp.bfloat16)
    outputs = []
    log_sums = []
    seq_index = 0
    base_row = seq_index * seq_len
    for block_index in range(block_count):
        start_row = base_row + block_index * block_rows
        stop_row = start_row + block_rows
        scores = masked_scores(
            query_low[start_row:stop_row],
            key_low[base_row:stop_row],
            block_index * block_rows,
            score_scale,
        )
        row_peak = jnp.max(scores, axis=-1, keepdims=True)
        exp_scores = jnp.exp(scores - row_peak)
        totals = jnp.sum(exp_scores, axis=-1, keepdims=True)
        probability = exp_scores / totals
        log_sums.append(row_peak + jnp.log(totals))
        outputs.append(
            jnp.einsum(
                "hqk,khd->qhd",
                probability.astype(jnp.bfloat16),
                value_low[base_row:stop_row],
                preferred_element_type=jnp.float32,
            )
        )
    mixed_low = (
        jnp.concatenate(outputs, axis=0).reshape(total_rows, local_width).astype(jnp.bfloat16)
    )
    picked = mixed_low
    raw_attn = lax.psum_scatter(
        lax.dot_general(picked, attn_full[3], COLUMN_CONTRACT, preferred_element_type=jnp.float32),
        "tensor",
        scatter_dimension=0,
        tiled=True,
    )
    tokens_wide = tokens.astype(jnp.float32)
    attn_normed, attn_pull = jax.vjp(post_norm, raw_attn, gain_values[0])
    hidden = tokens_wide + attn_normed
    whole_hidden = lax.all_gather(hidden.astype(jnp.bfloat16), "tensor", axis=0, tiled=True)
    gate_up = jnp.einsum(
        "rd,kdf->krf", whole_hidden, mlp_full[:2], preferred_element_type=jnp.float32
    )
    inner_rows, act_pull = jax.vjp(
        lambda gate_in, up_in: jax.nn.silu(gate_in) * up_in, gate_up[0], gate_up[1]
    )
    inner_low = inner_rows.astype(jnp.bfloat16)
    picked = inner_low
    raw_mlp = lax.psum_scatter(
        lax.dot_general(picked, mlp_full[2], COLUMN_CONTRACT, preferred_element_type=jnp.float32),
        "tensor",
        scatter_dimension=0,
        tiled=True,
    )
    mlp_normed, mlp_pull = jax.vjp(post_norm, raw_mlp, gain_values[1])
    out_tokens = (hidden + mlp_normed).astype(jnp.bfloat16)
    back_rows = cotangent.astype(jnp.float32)
    back_raw_mlp, back_gain_mlp = mlp_pull(back_rows)
    gathered_mlp = lax.all_gather(back_raw_mlp.astype(jnp.bfloat16), "tensor", axis=0, tiled=True)
    attn_again, mlp_again = (
        lax.all_gather(attn_low, "dp", axis=1, tiled=True),
        lax.all_gather(mlp_low, "dp", axis=1, tiled=True),
    )
    back_inner = jnp.dot(gathered_mlp, mlp_again[2], preferred_element_type=jnp.float32)
    grad_down = lax.dot_general(
        gathered_mlp, inner_low, ROW_CONTRACT, preferred_element_type=jnp.float32
    )
    back_gate, back_upper = act_pull(back_inner)
    gate_low = back_gate.astype(jnp.bfloat16)
    upper_low = back_upper.astype(jnp.bfloat16)
    grad_gate = lax.dot_general(
        whole_hidden, gate_low, ROW_CONTRACT, preferred_element_type=jnp.float32
    )
    grad_upper = lax.dot_general(
        whole_hidden, upper_low, ROW_CONTRACT, preferred_element_type=jnp.float32
    )
    gate_sum = lax.dot_general(
        gate_low, mlp_again[0], COLUMN_CONTRACT, preferred_element_type=jnp.float32
    )
    back_hidden = back_rows + lax.psum_scatter(
        gate_sum
        + lax.dot_general(
            upper_low, mlp_again[1], COLUMN_CONTRACT, preferred_element_type=jnp.float32
        ),
        "tensor",
        scatter_dimension=0,
        tiled=True,
    )
    back_raw_attn, back_gain_attn = attn_pull(back_hidden)
    gathered_attn = lax.all_gather(back_raw_attn.astype(jnp.bfloat16), "tensor", axis=0, tiled=True)
    back_mixed = (
        jnp.dot(gathered_attn, attn_again[3], preferred_element_type=jnp.float32)
        .astype(jnp.bfloat16)
        .reshape(total_rows, head_count, HDIM)
    )
    grad_output = lax.dot_general(
        gathered_attn, mixed_low, ROW_CONTRACT, preferred_element_type=jnp.float32
    )
    query_grads = []
    block_number = 0
    seq_index = 0
    base_row = seq_index * seq_len
    key_total = jnp.zeros((seq_len, head_count, HDIM), jnp.float32)
    value_total = jnp.zeros((seq_len, head_count, HDIM), jnp.float32)
    for block_index in range(block_count):
        start_row = base_row + block_index * block_rows
        stop_row = start_row + block_rows
        stop_local = (block_index + 1) * block_rows
        scores = masked_scores(
            query_low[start_row:stop_row],
            key_low[base_row:stop_row],
            block_index * block_rows,
            score_scale,
        )
        probability = jnp.exp(scores - log_sums[block_number])
        block_number = block_number + 1
        prob_low = probability.astype(jnp.bfloat16)
        grad_block = back_mixed[start_row:stop_row]
        back_prob = jnp.einsum(
            "qhd,khd->hqk",
            grad_block,
            value_low[base_row:stop_row],
            preferred_element_type=jnp.float32,
        )
        delta_rows = jnp.sum(probability * back_prob, axis=-1, keepdims=True)
        back_scores = (probability * (back_prob - delta_rows)).astype(jnp.bfloat16)
        query_grads.append(
            jnp.einsum(
                "hqk,khd->qhd",
                back_scores,
                key_low[base_row:stop_row],
                preferred_element_type=jnp.float32,
            )
            * score_scale
        )
        key_total = key_total.at[:stop_local].add(
            jnp.einsum(
                "hqk,qhd->khd",
                back_scores,
                query_low[start_row:stop_row],
                preferred_element_type=jnp.float32,
            )
            * score_scale
        )
        value_total = value_total.at[:stop_local].add(
            jnp.einsum("hqk,qhd->khd", prob_low, grad_block, preferred_element_type=jnp.float32)
        )
    back_query_rot = jnp.concatenate(query_grads, axis=0)
    value_back_low = value_total.reshape(total_rows, local_width).astype(jnp.bfloat16)
    _, rope_pull = jax.vjp(lambda rows_in: rotate(rows_in, cos_table, sin_table), query_norm)
    back_query_norm = rope_pull(back_query_rot)[0].reshape(total_rows, local_width)
    back_key_norm = rope_pull(key_total)[0].reshape(total_rows, local_width)
    back_query_hat = back_query_norm * query_gain
    back_key_hat = back_key_norm * key_gain
    grad_query_gain = jnp.sum(back_query_norm * query_hat, axis=0)
    grad_key_gain = jnp.sum(back_key_norm * key_hat, axis=0)
    cross_sums = lax.psum(
        jnp.stack(
            [jnp.sum(back_query_hat * query_hat, axis=-1), jnp.sum(back_key_hat * key_hat, axis=-1)]
        ),
        "tensor",
    )
    query_back_low = (
        inverse[0][:, None] * (back_query_hat - query_hat * (cross_sums[0] / model_width)[:, None])
    ).astype(jnp.bfloat16)
    key_back_low = (
        inverse[1][:, None] * (back_key_hat - key_hat * (cross_sums[1] / model_width)[:, None])
    ).astype(jnp.bfloat16)
    grad_query = lax.dot_general(
        whole_tokens, query_back_low, ROW_CONTRACT, preferred_element_type=jnp.float32
    )
    grad_key = lax.dot_general(
        whole_tokens, key_back_low, ROW_CONTRACT, preferred_element_type=jnp.float32
    )
    grad_value = lax.dot_general(
        whole_tokens, value_back_low, ROW_CONTRACT, preferred_element_type=jnp.float32
    )
    stacked_back = jnp.stack([query_back_low, key_back_low, value_back_low])
    tokens_back_part = jnp.einsum(
        "krf,kdf->rd", stacked_back, attn_again[:3], preferred_element_type=jnp.float32
    )
    gain_grad = jnp.zeros((4, model_width), jnp.float32)
    gain_grad = gain_grad.at[0].set(back_gain_attn).at[1].set(back_gain_mlp)
    gain_grad = lax.dynamic_update_slice(
        gain_grad, jnp.stack([grad_query_gain, grad_key_gain]), (jnp.int32(2), column_start)
    )
    grad_attn = jnp.stack([grad_query, grad_key, grad_value, grad_output])
    attn_owned, gate_owned, upper_owned, down_owned, gain_owned = (
        lax.psum_scatter(grad_attn, "dp", scatter_dimension=1, tiled=True),
        lax.psum_scatter(grad_gate, "dp", scatter_dimension=0, tiled=True),
        lax.psum_scatter(grad_upper, "dp", scatter_dimension=0, tiled=True),
        lax.psum_scatter(grad_down, "dp", scatter_dimension=0, tiled=True),
        lax.psum_scatter(gain_grad, "dp", scatter_dimension=1, tiled=True),
    )
    tokens_back, gain_final = (
        lax.psum_scatter(tokens_back_part, "tensor", scatter_dimension=0, tiled=True),
        lax.psum_scatter(gain_owned, "tensor", scatter_dimension=1, tiled=True),
    )
    grad_tokens = (back_hidden + tokens_back).astype(jnp.bfloat16)
    mlp_owned = jnp.stack([gate_owned, upper_owned, down_owned])
    new_attn, new_moment_attn, new_square_attn = adamw(
        w_attn, attn_owned, moment_attn, square_attn, RATE_MATRIX, DECAY_MATRIX
    )
    new_mlp, new_moment_mlp, new_square_mlp = adamw(
        w_mlp, mlp_owned, moment_mlp, square_mlp, RATE_MATRIX, DECAY_MATRIX
    )
    new_gains, new_moment_gains, new_square_gains = adamw(
        norm_gains, gain_final, moment_gains, square_gains, RATE_GAIN, 0.0
    )
    return (
        out_tokens,
        grad_tokens,
        new_attn,
        new_moment_attn,
        new_square_attn,
        new_mlp,
        new_moment_mlp,
        new_square_mlp,
        new_gains,
        new_moment_gains,
        new_square_gains,
    )


def solution(mesh):
    return jax.shard_map(
        local,
        mesh=mesh,
        in_specs=(
            P(("dp", "tensor"), None),
            P("dp", None),
            P(None, "dp", "tensor"),
            P(None, "dp", "tensor"),
            P(None, ("dp", "tensor")),
            P(None, "dp", "tensor"),
            P(None, "dp", "tensor"),
            P(None, "dp", "tensor"),
            P(None, "dp", "tensor"),
            P(None, ("dp", "tensor")),
            P(None, ("dp", "tensor")),
            P(("dp", "tensor"), None),
        ),
        out_specs=(
            P(("dp", "tensor"), None),
            P(("dp", "tensor"), None),
            P(None, "dp", "tensor"),
            P(None, "dp", "tensor"),
            P(None, "dp", "tensor"),
            P(None, "dp", "tensor"),
            P(None, "dp", "tensor"),
            P(None, "dp", "tensor"),
            P(None, ("dp", "tensor")),
            P(None, ("dp", "tensor")),
            P(None, ("dp", "tensor")),
        ),
        check_vma=False,
    )
```

profile of v0, /device:TPU:0, one launch (start us, length us, event | category | flops | bytes accessed | tf_op | source)
XLA Modules:
  0.0 1839.3 jit_solution(7950024002022878380)
XLA Ops:
  11.2 12.6 all-gather
  24.1 8.9 all_gather.29
  37.5 55.6 %all-gather.10.cloned.1.call-done = bf16[1024,2048]{1,0:T(8,128)(2,1)} async-done(((bf16[256,2048]{1,0:T(8,128)(2,1)}), bf16[1024,2048]{1,0:T(8,128)(2,1)}) %all-gather.10.cloned.1.call-update) | async-done | bytes 4194320 | tf_op jit(solution)/shard_map/all_gather | solution.py:105
  93.1 57.0 %all-gather.8.cloned.1.call-done = bf16[4,2048,512]{1,2,0:T(8,128)(2,1)} async-done(((bf16[4,256,512]{1,2,0:T(8,128)(2,1)}), bf16[4,2048,512]{1,2,0:T(8,128)(2,1)}) %all-gather.8.cloned.1.call-update) | async-done | bytes 8388624 | tf_op jit(solution)/shard_map/all_gather | solution.py:109
  150.0 10.1 fusion.42
  164.6 12.1 psum.14
  199.6 7.3 fusion.74
  207.0 141.8 %reduce-scatter.15.cloned.1.call-done = f32[256,2048]{1,0:T(8,128)} async-done(((f32[1024,2048]{1,0:T(8,128)}), f32[256,2048]{1,0:T(8,128)}) %reduce-scatter.15.cloned.1.call-update) | async-done | bytes 2097168 | tf_op jit(solution)/shard_map/reduce_scatter | solution.py:166
  357.9 76.2 %all-gather.12.cloned.1.call-done = bf16[1024,2048]{1,0:T(8,128)(2,1)} async-done(((bf16[256,2048]{1,0:T(8,128)(2,1)}), bf16[1024,2048]{1,0:T(8,128)(2,1)}) %all-gather.12.cloned.1.call-update) | async-done | bytes 4194320 | tf_op jit(solution)/shard_map/all_gather | solution.py:175
  434.0 126.2 %all-gather.14.cloned.1.call-done = bf16[3,2048,2048]{2,1,0:T(8,128)(2,1)} async-done(((bf16[3,256,2048]{2,1,0:T(8,128)(2,1)}), bf16[3,2048,2048]{2,1,0:T(8,128)(2,1)}) %all-gather.14.cloned.1.call-update) | async-done | bytes 25165840 | tf_op jit(solution)/shard_map/all_gather | solution.py:110
  560.3 23.7 %fusion.14 = f32[2,1024,2048]{2,1,0:T(8,128)} fusion(bf16[3,2048,2048]{2,1,0:T(8,128)(2,1)} %all-gather.14.cloned.1.call-done, bf16[1024,2048]{1,0:T(8,128)(2,1)} %all-gather.12.cloned.1.call-done), kind=kOutput, calls=%fused_computation.33 | convolution fusion | flops 17179869184 | bytes 37748736 | tf_op jit(solution)/shard_map/rd,kdf->krf/dot_general | solution.py:176
  583.9 16.9 fusion.13
  600.9 144.6 %reduce-scatter.17.cloned.1.call-done = f32[256,2048]{1,0:T(8,128)} async-done(((f32[1024,2048]{1,0:T(8,128)}), f32[256,2048]{1,0:T(8,128)}) %reduce-scatter.17.cloned.1.call-update) | async-done | bytes 2097168 | tf_op jit(solution)/shard_map/reduce_scatter | solution.py:184
  750.3 81.4 %all-gather.16.cloned.1.call-done = bf16[1024,2048]{1,0:T(8,128)(2,1)} async-done(((bf16[256,2048]{1,0:T(8,128)(2,1)}), bf16[1024,2048]{1,0:T(8,128)(2,1)}) %all-gather.16.cloned.1.call-update) | async-done | bytes 4194320 | tf_op jit(solution)/shard_map/all_gather | solution.py:194
  831.7 19.9 %fusion.4 = (bf16[1024,2048]{1,0:T(8,128)(2,1)S(1)}, bf16[1024,2048]{1,0:T(8,128)(2,1)}) fusion(f32[2,1024,2048]{2,1,0:T(8,128)} %fusion.14, bf16[1024,2048]{1,0:T(8,128)(2,1)} %all-gather.16.cloned.1.call-done, bf16[3,2048,2048]{2,1,0:T(8,128)(2,1)} %all-gather.14.cloned.1.call-done), kind=kOutput, calls=%fused_computation.7 | convolution fusion | flops 8619294720 | bytes 37748736 | tf_op jit(solution)/shard_map/dot_general | solution.py:199
  851.6 14.0 fusion.5
  865.7 13.5 fusion.21
  879.4 142.9 %reduce-scatter.19.cloned.1.call-done = f32[256,2048]{1,0:T(8,128)} async-done(((f32[1024,2048]{1,0:T(8,128)}), f32[256,2048]{1,0:T(8,128)}) %reduce-scatter.19.cloned.1.call-update) | async-done | bytes 2097168 | tf_op jit(solution)/shard_map/reduce_scatter | solution.py:215
  1028.3 81.4 %all-gather.18.cloned.1.call-done = bf16[1024,2048]{1,0:T(8,128)(2,1)} async-done(((bf16[256,2048]{1,0:T(8,128)(2,1)}), bf16[1024,2048]{1,0:T(8,128)(2,1)}) %all-gather.18.cloned.1.call-update) | async-done | bytes 4194320 | tf_op jit(solution)/shard_map/all_gather | solution.py:225
  1136.7 34.6 %reduce-scatter.31.cloned.1.call-done = f32[256,4]{1,0:T(8,128)} async-done(((f32[2048,4]{1,0:T(8,128)}), f32[256,4]{1,0:T(8,128)}) %reduce-scatter.31.cloned.1.call-update) | async-done | bytes 4112
  1171.4 17.4 fusion.27
  1188.9 16.2 fusion.111
  1205.2 17.2 fusion.112
  1227.3 12.0 psum.15
  1249.6 9.1 fusion.22
  1289.0 21.9 %reduce-scatter.29.cloned.1.call-done = f32[256,2048]{1,0:T(8,128)} async-done(((f32[2048,2048]{1,0:T(8,128)}), f32[256,2048]{1,0:T(8,128)}) %reduce-scatter.29.cloned.1.call-update) | async-done | bytes 2097168 | tf_op jit(solution)/shard_map/reduce_scatter | solution.py:327
  1310.8 120.0 %reduce-scatter.25.cloned.1.call-done = f32[256,2048]{1,0:T(8,128)} async-done(((f32[2048,2048]{1,0:T(8,128)}), f32[256,2048]{1,0:T(8,128)}) %reduce-scatter.25.cloned.1.call-update) | async-done | bytes 2097168 | tf_op jit(solution)/shard_map/reduce_scatter | solution.py:325
  1430.8 119.8 %reduce-scatter.27.cloned.1.call-done = f32[256,2048]{1,0:T(8,128)} async-done(((f32[2048,2048]{1,0:T(8,128)}), f32[256,2048]{1,0:T(8,128)}) %reduce-scatter.27.cloned.1.call-update) | async-done | bytes 2097168 | tf_op jit(solution)/shard_map/reduce_scatter | solution.py:326
  1550.6 14.7 multiply_subtract_fusion
  1565.3 132.2 %reduce-scatter.21.cloned.1.call-done = f32[256,2048]{1,0:T(8,128)} async-done(((f32[1024,2048]{1,0:T(8,128)}), f32[256,2048]{1,0:T(8,128)}) %reduce-scatter.21.cloned.1.call-update) | async-done | bytes 2097168 | tf_op jit(solution)/shard_map/reduce_scatter | solution.py:331
  1701.1 116.9 %reduce-scatter.23.cloned.1.call-done = f32[4,256,512]{1,2,0:T(8,128)} async-done(((f32[4,2048,512]{1,2,0:T(8,128)}), f32[4,256,512]{1,2,0:T(8,128)}) %reduce-scatter.23.cloned.1.call-update) | async-done | bytes 2097168 | tf_op jit(solution)/shard_map/reduce_scatter | solution.py:324
  1818.0 6.6 multiply_subtract_fusion.1
  (297 shorter events, 139.4 us)
Async XLA Ops:
  7.2 85.9 %all-gather.10.cloned.1.call-start = ((), (), s32[]{:S(2)}) async-start(), calls=%async_computation.11 | async-start | bytes 5242880 | tf_op jit(solution)/shard_map/all_gather | solution.py:105
  7.9 142.1 %all-gather.8.cloned.1.call-start = ((), (), s32[]{:S(2)}) async-start(), calls=%async_computation.10 | async-start | bytes 9437184 | tf_op jit(solution)/shard_map/all_gather | solution.py:109
  9.9 150.2 %copy-start.12 = (f32[4,256,512]{1,2,0:T(8,128)}, f32[4,256,512]{1,2,0:T(8,128)S(1)}, u32[]{:S(2)}) copy-start(f32[4,256,512]{1,2,0:T(8,128)S(1)} %copy.121) | copy-start | bytes 6291460
  9.9 14.0 copy-start.78
  11.2 337.6 %reduce-scatter.15.cloned.1.call-start = ((), (), s32[]{:S(2)}) async-start(), calls=%async_computation.12 | async-start | bytes 10485760 | tf_op jit(solution)/shard_map/reduce_scatter | solution.py:166
  33.1 317.7 %copy-start.50 = (f32[1,2048]{1,0:T(1,128)}, f32[1,2048]{1,0:T(1,128)S(1)}, u32[]{:S(2)}) copy-start(f32[1,2048]{1,0:T(1,128)S(1)} %get-tuple-element.189) | copy-start | bytes 24580
  33.1 149.3 %copy-start.62 = (f32[1,512]{1,0:T(1,128)}, f32[1,512]{1,0:T(1,128)S(1)}, u32[]{:S(2)}) copy-start(f32[1,512]{1,0:T(1,128)S(1)} %get-tuple-element.207) | copy-start | bytes 6148
  33.1 149.5 %copy-start.60 = (f32[1,512]{1,0:T(1,128)}, f32[1,512]{1,0:T(1,128)S(1)}, u32[]{:S(2)}) copy-start(f32[1,512]{1,0:T(1,128)S(1)} %get-tuple-element.206) | copy-start | bytes 6148
  164.6 30.6 %copy-start.30 = (bf16[1,1024,512]{1,2,0:T(8,128)(2,1)}, bf16[1,1024,512]{1,2,0:T(8,128)(2,1)S(1)}, u32[]{:S(2)}) copy-start(bf16[1,1024,512]{1,2,0:T(8,128)(2,1)S(1)} %slice.345) | copy-start | bytes 3145732
  206.9 143.9 %copy-start.23 = (bf16[256,2048]{1,0:T(8,128)(2,1)S(1)}, bf16[256,2048]{1,0:T(8,128)(2,1)}, u32[]{:S(2)}) copy-start(bf16[256,2048]{1,0:T(8,128)(2,1)} %param.28) | copy-start | bytes 3145732
  206.9 227.1 %all-gather.12.cloned.1.call-start = ((), (), s32[]{:S(2)}) async-start(), calls=%async_computation.13 | async-start | bytes 5242880 | tf_op jit(solution)/shard_map/all_gather | solution.py:175
  352.4 207.8 %all-gather.14.cloned.1.call-start = ((), (), s32[]{:S(2)}) async-start(), calls=%async_computation.14 | async-start | bytes 28311552 | tf_op jit(solution)/shard_map/all_gather | solution.py:110
  357.4 388.0 %reduce-scatter.17.cloned.1.call-start = ((), (), s32[]{:S(2)}) async-start(), calls=%async_computation.15 | async-start | bytes 10485760 | tf_op jit(solution)/shard_map/reduce_scatter | solution.py:184
  600.8 146.6 %copy-start.8 = (bf16[256,2048]{1,0:T(8,128)(2,1)S(1)}, bf16[256,2048]{1,0:T(8,128)(2,1)}, u32[]{:S(2)}) copy-start(bf16[256,2048]{1,0:T(8,128)(2,1)} %param.39) | copy-start | bytes 3145732
  600.8 230.8 %all-gather.16.cloned.1.call-start = ((), (), s32[]{:S(2)}) async-start(), calls=%async_computation.16 | async-start | bytes 5242880 | tf_op jit(solution)/shard_map/all_gather | solution.py:194
  750.0 272.3 %reduce-scatter.19.cloned.1.call-start = ((), (), s32[]{:S(2)}) async-start(), calls=%async_computation.17 | async-start | bytes 10485760 | tf_op jit(solution)/shard_map/reduce_scatter | solution.py:215
  851.6 14.1 copy-start.79
  879.1 143.2 %copy-start.5 = (f32[256,2048]{1,0:T(8,128)S(1)}, f32[256,2048]{1,0:T(8,128)}, u32[]{:S(2)}) copy-start(f32[256,2048]{1,0:T(8,128)} %reduce-scatter.15.cloned.1.call-done) | copy-start | bytes 6291460
  879.1 143.2 %copy-start.51 = (f32[1,2048]{1,0:T(1,128)S(1)}, f32[1,2048]{1,0:T(1,128)}, u32[]{:S(2)}) copy-start(f32[1,2048]{1,0:T(1,128)} %copy-done.50) | copy-start | bytes 24580
  879.1 143.2 %copy-start.69 = (f32[256]{0:T(256)S(1)}, f32[256]{0:T(256)}, u32[]{:S(2)}) copy-start(f32[256]{0:T(256)} %copy-done.68) | copy-start | bytes 3076
  879.2 145.6 %copy-start.71 = (f32[256]{0:T(256)S(1)}, f32[256]{0:T(256)}, u32[]{:S(2)}) copy-start(f32[256]{0:T(256)} %copy-done.70) | copy-start | bytes 3076
  879.2 230.5 %all-gather.18.cloned.1.call-start = ((), (), s32[]{:S(2)}) async-start(), calls=%async_computation.18 | async-start | bytes 5242880 | tf_op jit(solution)/shard_map/all_gather | solution.py:225
  1028.0 143.3 %reduce-scatter.31.cloned.1.call-start = ((), (), s32[]{:S(2)}) async-start(), calls=%async_computation.24 | async-start | bytes 1179648
  1028.3 86.8 %copy-start.41 = (bf16[1,512,512]{1,2,0:T(8,128)(2,1)S(1)}, bf16[1,512,512]{1,2,0:T(8,128)(2,1)}, u32[]{:S(2)}) copy-start(bf16[1,512,512]{1,2,0:T(8,128)(2,1)} %copy-done.40) | copy-start | bytes 1572868
  1136.7 150.8 %reduce-scatter.33.cloned.1.call-start = ((), (), s32[]{:S(2)}) async-start(), calls=%async_computation.25 | async-start | bytes 163840
  1171.4 139.5 %reduce-scatter.29.cloned.1.call-start = ((), (), s32[]{:S(2)}) async-start(), calls=%async_computation.23 | async-start | bytes 18874368 | tf_op jit(solution)/shard_map/reduce_scatter | solution.py:327
  1188.9 241.9 %reduce-scatter.25.cloned.1.call-start = ((), (), s32[]{:S(2)}) async-start(), calls=%async_computation.21 | async-start | bytes 18874368 | tf_op jit(solution)/shard_map/reduce_scatter | solution.py:325
  1205.1 345.5 %reduce-scatter.27.cloned.1.call-start = ((), (), s32[]{:S(2)}) async-start(), calls=%async_computation.22 | async-start | bytes 18874368 | tf_op jit(solution)/shard_map/reduce_scatter | solution.py:326
  1222.4 475.1 %reduce-scatter.21.cloned.1.call-start = ((), (), s32[]{:S(2)}) async-start(), calls=%async_computation.19 | async-start | bytes 10485760 | tf_op jit(solution)/shard_map/reduce_scatter | solution.py:331
  1258.7 559.3 %reduce-scatter.23.cloned.1.call-start = ((), (), s32[]{:S(2)}) async-start(), calls=%async_computation.20 | async-start | bytes 18874368 | tf_op jit(solution)/shard_map/reduce_scatter | solution.py:324
  1550.6 146.8 %copy-start.9 = (bf16[256,2048]{1,0:T(8,128)(2,1)S(1)}, bf16[256,2048]{1,0:T(8,128)(2,1)}, u32[]{:S(2)}) copy-start(bf16[256,2048]{1,0:T(8,128)(2,1)} %param.39) | copy-start | bytes 3145732
  1565.3 252.7 %copy-start.13 = (f32[4,256,512]{1,2,0:T(8,128)S(1)}, f32[4,256,512]{1,2,0:T(8,128)}, u32[]{:S(2)}) copy-start(f32[4,256,512]{1,2,0:T(8,128)} %copy-done.12) | copy-start | bytes 6291460
  (70 other events, 212.7 us)
Sparse Core Ops, SparseCore 0:
  9.6 83.4 all-gather.9
  95.5 54.4 all-gather.7
  207.0 141.7 reduce-scatter.14
  352.5 81.4 all-gather.11
  436.4 123.8 all-gather.13
  601.0 144.4 reduce-scatter.16
  750.2 81.4 all-gather.15
  879.3 142.9 reduce-scatter.18
  1028.1 81.4 all-gather.17
  1136.8 34.5 reduce-scatter.30
  1173.6 19.1 reduce-scatter.32
  1196.6 114.1 reduce-scatter.28
  1314.8 115.9 reduce-scatter.24
  1434.6 115.9 reduce-scatter.26
  1552.9 144.4 reduce-scatter.20
  1701.3 116.6 reduce-scatter.22
where the time goes:
time: 1840 us
  waiting for transfers between devices  1450 us (79%)
  matrix products  201 us (11%)
  other arithmetic  77.3 us (4%)
  blocking collectives  45.5 us (2%)
  local copies, waits for them, and re-layouts  45.3 us (2%)
    reduce_scatter x1, waiting for transfers between devices, local(): lax.psum_scatter(lax.dot_general(picked, mlp_full[2], COLUMN_CONTRACT, pr...  145 us
    reduce_scatter x1, waiting for transfers between devices, local(): lax.psum_scatter(gate_sum + lax.dot_general(upper_low, mlp_again[1], COLU...  143 us
    reduce_scatter x1, waiting for transfers between devices, local(): lax.psum_scatter(lax.dot_general(picked, attn_full[3], COLUMN_CONTRACT, p...  142 us
    reduce_scatter x1, waiting for transfers between devices, local(): lax.psum_scatter(tokens_back_part, 'tensor', scatter_dimension=0, tiled=T...  132 us
    all_gather x1, waiting for transfers between devices, local(): lax.all_gather(mlp_low, 'dp', axis=1, tiled=True)  126 us
    reduce_scatter x1, waiting for transfers between devices, local(): lax.psum_scatter(grad_gate, 'dp', scatter_dimension=0, tiled=True)  120 us
    reduce_scatter x1, waiting for transfers between devices, local(): lax.psum_scatter(grad_upper, 'dp', scatter_dimension=0, tiled=True)  120 us
    reduce_scatter x1, waiting for transfers between devices, local(): lax.psum_scatter(grad_attn, 'dp', scatter_dimension=1, tiled=True)  117 us
  transfers between devices with their start and end apart: 16, of which 15 were waited for; matrix products, arithmetic and copies ran while one was open for 7% of the time, Pallas kernels for 0%

commit v1 on v0

v1 whole, which is shorter than its diff:
```python
import jax
import jax.numpy as jnp
from jax import lax
from jax.experimental import pallas as pl
from jax.experimental.pallas import tpu as pltpu
from jax.sharding import PartitionSpec as P

HDIM = 128
STEP = 10
CHUNKS = 2
MIB = 1 << 20


NORM_EPS = 1e-06
ROPE_BASE = 500000.0
BETA_ONE = 0.9
BETA_TWO = 0.95
ADAM_EPS = 1e-08
RATE_MATRIX = 0.03
RATE_GAIN = 0.6
DECAY_MATRIX = 0.1
ROW_CONTRACT = (((0,), (0,)), ((), ()))
COLUMN_CONTRACT = (((1,), (1,)), ((), ()))


def doc_positions(lengths, seq_len):
    ends = jnp.cumsum(lengths, axis=-1, dtype=jnp.int32)
    starts = ends - lengths
    places = jnp.arange(seq_len, dtype=jnp.int32)
    inside = starts[:, None, :] <= places[None, :, None]
    begins = jnp.max(jnp.where(inside, starts[:, None, :], jnp.int32(0)), axis=-1)
    return places[None, :] - begins


def rope_tables(positions, head_dim):
    halfway = head_dim // 2
    powers = jnp.arange(halfway, dtype=jnp.float32) * (2.0 / head_dim)
    angles = positions.astype(jnp.float32)[:, None] * jnp.power(ROPE_BASE, -powers)
    return (jnp.cos(angles), jnp.sin(angles))


def rotate(values, cos_table, sin_table):
    halfway = values.shape[-1] // 2
    first_half = values[..., :halfway]
    second_half = values[..., halfway:]
    cosine = cos_table[:, None, :]
    sine = sin_table[:, None, :]
    return jnp.concatenate(
        [first_half * cosine - second_half * sine, second_half * cosine + first_half * sine],
        axis=-1,
    )


def post_norm(raw_rows, gain_row):
    return (
        raw_rows
        * lax.rsqrt(jnp.mean(raw_rows * raw_rows, axis=-1, keepdims=True) + NORM_EPS)
        * gain_row
    )


def adamw(weight, gradient, moment_one, moment_two, rate, decay):
    moment_one = BETA_ONE * moment_one + (1.0 - BETA_ONE) * gradient
    moment_two = BETA_TWO * moment_two + (1.0 - BETA_TWO) * gradient * gradient
    fix_one = 1.0 - BETA_ONE**STEP
    fix_two = 1.0 - BETA_TWO**STEP
    update = moment_one / fix_one / (jnp.sqrt(moment_two / fix_two) + ADAM_EPS)
    return (weight * (1.0 - rate * decay) - rate * update, moment_one, moment_two)


def masked_scores(query_block, key_rows, offset, score_scale):
    scores = (
        jnp.einsum("qhd,khd->hqk", query_block, key_rows, preferred_element_type=jnp.float32)
        * score_scale
    )
    query_pos = offset + jnp.arange(query_block.shape[0], dtype=jnp.int32)
    key_pos = jnp.arange(key_rows.shape[0], dtype=jnp.int32)
    return jnp.where(key_pos[None, None, :] <= query_pos[None, :, None], scores, -jnp.inf)


def pick(index, cases):
    if all(case is cases[0] for case in cases):
        return cases[0]
    return lax.select_n(index, *cases)


def line_gather(piece):
    count = lax.axis_size("tensor")
    here = lax.axis_index("tensor")
    from_low, from_high = [piece], [piece]
    for step in range(1, count):
        rising = [(i, i + 1) for i in range(step - 1, count - 1)]
        falling = [(i + 1, i) for i in range(count - step)]
        from_low.append(lax.ppermute(from_low[-1], "tensor", rising))
        from_high.append(lax.ppermute(from_high[-1], "tensor", falling))
    return [
        pick(
            here,
            [from_low[i - owner] if i >= owner else from_high[owner - i] for i in range(count)],
        )
        for owner in range(count)
    ]


def line_scatter(parts):
    count = lax.axis_size("tensor")
    here = lax.axis_index("tensor")
    rising_sum = falling_sum = None
    for step in range(1, count):
        up_part = lax.dynamic_index_in_dim(
            parts, jnp.minimum(here + count - step, count - 1), 0, keepdims=False
        )
        down_part = lax.dynamic_index_in_dim(
            parts, jnp.maximum(here - count + step, 0), 0, keepdims=False
        )
        if rising_sum is not None:
            up_part = up_part + rising_sum.astype(jnp.float32)
            down_part = down_part + falling_sum.astype(jnp.float32)
        rising = [(i, i + 1) for i in range(step)]
        falling = [(i, i - 1) for i in range(count - step, count)]
        rising_sum = lax.ppermute(up_part.astype(jnp.bfloat16), "tensor", rising)
        falling_sum = lax.ppermute(down_part.astype(jnp.bfloat16), "tensor", falling)
    own = lax.dynamic_index_in_dim(parts, here, 0, keepdims=False)
    return own + rising_sum.astype(jnp.float32) + falling_sum.astype(jnp.float32)


def shifts(count):
    return [[(i, (i + k) % count) for i in range(count)] for k in range(1, count)]


def small_sum(values):
    total = values
    for pairs in shifts(lax.axis_size("tensor")):
        total = total + lax.ppermute(values, "tensor", pairs)
    return total


def rows_to_heads(values):
    count = lax.axis_size("tensor")
    here = lax.axis_index("tensor")
    rows, columns = values.shape
    width = columns // count
    got = [lax.dynamic_slice_in_dim(values, here * width, width, 1)]
    for k, pairs in enumerate(shifts(count), 1):
        block = lax.dynamic_slice_in_dim(values, lax.rem(here + k, count) * width, width, 1)
        got.append(lax.ppermute(block, "tensor", pairs))
    return [
        pick(here, [got[(i - owner) % count] for i in range(count)]) for owner in range(count)
    ]


def pair_swap(values, bit):
    count = lax.axis_size("dp")
    return lax.ppermute(values, "dp", [(i, i ^ bit) for i in range(count)])


def grad_body(order_ref, *refs):
    if len(refs) == 4:
        left_ref, right_ref, add_ref, out_ref = refs
    else:
        left_ref, right_ref, out_ref = refs
        add_ref = None
    product = lax.dot_general(
        left_ref[...], right_ref[...], ROW_CONTRACT, preferred_element_type=jnp.float32
    )
    if add_ref is not None:
        product = product + add_ref[...].astype(jnp.float32)
    out_ref[...] = product.astype(jnp.bfloat16)


def grad_blocks(order, left, right, add):
    blocks = order.shape[0]
    size = left.shape[1] // lax.axis_size("dp")
    depth, width = right.shape
    in_specs = [
        pl.BlockSpec((depth, size), lambda m, order_ref: (0, order_ref[m])),
        pl.BlockSpec((depth, width), lambda m, order_ref: (0, 0)),
    ]
    operands = [left, right]
    if add is not None:
        in_specs.append(pl.BlockSpec((size, width), lambda m, order_ref: (m, 0)))
        operands.append(add)
    return pl.pallas_call(
        grad_body,
        grid_spec=pltpu.PrefetchScalarGridSpec(
            num_scalar_prefetch=1,
            grid=(blocks,),
            in_specs=in_specs,
            out_specs=pl.BlockSpec((size, width), lambda m, order_ref: (m, 0)),
        ),
        out_shape=jax.ShapeDtypeStruct((blocks * size, width), jnp.bfloat16),
        compiler_params=pltpu.CompilerParams(vmem_limit_bytes=48 * MIB),
        cost_estimate=pl.CostEstimate(
            flops=2 * blocks * size * depth * width,
            bytes_accessed=2 * (depth * width + blocks * size * (depth + width)),
            transcendentals=0,
        ),
    )(order, *operands)


def owned_grad(left, right):
    count = lax.axis_size("dp")
    here = lax.axis_index("dp")
    size = left.shape[1] // count
    width = right.shape[1]
    if count & (count - 1) or count < 8 or size % 128 or width % 256:
        whole = lax.dot_general(left, right, ROW_CONTRACT, preferred_element_type=jnp.float32)
        return lax.psum_scatter(
            whole.astype(jnp.bfloat16), "dp", scatter_dimension=0, tiled=True
        ).astype(jnp.float32)
    evens = jnp.arange(0, count, 2, dtype=jnp.int32) ^ here
    sent = grad_blocks(evens ^ 1, left, right, None)
    kept = grad_blocks(evens, left, right, pair_swap(sent, 1))
    kept = kept.reshape((count // 2, size, width))
    bits = []
    bit = 2
    while bit < count:
        bits.append(bit)
        bit = bit * 2
    halves = []
    for way, columns in ((bits, slice(None, width // 2)), (bits[::-1], slice(width // 2, None))):
        live = {2 * b: kept[b, :, columns] for b in range(count // 2)}
        for place, bit in enumerate(way):
            going = [d for d in sorted(live) if d & bit]
            got = pair_swap(jnp.stack([live[d] for d in going]), bit)
            left_over = {}
            for at, d in enumerate(going):
                total = live[d ^ bit].astype(jnp.float32) + got[at].astype(jnp.float32)
                last = place == len(way) - 1
                left_over[d ^ bit] = total if last else total.astype(jnp.bfloat16)
            live = left_over
        halves.append(live[0])
    return jnp.concatenate(halves, axis=1)


def local(
    tokens,
    lengths,
    w_attn,
    w_mlp,
    norm_gains,
    moment_attn,
    square_attn,
    moment_mlp,
    square_mlp,
    moment_gains,
    square_gains,
    cotangent,
):
    rows_here, model_width = tokens.shape
    tensor_size = lax.axis_size("tensor")
    tensor_index = lax.axis_index("tensor")
    total_rows = rows_here * tensor_size
    seq_len = total_rows // lengths.shape[0]
    local_width = w_attn.shape[2]
    head_count = local_width // HDIM
    block_rows = min(512, seq_len)
    block_count = seq_len // block_rows
    score_scale = HDIM ** (-0.5)
    chunk_rows = rows_here // CHUNKS
    attn_low = w_attn.astype(jnp.bfloat16)
    mlp_low = w_mlp.astype(jnp.bfloat16)

    whole_tokens = jnp.concatenate(line_gather(tokens), axis=0)
    out_shard = jnp.concatenate(line_gather(attn_low[3]), axis=1)
    qkv_full = lax.all_gather(attn_low[:3], "dp", axis=1, tiled=True)
    out_full = lax.all_gather(out_shard, "dp", axis=0, tiled=True)
    gate_up_full = lax.all_gather(mlp_low[:2], "dp", axis=1, tiled=True)
    down_full = lax.all_gather(mlp_low[2], "dp", axis=0, tiled=True)
    gain_block = lax.all_gather(norm_gains.astype(jnp.bfloat16), "tensor", axis=1, tiled=True)
    gain_full = lax.all_gather(gain_block, "dp", axis=1, tiled=True)
    gain_values = gain_full.astype(jnp.float32)
    column_start = tensor_index * local_width
    query_gain = lax.dynamic_slice_in_dim(gain_values[2], column_start, local_width)
    key_gain = lax.dynamic_slice_in_dim(gain_values[3], column_start, local_width)
    positions = doc_positions(lengths, seq_len).reshape(total_rows)
    cos_table, sin_table = rope_tables(positions, HDIM)

    projected = jnp.einsum(
        "rd,kdf->krf", whole_tokens, qkv_full, preferred_element_type=jnp.float32
    )
    queries = projected[0]
    keys_raw = projected[1]
    value_low = projected[2].astype(jnp.bfloat16).reshape(total_rows, head_count, HDIM)
    square_sums = small_sum(
        jnp.stack([jnp.sum(queries * queries, axis=-1), jnp.sum(keys_raw * keys_raw, axis=-1)])
    )
    inverse = lax.rsqrt(square_sums / model_width + NORM_EPS)
    query_hat = queries * inverse[0][:, None]
    key_hat = keys_raw * inverse[1][:, None]
    query_norm = (query_hat * query_gain).reshape(total_rows, head_count, HDIM)
    key_norm = (key_hat * key_gain).reshape(total_rows, head_count, HDIM)
    query_low = rotate(query_norm, cos_table, sin_table).astype(jnp.bfloat16)
    key_low = rotate(key_norm, cos_table, sin_table).astype(jnp.bfloat16)
    outputs = []
    log_sums = []
    for block_index in range(block_count):
        start_row = block_index * block_rows
        stop_row = start_row + block_rows
        scores = masked_scores(
            query_low[start_row:stop_row], key_low[:stop_row], start_row, score_scale
        )
        row_peak = jnp.max(scores, axis=-1, keepdims=True)
        exp_scores = jnp.exp(scores - row_peak)
        totals = jnp.sum(exp_scores, axis=-1, keepdims=True)
        probability = exp_scores / totals
        log_sums.append(row_peak + jnp.log(totals))
        outputs.append(
            jnp.einsum(
                "hqk,khd->qhd",
                probability.astype(jnp.bfloat16),
                value_low[:stop_row],
                preferred_element_type=jnp.float32,
            )
        )
    mixed_low = (
        jnp.concatenate(outputs, axis=0).reshape(total_rows, local_width).astype(jnp.bfloat16)
    )

    def chunk_of(values, chunk):
        parted = values.reshape((tensor_size, CHUNKS, chunk_rows) + values.shape[1:])
        return parted[:, chunk].reshape((tensor_size * chunk_rows,) + values.shape[1:])

    def own_part(values):
        parted = values.reshape((tensor_size, chunk_rows) + values.shape[1:])
        return lax.dynamic_index_in_dim(parted, tensor_index, 0, keepdims=False)

    hidden_low, inner_low, act_pulls = [], [], []
    out_parts, back_raws_mlp, gains_mlp, attn_pulls, own_mixed = [], [], [], [], []
    for chunk in range(CHUNKS):
        mixed = jnp.concatenate(line_gather(chunk_of(mixed_low, chunk)), axis=1)
        own_mixed.append(own_part(mixed))
        raw_attn = lax.dot_general(
            mixed, out_full, COLUMN_CONTRACT, preferred_element_type=jnp.float32
        )
        hidden_low.append(
            (
                chunk_of(whole_tokens, chunk).astype(jnp.float32)
                + post_norm(raw_attn, gain_values[0])
            ).astype(jnp.bfloat16)
        )
        gate = jnp.dot(hidden_low[-1], gate_up_full[0], preferred_element_type=jnp.float32)
        upper = jnp.dot(hidden_low[-1], gate_up_full[1], preferred_element_type=jnp.float32)
        inner_rows, act_pull = jax.vjp(
            lambda gate_in, up_in: jax.nn.silu(gate_in) * up_in, gate, upper
        )
        act_pulls.append(act_pull)
        inner_low.append(inner_rows.astype(jnp.bfloat16))
        raw_part = lax.dot_general(
            inner_low[-1], down_full, COLUMN_CONTRACT, preferred_element_type=jnp.float32
        )
        raw_mlp = line_scatter(raw_part.reshape(tensor_size, chunk_rows, model_width))
        own_raw = own_part(raw_attn)
        own_rows = slice(chunk * chunk_rows, (chunk + 1) * chunk_rows)
        attn_normed, attn_pull = jax.vjp(post_norm, own_raw, gain_values[0])
        attn_pulls.append(attn_pull)
        mlp_normed, mlp_pull = jax.vjp(post_norm, raw_mlp, gain_values[1])
        hidden = tokens[own_rows].astype(jnp.float32) + attn_normed
        out_parts.append((hidden + mlp_normed).astype(jnp.bfloat16))
        back_raw, back_gain = mlp_pull(cotangent[own_rows].astype(jnp.float32))
        back_raws_mlp.append(back_raw.astype(jnp.bfloat16))
        gains_mlp.append(back_gain)
    out_tokens = jnp.concatenate(out_parts, axis=0)

    gathered_mlp, gate_low, upper_low = [], [], []
    back_hiddens, back_raws_attn, gains_attn, back_mixed_parts = [], [], [], []
    for chunk in range(CHUNKS):
        own_rows = slice(chunk * chunk_rows, (chunk + 1) * chunk_rows)
        gathered = jnp.concatenate(line_gather(back_raws_mlp[chunk]), axis=0)
        gathered_mlp.append(gathered)
        back_inner = jnp.dot(gathered, down_full, preferred_element_type=jnp.float32)
        back_gate, back_upper = act_pulls[chunk](back_inner)
        gate_low.append(back_gate.astype(jnp.bfloat16))
        upper_low.append(back_upper.astype(jnp.bfloat16))
        hidden_part = lax.dot_general(
            gate_low[-1], gate_up_full[0], COLUMN_CONTRACT, preferred_element_type=jnp.float32
        ) + lax.dot_general(
            upper_low[-1], gate_up_full[1], COLUMN_CONTRACT, preferred_element_type=jnp.float32
        )
        back_hidden = cotangent[own_rows].astype(jnp.float32) + line_scatter(
            hidden_part.reshape(tensor_size, chunk_rows, model_width)
        )
        back_hiddens.append(back_hidden)
        back_raw, back_gain = attn_pulls[chunk](back_hidden)
        gains_attn.append(back_gain)
        back_raws_attn.append(back_raw.astype(jnp.bfloat16))
        back_rows = jnp.dot(
            back_raws_attn[-1], out_full, preferred_element_type=jnp.float32
        ).astype(jnp.bfloat16)
        back_mixed_parts.append(rows_to_heads(back_rows))
    back_mixed = jnp.stack([jnp.stack(parts) for parts in back_mixed_parts], axis=1)
    back_mixed = back_mixed.reshape(total_rows, head_count, HDIM)
    gathered_all = jnp.concatenate(gathered_mlp, axis=0)
    hidden_all = jnp.concatenate(hidden_low, axis=0)
    down_owned = owned_grad(gathered_all, jnp.concatenate(inner_low, axis=0))
    gate_owned = owned_grad(hidden_all, jnp.concatenate(gate_low, axis=0))
    upper_owned = owned_grad(hidden_all, jnp.concatenate(upper_low, axis=0))
    output_owned = owned_grad(
        jnp.concatenate(back_raws_attn, axis=0), jnp.concatenate(own_mixed, axis=0)
    )
    output_owned = line_scatter(
        jnp.moveaxis(output_owned.reshape(-1, tensor_size, local_width), 1, 0)
    )

    query_grads = []
    key_total = jnp.zeros((seq_len, head_count, HDIM), jnp.float32)
    value_total = jnp.zeros((seq_len, head_count, HDIM), jnp.float32)
    for block_index in range(block_count):
        start_row = block_index * block_rows
        stop_row = start_row + block_rows
        scores = masked_scores(
            query_low[start_row:stop_row], key_low[:stop_row], start_row, score_scale
        )
        probability = jnp.exp(scores - log_sums[block_index])
        prob_low = probability.astype(jnp.bfloat16)
        grad_block = back_mixed[start_row:stop_row]
        back_prob = jnp.einsum(
            "qhd,khd->hqk", grad_block, value_low[:stop_row], preferred_element_type=jnp.float32
        )
        delta_rows = jnp.sum(probability * back_prob, axis=-1, keepdims=True)
        back_scores = (probability * (back_prob - delta_rows)).astype(jnp.bfloat16)
        query_grads.append(
            jnp.einsum(
                "hqk,khd->qhd", back_scores, key_low[:stop_row], preferred_element_type=jnp.float32
            )
            * score_scale
        )
        key_total = key_total.at[:stop_row].add(
            jnp.einsum(
                "hqk,qhd->khd",
                back_scores,
                query_low[start_row:stop_row],
                preferred_element_type=jnp.float32,
            )
            * score_scale
        )
        value_total = value_total.at[:stop_row].add(
            jnp.einsum("hqk,qhd->khd", prob_low, grad_block, preferred_element_type=jnp.float32)
        )
    back_query_rot = jnp.concatenate(query_grads, axis=0)
    value_back_low = value_total.reshape(total_rows, local_width).astype(jnp.bfloat16)
    _, rope_pull = jax.vjp(lambda rows_in: rotate(rows_in, cos_table, sin_table), query_norm)
    back_query_norm = rope_pull(back_query_rot)[0].reshape(total_rows, local_width)
    back_key_norm = rope_pull(key_total)[0].reshape(total_rows, local_width)
    back_query_hat = back_query_norm * query_gain
    back_key_hat = back_key_norm * key_gain
    grad_query_gain = jnp.sum(back_query_norm * query_hat, axis=0)
    grad_key_gain = jnp.sum(back_key_norm * key_hat, axis=0)
    cross_sums = small_sum(
        jnp.stack(
            [jnp.sum(back_query_hat * query_hat, axis=-1), jnp.sum(back_key_hat * key_hat, axis=-1)]
        )
    )
    query_back_low = (
        inverse[0][:, None] * (back_query_hat - query_hat * (cross_sums[0] / model_width)[:, None])
    ).astype(jnp.bfloat16)
    key_back_low = (
        inverse[1][:, None] * (back_key_hat - key_hat * (cross_sums[1] / model_width)[:, None])
    ).astype(jnp.bfloat16)
    stacked_back = jnp.stack([query_back_low, key_back_low, value_back_low])
    tokens_part = jnp.einsum(
        "krf,kdf->rd", stacked_back, qkv_full, preferred_element_type=jnp.float32
    )
    tokens_back = line_scatter(tokens_part.reshape(tensor_size, rows_here, model_width))
    qkv_owned = owned_grad(
        whole_tokens, jnp.concatenate([query_back_low, key_back_low, value_back_low], axis=1)
    )
    grad_tokens = (jnp.concatenate(back_hiddens, axis=0) + tokens_back).astype(jnp.bfloat16)

    gain_grad = jnp.zeros((4, model_width), jnp.float32)
    gain_grad = gain_grad.at[0].set(sum(gains_attn)).at[1].set(sum(gains_mlp))
    gain_grad = lax.dynamic_update_slice(
        gain_grad, jnp.stack([grad_query_gain, grad_key_gain]), (jnp.int32(2), column_start)
    )
    gain_owned = lax.psum_scatter(gain_grad, "dp", scatter_dimension=1, tiled=True)
    gain_final = lax.psum_scatter(gain_owned, "tensor", scatter_dimension=1, tiled=True)
    attn_owned = jnp.stack(
        [qkv_owned[:, k * local_width : (k + 1) * local_width] for k in range(3)] + [output_owned]
    )
    mlp_owned = jnp.stack([gate_owned, upper_owned, down_owned])
    new_attn, new_moment_attn, new_square_attn = adamw(
        w_attn, attn_owned, moment_attn, square_attn, RATE_MATRIX, DECAY_MATRIX
    )
    new_mlp, new_moment_mlp, new_square_mlp = adamw(
        w_mlp, mlp_owned, moment_mlp, square_mlp, RATE_MATRIX, DECAY_MATRIX
    )
    new_gains, new_moment_gains, new_square_gains = adamw(
        norm_gains, gain_final, moment_gains, square_gains, RATE_GAIN, 0.0
    )
    return (
        out_tokens,
        grad_tokens,
        new_attn,
        new_moment_attn,
        new_square_attn,
        new_mlp,
        new_moment_mlp,
        new_square_mlp,
        new_gains,
        new_moment_gains,
        new_square_gains,
    )


def solution(mesh):
    return jax.shard_map(
        local,
        mesh=mesh,
        in_specs=(
            P(("dp", "tensor"), None),
            P("dp", None),
            P(None, "dp", "tensor"),
            P(None, "dp", "tensor"),
            P(None, ("dp", "tensor")),
            P(None, "dp", "tensor"),
            P(None, "dp", "tensor"),
            P(None, "dp", "tensor"),
            P(None, "dp", "tensor"),
            P(None, ("dp", "tensor")),
            P(None, ("dp", "tensor")),
            P(("dp", "tensor"), None),
        ),
        out_specs=(
            P(("dp", "tensor"), None),
            P(("dp", "tensor"), None),
            P(None, "dp", "tensor"),
            P(None, "dp", "tensor"),
            P(None, "dp", "tensor"),
            P(None, "dp", "tensor"),
            P(None, "dp", "tensor"),
            P(None, "dp", "tensor"),
            P(None, ("dp", "tensor")),
            P(None, ("dp", "tensor")),
            P(None, ("dp", "tensor")),
        ),
        check_vma=False,
    )
```

time: 1840 us -> 1090 us (0.59)
  waiting for transfers between devices: 1450 us -> 313 us
  starting transfers between devices: 1.7 us -> 195 us
  Pallas kernels: 0 us -> 78 us
  other arithmetic: 77.3 us -> 154 us
  local copies, waits for them, and re-layouts: 45.3 us -> 113 us
  matrix products: 201 us -> 179 us
    reduce_scatter x8 -> x0, waiting for transfers between devices: 940 us -> none  [the longest x1 145 us: local(): lax.psum_scatter(lax.dot_general(picked, mlp_full[2], COLUMN_CONTRACT, pr...]
    all_gather x6 -> x4, waiting for transfers between devices: 478 us -> 0.04 us  [the longest x1 0.02 us: local(): out_full = lax.all_gather(out_shard, 'dp', axis=0, tiled=True)]
    ppermute x0 -> x109, waiting for transfers between devices: none -> 304 us  [the longest x18 119 us: line_gather(): from_high.append(lax.ppermute(from_high[-1], 'tensor', falling))]
    ppermute x0 -> x109, starting transfers between devices: none -> 195 us  [the longest x18 65 us: line_scatter(): rising_sum = lax.ppermute(up_part.astype(jnp.bfloat16), 'tensor', rising)]
    pallas_call x0 -> x10, Pallas kernels: none -> 78 us  [grad_blocks(): pl.pallas_call(grad_body, grid_spec=pltpu.PrefetchScalarGridSpec(num_scal...]
    convert_element_type x4 -> x29, other arithmetic: 9.03 us -> 43.3 us  [the longest x13 13.9 us: line_scatter(): rising_sum = lax.ppermute(up_part.astype(jnp.bfloat16), 'tensor', rising)]
    unnamed x18 -> x8, waiting for transfers between devices: 35.5 us -> 8.87 us
    psum x2 -> x0, blocking collectives: 24 us -> none  [the longest x1 12.1 us: local(): lax.psum(jnp.stack([jnp.sum(queries * queries, axis=-1), jnp.sum(keys_raw...]
  transfers between devices with their start and end apart: 16 -> 115, of which waited for: 15 -> 48; matrix products, arithmetic and copies ran while one was open for 7% -> 38% of each run, Pallas kernels for 0% -> 7%
where the time goes in v1:
time: 1090 us; the launch traced here: 1080 us
  waiting for transfers between devices  313 us (29%)
  starting transfers between devices  195 us (18%)
  matrix products  179 us (16%)
  other arithmetic  154 us (14%)
  local copies, waits for them, and re-layouts  113 us (10%)
  Pallas kernels  78 us (7%)
  blocking collectives  32.5 us (3%)
  between operations  17.8 us (2%)
    ppermute x18, waiting for transfers between devices, line_gather(): from_high.append(lax.ppermute(from_high[-1], 'tensor', falling))  119 us
    ppermute x25, waiting for transfers between devices, pair_swap(): return lax.ppermute(values, 'dp', [(i, i ^ bit) for i in range(count)])  92.1 us
    pallas_call x10, Pallas kernels, grad_blocks(): pl.pallas_call(grad_body, grid_spec=pltpu.PrefetchScalarGridSpec(num_scal...  78 us
    ppermute x18, starting transfers between devices, line_scatter(): rising_sum = lax.ppermute(up_part.astype(jnp.bfloat16), 'tensor', rising)  65 us
    unnamed x315, local copies, waits for them, and re-layouts  53.3 us
    ppermute x18, waiting for transfers between devices, line_scatter(): rising_sum = lax.ppermute(up_part.astype(jnp.bfloat16), 'tensor', rising)  50.1 us
    ppermute x18, starting transfers between devices, line_gather(): from_low.append(lax.ppermute(from_low[-1], 'tensor', rising))  41 us
    dot_general x2, matrix products, local(): jnp.dot(gathered, down_full, preferred_element_type=jnp.float32)  27.8 us
  transfers between devices with their start and end apart: 115, of which 48 were waited for; matrix products, arithmetic and copies ran while one was open for 38% of the time, Pallas kernels for 7%

profile of v1, /device:TPU:0, one launch (start us, length us, event | category | flops | bytes accessed | tf_op | source)
XLA Modules:
  0.0 1082.0 jit_solution(9844519279140374693)
XLA Ops:
  55.4 16.8 %collective-permute-done = bf16[256,2048]{1,0:T(8,128)(2,1)} collective-permute-done((bf16[256,2048]{1,0:T(8,128)(2,1)}, bf16[256,2048]{1,0:T(8,128)(2,1)}, u32[]{:S(2)}, u32[]{:S(2)}) %collective-permute-start) | collective-permute-done | bytes 1048608 | tf_op jit(solution)/shard_map/ppermute | solution.py:94
  78.6 23.3 %all-gather.1 = bf16[4,64,4]{1,2,0:T(4,128)(2,1)S(1)} all-gather(bf16[1,64,4]{1,2,0:T(4,128)(2,1)S(1)} %convert_bitcast_fusion), channel_id=1, replica_groups=mesh['dp'=8,'tensor'=4] {'tensor'}, dimensions={0}, use_global_device_ids=true | all-gather | bytes 2560 | tf_op jit(solution)/shard_map/all_gather | solution.py:270
  102.2 9.1 all_gather.20
  117.4 22.7 %collective-permute-done.5 = bf16[256,2048]{1,0:T(8,128)(2,1)S(1)} collective-permute-done((bf16[256,2048]{1,0:T(8,128)(2,1)S(1)}, bf16[256,2048]{1,0:T(8,128)(2,1)S(1)}, u32[]{:S(2)}, u32[]{:S(2)}) %collective-permute-start.5) | collective-permute-done | bytes 1048608 | tf_op jit(solution)/shard_map/ppermute | solution.py:95
  143.8 11.8 %fusion.45 = f32[3,1024,512]{2,1,0:T(8,128)S(1)} fusion(bf16[3,2048,512]{1,2,0:T(8,128)(2,1)} %all-gather.7.cloned.1.call-done, bf16[256,2048]{1,0:T(8,128)(2,1)} %get-tuple-element.252, bf16[256,2048]{1,0:T(8,128)(2,1)} %get-tuple-element.251, bf16[256,2048]{1,0:T(8,128)(2,1)S(1)} %get-tuple-element.250, bf16[256,2048]{1,0:T(8,128)(2,1)S(1)} %get-tuple-element.249), kind=kOutput, calls=%fused_computation.95 | convolution fusion | flops 6459228160 | bytes 16777216 | tf_op jit(solution)/shard_map/rd,kdf->krf/dot_general | solution.py:279
  212.2 9.8 collective-permute-done.12
  234.5 9.9 collective-permute-done.13
  255.6 8.9 collective-permute-done.14
  318.9 11.7 %multiply_convert_fusion.4 = (bf16[512,2048]{1,0:T(8,128)(2,1)S(1)}, f32[512,2048]{1,0:T(8,128)}) fusion(f32[512,2048]{1,0:T(8,128)S(1)} %fusion.13, bf16[512,2048]{1,0:T(8,128)(2,1)S(1)} %copy-done.41, bf16[2,2048,2048]{2,1,0:T(8,128)(2,1)} %all-gather.11.cloned.1.call-done), kind=kOutput, calls=%fused_computation.71 | convolution fusion | flops 4301258752 | bytes 20971520 | tf_op jit(solution)/shard_map/dot_general | solution.py:343
  343.4 8.9 collective-permute-done.33
  385.7 11.9 %collective-permute-done.23 = bf16[128,2048]{1,0:T(8,128)(2,1)S(1)} collective-permute-done((bf16[128,2048]{1,0:T(8,128)(2,1)S(1)}, bf16[128,2048]{1,0:T(8,128)(2,1)S(1)}, u32[]{:S(2)}, u32[]{:S(2)}) %collective-permute-start.23) | collective-permute-done | bytes 524320 | tf_op jit(solution)/shard_map/ppermute | solution.py:121
  435.6 8.9 collective-permute-done.54
  457.8 9.2 collective-permute-done.55
  469.6 8.7 collective-permute-done.44
  478.6 13.2 %multiply_convert_fusion.3 = (bf16[512,2048]{1,0:T(8,128)(2,1)}, bf16[512,2048]{1,0:T(8,128)(2,1)S(1)}) fusion(f32[512,2048]{1,0:T(8,128)} %copy-done.136, f32[512,2048]{1,0:T(8,128)} %get-tuple-element.326, bf16[1,2048,2048]{2,1,0:T(8,128)(2,1)} %all-gather.13.cloned.1.call-done, bf16[128,2048]{1,0:T(8,128)(2,1)S(1)} %get-tuple-element.163, ...), kind=kOutput, calls=%fused_computation.70 | convolution fusion | flops 4318035968 | bytes 23068672 | tf_op jit(solution)/shard_map/dot_general | solution.py:371
  491.8 10.2 fusion.12
  502.0 9.8 fusion.43
  518.3 14.6 %multiply_convert_fusion.2 = (bf16[512,2048]{1,0:T(8,128)(2,1)}, bf16[512,2048]{1,0:T(8,128)(2,1)S(1)}) fusion(f32[512,2048]{1,0:T(8,128)} %copy-done.135, f32[512,2048]{1,0:T(8,128)} %get-tuple-element.324, bf16[1,2048,2048]{2,1,0:T(8,128)(2,1)} %all-gather.13.cloned.1.call-done, bf16[128,2048]{1,0:T(8,128)(2,1)S(1)} %get-tuple-element.155, ...), kind=kOutput, calls=%fused_computation.69 | convolution fusion | flops 4318035968 | bytes 23068672 | tf_op jit(solution)/shard_map/dot_general | solution.py:371
  533.0 9.6 fusion.11
  542.6 8.8 fusion.44
  556.5 9.3 shard_map.221
  588.2 9.3 shard_map.219
  729.7 8.9 fusion.37
  756.7 8.8 reduce-scatter.7.cloned.1.call-done
  770.5 8.6 shard_map.222
  786.8 8.6 shard_map.220
  797.0 8.6 shard_map.218
  834.0 10.2 collective-permute-done.100
  847.9 18.2 %collective-permute-done.95 = bf16[2,256,1024]{2,1,0:T(8,128)(2,1)} collective-permute-done((bf16[2,256,1024]{2,1,0:T(8,128)(2,1)}, bf16[2,256,1024]{2,1,0:T(8,128)(2,1)}, u32[]{:S(2)}, u32[]{:S(2)}) %collective-permute-start.95) | collective-permute-done | bytes 1048608 | tf_op jit(solution)/shard_map/ppermute | solution.py:154
  898.8 27.4 %collective-permute-done.106 = bf16[1,256,1024]{2,1,0:T(8,128)(2,1)} collective-permute-done((bf16[1,256,1024]{2,1,0:T(8,128)(2,1)}, bf16[1,256,1024]{2,1,0:T(8,128)(2,1)}, u32[]{:S(2)}, u32[]{:S(2)}) %collective-permute-start.106) | collective-permute-done | bytes 524320 | tf_op jit(solution)/shard_map/ppermute | solution.py:154
  993.3 12.1 %multiply_subtract_fusion = (f32[3,256,2048]{2,1,0:T(8,128)}, f32[3,256,2048]{2,1,0:T(8,128)}, f32[3,256,2048]{2,1,0:T(8,128)}) fusion(f32[3,256,2048]{2,1,0:T(8,128)S(1)} %bitcast.500, f32[1,256,2048]{2,1,0:T(8,128)S(1)} %maximum_bitcast_fusion.2, f32[1,256,2048]{2,1,0:T(8,128)S(1)} %maximum_bitcast_fusion.1, f32[1,256,2048]{2,1,0:T(8,128)S(1)} %maximum_bitcast_fusion, ...), kind=kLoop, calls=%fused_computation.21 | loop fusion | flops 25165824 | bytes 44040192 | tf_op jit(solution)/shard_map/sub | solution.py:68
  1050.4 9.6 collective-permute-start.90
  (751 shorter events, 686.6 us)
Async XLA Ops:
  7.2 136.6 %all-gather.7.cloned.1.call-start = ((), (), s32[]{:S(2)}) async-start(), calls=%async_computation.2 | async-start | bytes 7077888 | tf_op jit(solution)/shard_map/all_gather | solution.py:266
  10.4 258.0 %all-gather.9.cloned.1.call-start = ((), (), s32[]{:S(2)}) async-start(), calls=%async_computation.3 | async-start | bytes 9437184 | tf_op jit(solution)/shard_map/all_gather | solution.py:267
  45.7 240.0 %all-gather.11.cloned.1.call-start = ((), (), s32[]{:S(2)}) async-start(), calls=%async_computation.4 | async-start | bytes 18874368 | tf_op jit(solution)/shard_map/all_gather | solution.py:268
  50.5 250.8 %all-gather.13.cloned.1.call-start = ((), (), s32[]{:S(2)}) async-start(), calls=%async_computation.5 | async-start | bytes 9437184 | tf_op jit(solution)/shard_map/all_gather | solution.py:269
  55.3 710.2 %reduce-scatter.7.cloned.1.call-start = ((), (), s32[]{:S(2)}) async-start(), calls=%async_computation.6 | async-start | bytes 1179648
  72.2 39.8 %collective-permute-start.1 = (bf16[256,2048]{1,0:T(8,128)(2,1)}, bf16[256,2048]{1,0:T(8,128)(2,1)S(1)}, u32[]{:S(2)}, u32[]{:S(2)}) collective-permute-start(bf16[256,2048]{1,0:T(8,128)(2,1)} %collective-permute-done), channel_id=1, source_target_pairs={{1,2},{2,3},{5,6},{6,7},{9,10},{10,11},{13,14},{14,15},{17,18},{18... | collective-permute-start | bytes 3145736 | tf_op jit(solution)/shard_map/ppermute | solution.py:94
  77.3 35.4 %collective-permute-start.4 = (bf16[256,2048]{1,0:T(8,128)(2,1)}, bf16[256,2048]{1,0:T(8,128)(2,1)S(1)}, u32[]{:S(2)}, u32[]{:S(2)}) collective-permute-start(bf16[256,2048]{1,0:T(8,128)(2,1)} %collective-permute-done.3), channel_id=1, source_target_pairs={{1,0},{2,1},{5,4},{6,5},{9,8},{10,9},{13,12},{14,13},{17,16},{18,1... | collective-permute-start | bytes 3145736 | tf_op jit(solution)/shard_map/ppermute | solution.py:95
  310.1 31.9 %collective-permute-start.21 = (bf16[128,2048]{1,0:T(8,128)(2,1)S(1)}, bf16[128,2048]{1,0:T(8,128)(2,1)S(1)}, u32[]{:S(2)}, u32[]{:S(2)}) collective-permute-start(bf16[128,2048]{1,0:T(8,128)(2,1)S(1)} %get-tuple-element.227), channel_id=1, source_target_pairs={{0,1},{4,5},{8,9},{12,13},{16,17},{20,21},{24,25},{28,29}} | collective-permute-start | bytes 1572872 | tf_op jit(solution)/shard_map/ppermute | solution.py:121
  457.1 59.8 %collective-permute-start.53 = (bf16[128,2048]{1,0:T(8,128)(2,1)S(1)}, bf16[128,2048]{1,0:T(8,128)(2,1)S(1)}, u32[]{:S(2)}, u32[]{:S(2)}) collective-permute-start(bf16[128,2048]{1,0:T(8,128)(2,1)S(1)} %collective-permute-done.52), channel_id=1, source_target_pairs={{2,3},{6,7},{10,11},{14,15},{18,19},{22,23},{26,27},{30,31}} | collective-permute-start | bytes 1572872 | tf_op jit(solution)/shard_map/ppermute | solution.py:94
  467.0 50.9 %collective-permute-start.56 = (bf16[128,2048]{1,0:T(8,128)(2,1)S(1)}, bf16[128,2048]{1,0:T(8,128)(2,1)S(1)}, u32[]{:S(2)}, u32[]{:S(2)}) collective-permute-start(bf16[128,2048]{1,0:T(8,128)(2,1)S(1)} %collective-permute-done.55), channel_id=1, source_target_pairs={{1,0},{5,4},{9,8},{13,12},{17,16},{21,20},{25,24},{29,28}} | collective-permute-start | bytes 1572872 | tf_op jit(solution)/shard_map/ppermute | solution.py:95
  513.0 52.8 %collective-permute-start.45 = (bf16[128,2048]{1,0:T(8,128)(2,1)}, bf16[128,2048]{1,0:T(8,128)(2,1)}, u32[]{:S(2)}, u32[]{:S(2)}) collective-permute-start(bf16[128,2048]{1,0:T(8,128)(2,1)} %get-tuple-element.219), channel_id=1, source_target_pairs={{0,1},{4,5},{8,9},{12,13},{16,17},{20,21},{24,25},{28,29}} | collective-permute-start | bytes 1572872 | tf_op jit(solution)/shard_map/ppermute | solution.py:121
  515.2 59.4 %collective-permute-start.48 = (bf16[128,2048]{1,0:T(8,128)(2,1)}, bf16[128,2048]{1,0:T(8,128)(2,1)}, u32[]{:S(2)}, u32[]{:S(2)}) collective-permute-start(bf16[128,2048]{1,0:T(8,128)(2,1)} %get-tuple-element.220), channel_id=1, source_target_pairs={{3,2},{7,6},{11,10},{15,14},{19,18},{23,22},{27,26},{31,30}} | collective-permute-start | bytes 1572872 | tf_op jit(solution)/shard_map/ppermute | solution.py:122
  574.6 195.8 %collective-permute-start.104 = (bf16[1024,2048]{1,0:T(8,128)(2,1)}, bf16[1024,2048]{1,0:T(8,128)(2,1)}, u32[]{:S(2)}, u32[]{:S(2)}) collective-permute-start(bf16[1024,2048]{1,0:T(8,128)(2,1)} %shard_map.221), channel_id=1, source_target_pairs={{0,4},{4,0},{8,12},{12,8},{16,20},{20,16},{24,28},{28,24},{1,5},{5... | collective-permute-start | bytes 12582920 | tf_op jit(solution)/shard_map/ppermute | solution.py:154
  624.5 157.8 %collective-permute-start.99 = (bf16[1024,2048]{1,0:T(8,128)(2,1)}, bf16[1024,2048]{1,0:T(8,128)(2,1)}, u32[]{:S(2)}, u32[]{:S(2)}) collective-permute-start(bf16[1024,2048]{1,0:T(8,128)(2,1)} %shard_map.219), channel_id=1, source_target_pairs={{0,4},{4,0},{8,12},{12,8},{16,20},{20,16},{24,28},{28,24},{1,5},{5... | collective-permute-start | bytes 12582920 | tf_op jit(solution)/shard_map/ppermute | solution.py:154
  724.9 99.6 %reduce-scatter.9.cloned.1.call-start = ((), (), s32[]{:S(2)}) async-start(), calls=%async_computation.7 | async-start | bytes 163840
  724.9 70.5 %collective-permute-start.94 = (bf16[1024,2048]{1,0:T(8,128)(2,1)}, bf16[1024,2048]{1,0:T(8,128)(2,1)}, u32[]{:S(2)}, u32[]{:S(2)}) collective-permute-start(bf16[1024,2048]{1,0:T(8,128)(2,1)} %copy-done.3), channel_id=1, source_target_pairs={{0,4},{4,0},{8,12},{12,8},{16,20},{20,16},{24,28},{28,24},{1,5},{5... | collective-permute-start | bytes 12582920 | tf_op jit(solution)/shard_map/ppermute | solution.py:154
  725.0 240.2 %collective-permute-start.83 = (bf16[1024,2048]{1,0:T(8,128)(2,1)}, bf16[1024,2048]{1,0:T(8,128)(2,1)}, u32[]{:S(2)}, u32[]{:S(2)}) collective-permute-start(bf16[1024,2048]{1,0:T(8,128)(2,1)} %shard_map.215), channel_id=1, source_target_pairs={{0,4},{4,0},{8,12},{12,8},{16,20},{20,16},{24,28},{28,24},{1,5},{5... | collective-permute-start | bytes 12582920 | tf_op jit(solution)/shard_map/ppermute | solution.py:154
  767.5 40.8 %collective-permute-start.75 = (bf16[256,2048]{1,0:T(8,128)(2,1)S(1)}, bf16[256,2048]{1,0:T(8,128)(2,1)S(1)}, u32[]{:S(2)}, u32[]{:S(2)}) collective-permute-start(bf16[256,2048]{1,0:T(8,128)(2,1)S(1)} %get-tuple-element.184), channel_id=1, source_target_pairs={{3,2},{7,6},{11,10},{15,14},{19,18},{23,22},{27,26},{31,30}} | collective-permute-start | bytes 3145736 | tf_op jit(solution)/shard_map/ppermute | solution.py:122
  770.4 103.1 %collective-permute-start.78 = (bf16[1024,1536]{1,0:T(8,128)(2,1)}, bf16[1024,1536]{1,0:T(8,128)(2,1)}, u32[]{:S(2)}, u32[]{:S(2)}) collective-permute-start(bf16[1024,1536]{1,0:T(8,128)(2,1)} %shard_map.213), channel_id=1, source_target_pairs={{0,4},{4,0},{8,12},{12,8},{16,20},{20,16},{24,28},{28,24},{1,5},{5... | collective-permute-start | bytes 9437192 | tf_op jit(solution)/shard_map/ppermute | solution.py:154
  808.3 35.9 %collective-permute-start.100 = (bf16[2,256,1024]{2,1,0:T(8,128)(2,1)}, bf16[2,256,1024]{2,1,0:T(8,128)(2,1)}, u32[]{:S(2)}, u32[]{:S(2)}) collective-permute-start(bf16[2,256,1024]{2,1,0:T(8,128)(2,1)} %pad_maximum_fusion.19), channel_id=1, source_target_pairs={{0,8},{4,12},{8,0},{12,4},{16,24},{20,28},{24,16},{28,20},{1,9},{5... | collective-permute-start | bytes 3145736 | tf_op jit(solution)/shard_map/ppermute | solution.py:154
  809.8 56.4 %collective-permute-start.95 = (bf16[2,256,1024]{2,1,0:T(8,128)(2,1)}, bf16[2,256,1024]{2,1,0:T(8,128)(2,1)}, u32[]{:S(2)}, u32[]{:S(2)}) collective-permute-start(bf16[2,256,1024]{2,1,0:T(8,128)(2,1)} %pad_maximum_fusion.18), channel_id=1, source_target_pairs={{0,8},{4,12},{8,0},{12,4},{16,24},{20,28},{24,16},{28,20},{1,9},{5... | collective-permute-start | bytes 3145736 | tf_op jit(solution)/shard_map/ppermute | solution.py:154
  821.7 47.9 %collective-permute-start.76 = (bf16[256,2048]{1,0:T(8,128)(2,1)S(1)}, bf16[256,2048]{1,0:T(8,128)(2,1)}, u32[]{:S(2)}, u32[]{:S(2)}) collective-permute-start(bf16[256,2048]{1,0:T(8,128)(2,1)S(1)} %get-tuple-element.182), channel_id=1, source_target_pairs={{2,1},{3,2},{6,5},{7,6},{10,9},{11,10},{14,13},{15,14},{18,17},{19... | collective-permute-start | bytes 3145736 | tf_op jit(solution)/shard_map/ppermute | solution.py:122
  844.2 38.0 %collective-permute-start.107 = (bf16[2,256,1024]{2,1,0:T(8,128)(2,1)S(1)}, bf16[2,256,1024]{2,1,0:T(8,128)(2,1)S(1)}, u32[]{:S(2)}, u32[]{:S(2)}) collective-permute-start(bf16[2,256,1024]{2,1,0:T(8,128)(2,1)S(1)} %stack.185), channel_id=1, source_target_pairs={{0,16},{4,20},{8,24},{12,28},{16,0},{20,4},{24,8},{28,12},{1,17},{... | collective-permute-start | bytes 3145736 | tf_op jit(solution)/shard_map/ppermute | solution.py:154
  866.1 31.3 %collective-permute-start.102 = (bf16[2,256,1024]{2,1,0:T(8,128)(2,1)}, bf16[2,256,1024]{2,1,0:T(8,128)(2,1)}, u32[]{:S(2)}, u32[]{:S(2)}) collective-permute-start(bf16[2,256,1024]{2,1,0:T(8,128)(2,1)} %stack.184), channel_id=1, source_target_pairs={{0,16},{4,20},{8,24},{12,28},{16,0},{20,4},{24,8},{28,12},{1,17},{... | collective-permute-start | bytes 3145736 | tf_op jit(solution)/shard_map/ppermute | solution.py:154
  869.6 72.4 %collective-permute-start.97 = (bf16[2,256,1024]{2,1,0:T(8,128)(2,1)}, bf16[2,256,1024]{2,1,0:T(8,128)(2,1)}, u32[]{:S(2)}, u32[]{:S(2)}) collective-permute-start(bf16[2,256,1024]{2,1,0:T(8,128)(2,1)} %stack.183), channel_id=1, source_target_pairs={{0,16},{4,20},{8,24},{12,28},{16,0},{20,4},{24,8},{28,12},{1,17},{... | collective-permute-start | bytes 3145736 | tf_op jit(solution)/shard_map/ppermute | solution.py:154
  873.5 52.7 %collective-permute-start.106 = (bf16[1,256,1024]{2,1,0:T(8,128)(2,1)}, bf16[1,256,1024]{2,1,0:T(8,128)(2,1)}, u32[]{:S(2)}, u32[]{:S(2)}) collective-permute-start(bf16[1,256,1024]{2,1,0:T(8,128)(2,1)} %add_convert_fusion.4), channel_id=1, source_target_pairs={{0,16},{4,20},{8,24},{12,28},{16,0},{20,4},{24,8},{28,12},{1,17},{... | collective-permute-start | bytes 1572872 | tf_op jit(solution)/shard_map/ppermute | solution.py:154
  882.2 55.2 %collective-permute-start.101 = (bf16[1,256,1024]{2,1,0:T(8,128)(2,1)}, bf16[1,256,1024]{2,1,0:T(8,128)(2,1)}, u32[]{:S(2)}, u32[]{:S(2)}) collective-permute-start(bf16[1,256,1024]{2,1,0:T(8,128)(2,1)} %add_convert_fusion.8), channel_id=1, source_target_pairs={{0,16},{4,20},{8,24},{12,28},{16,0},{20,4},{24,8},{28,12},{1,17},{... | collective-permute-start | bytes 1572872 | tf_op jit(solution)/shard_map/ppermute | solution.py:154
  897.4 51.1 %collective-permute-start.96 = (bf16[1,256,1024]{2,1,0:T(8,128)(2,1)}, bf16[1,256,1024]{2,1,0:T(8,128)(2,1)S(1)}, u32[]{:S(2)}, u32[]{:S(2)}) collective-permute-start(bf16[1,256,1024]{2,1,0:T(8,128)(2,1)} %add_convert_fusion.12), channel_id=1, source_target_pairs={{0,16},{4,20},{8,24},{12,28},{16,0},{20,4},{24,8},{28,12},{1,17},{... | collective-permute-start | bytes 1572872 | tf_op jit(solution)/shard_map/ppermute | solution.py:154
  942.0 75.0 %collective-permute-start.74 = (bf16[256,2048]{1,0:T(8,128)(2,1)}, bf16[256,2048]{1,0:T(8,128)(2,1)}, u32[]{:S(2)}, u32[]{:S(2)}) collective-permute-start(bf16[256,2048]{1,0:T(8,128)(2,1)} %get-tuple-element.181), channel_id=1, source_target_pairs={{0,1},{1,2},{2,3},{4,5},{5,6},{6,7},{8,9},{9,10},{10,11},{12,13},{... | collective-permute-start | bytes 3145736 | tf_op jit(solution)/shard_map/ppermute | solution.py:121
  948.6 69.4 %collective-permute-start.77 = (bf16[256,2048]{1,0:T(8,128)(2,1)}, bf16[256,2048]{1,0:T(8,128)(2,1)}, u32[]{:S(2)}, u32[]{:S(2)}) collective-permute-start(bf16[256,2048]{1,0:T(8,128)(2,1)} %fusion.73), channel_id=1, source_target_pairs={{1,0},{2,1},{3,2},{5,4},{6,5},{7,6},{9,8},{10,9},{11,10},{13,12},{... | collective-permute-start | bytes 3145736 | tf_op jit(solution)/shard_map/ppermute | solution.py:122
  981.6 55.2 %collective-permute-start.80 = (bf16[1,256,768]{1,2,0:T(8,128)(2,1)}, bf16[1,256,768]{1,2,0:T(8,128)(2,1)}, u32[]{:S(2)}, u32[]{:S(2)}) collective-permute-start(bf16[1,256,768]{1,2,0:T(8,128)(2,1)} %add_convert_fusion.22), channel_id=1, source_target_pairs={{0,16},{4,20},{8,24},{12,28},{16,0},{20,4},{24,8},{28,12},{1,17},{... | collective-permute-start | bytes 1179656 | tf_op jit(solution)/shard_map/ppermute | solution.py:154
  1012.2 33.2 %collective-permute-start.82 = (bf16[1,256,768]{1,2,0:T(8,128)(2,1)S(1)}, bf16[1,256,768]{1,2,0:T(8,128)(2,1)S(1)}, u32[]{:S(2)}, u32[]{:S(2)}) collective-permute-start(bf16[1,256,768]{1,2,0:T(8,128)(2,1)S(1)} %add_convert_fusion.20), channel_id=1, source_target_pairs={{0,8},{4,12},{8,0},{12,4},{16,24},{20,28},{24,16},{28,20},{1,9},{5... | collective-permute-start | bytes 1179656 | tf_op jit(solution)/shard_map/ppermute | solution.py:154
  (228 other events, 3257.7 us)
Sparse Core Ops, SparseCore 0:
  10.5 49.3 all-gather.6
  62.3 56.0 all-gather.8
  120.9 89.8 all-gather.10
  212.5 54.3 all-gather.12
  725.0 40.4 reduce-scatter.6
  767.6 19.4 reduce-scatter.8

commit v2 on v1

v2 whole, which is shorter than its diff:
```python
import jax
import jax.numpy as jnp
from jax import lax
from jax.experimental import pallas as pl
from jax.experimental.pallas import tpu as pltpu
from jax.sharding import PartitionSpec as P

HDIM = 128
STEP = 10
CHUNKS = 2
MIB = 1 << 20


NORM_EPS = 1e-06
ROPE_BASE = 500000.0
BETA_ONE = 0.9
BETA_TWO = 0.95
ADAM_EPS = 1e-08
RATE_MATRIX = 0.03
RATE_GAIN = 0.6
DECAY_MATRIX = 0.1
ROW_CONTRACT = (((0,), (0,)), ((), ()))
COLUMN_CONTRACT = (((1,), (1,)), ((), ()))


def doc_positions(lengths, seq_len):
    ends = jnp.cumsum(lengths, axis=-1, dtype=jnp.int32)
    starts = ends - lengths
    places = jnp.arange(seq_len, dtype=jnp.int32)
    inside = starts[:, None, :] <= places[None, :, None]
    begins = jnp.max(jnp.where(inside, starts[:, None, :], jnp.int32(0)), axis=-1)
    return places[None, :] - begins


def rope_tables(positions, head_dim):
    halfway = head_dim // 2
    powers = jnp.arange(halfway, dtype=jnp.float32) * (2.0 / head_dim)
    angles = positions.astype(jnp.float32)[:, None] * jnp.power(ROPE_BASE, -powers)
    return (jnp.cos(angles), jnp.sin(angles))


def post_norm(raw_rows, gain_row):
    return (
        raw_rows
        * lax.rsqrt(jnp.mean(raw_rows * raw_rows, axis=-1, keepdims=True) + NORM_EPS)
        * gain_row
    )


def adamw(weight, gradient, moment_one, moment_two, rate, decay):
    moment_one = BETA_ONE * moment_one + (1.0 - BETA_ONE) * gradient
    moment_two = BETA_TWO * moment_two + (1.0 - BETA_TWO) * gradient * gradient
    fix_one = 1.0 - BETA_ONE**STEP
    fix_two = 1.0 - BETA_TWO**STEP
    update = moment_one / fix_one / (jnp.sqrt(moment_two / fix_two) + ADAM_EPS)
    return (weight * (1.0 - rate * decay) - rate * update, moment_one, moment_two)


def pick(index, cases):
    if all(case is cases[0] for case in cases):
        return cases[0]
    return lax.select_n(index, *cases)


def after(values, *waits):
    return lax.optimization_barrier((values, waits))[0]


def chunk_scatter(part):
    return lax.psum_scatter(
        part.astype(jnp.bfloat16), "tensor", scatter_dimension=0, tiled=True
    ).astype(jnp.float32)


def line_hop(step, up, down):
    count = lax.axis_size("tensor")
    rising = [(i, i + 1) for i in range(step - 1, count - 1)]
    falling = [(i + 1, i) for i in range(count - step)]
    return lax.ppermute(up, "tensor", rising), lax.ppermute(down, "tensor", falling)


def line_pieces(piece, hops):
    count = lax.axis_size("tensor")
    here = lax.axis_index("tensor")
    low = [piece] + [hop[0] for hop in hops]
    high = [piece] + [hop[1] for hop in hops]
    return [
        pick(here, [low[i - owner] if i >= owner else high[owner - i] for i in range(count)])
        for owner in range(count)
    ]


def line_gather(piece, work=None):
    hops, given = [], ()
    pair = (piece, piece)
    for step in range(1, lax.axis_size("tensor")):
        pair = line_hop(step, *pair)
        if work is not None and step - 1 < len(work):
            given = work[step - 1](given)
            pair, given = lax.optimization_barrier((pair, given))
        hops.append(pair)
    pieces = line_pieces(piece, hops)
    return pieces if work is None else (pieces, given)


def shift_gather(piece):
    count = lax.axis_size("tensor")
    here = lax.axis_index("tensor")
    got = [piece] + [lax.ppermute(piece, "tensor", pairs) for pairs in shifts(count)]
    return [
        pick(here, [got[(i - owner) % count] for i in range(count)]) for owner in range(count)
    ]


def line_scatter(parts):
    count = lax.axis_size("tensor")
    here = lax.axis_index("tensor")
    rising_sum = falling_sum = None
    for step in range(1, count):
        up_part = lax.dynamic_index_in_dim(
            parts, jnp.minimum(here + count - step, count - 1), 0, keepdims=False
        )
        down_part = lax.dynamic_index_in_dim(
            parts, jnp.maximum(here - count + step, 0), 0, keepdims=False
        )
        if rising_sum is not None:
            up_part = up_part + rising_sum.astype(jnp.float32)
            down_part = down_part + falling_sum.astype(jnp.float32)
        rising = [(i, i + 1) for i in range(step)]
        falling = [(i, i - 1) for i in range(count - step, count)]
        rising_sum = lax.ppermute(up_part.astype(jnp.bfloat16), "tensor", rising)
        falling_sum = lax.ppermute(down_part.astype(jnp.bfloat16), "tensor", falling)
    own = lax.dynamic_index_in_dim(parts, here, 0, keepdims=False)
    return own + rising_sum.astype(jnp.float32) + falling_sum.astype(jnp.float32)


def shift_scatter(values, width):
    count = lax.axis_size("tensor")
    here = lax.axis_index("tensor")
    total = lax.dynamic_slice_in_dim(values, here * width, width, 1)
    for k, pairs in enumerate(shifts(count), 1):
        part = lax.dynamic_slice_in_dim(values, lax.rem(here + k, count) * width, width, 1)
        got = lax.ppermute(part.astype(jnp.bfloat16), "tensor", pairs)
        total = total + got.astype(jnp.float32)
    return total


def shifts(count):
    return [[(i, (i + k) % count) for i in range(count)] for k in range(1, count)]


def small_sum(values):
    total = values
    for pairs in shifts(lax.axis_size("tensor")):
        total = total + lax.ppermute(values, "tensor", pairs)
    return total


def rows_to_heads(values):
    count = lax.axis_size("tensor")
    here = lax.axis_index("tensor")
    rows, columns = values.shape
    width = columns // count
    got = [lax.dynamic_slice_in_dim(values, here * width, width, 1)]
    for k, pairs in enumerate(shifts(count), 1):
        block = lax.dynamic_slice_in_dim(values, lax.rem(here + k, count) * width, width, 1)
        got.append(lax.ppermute(block, "tensor", pairs))
    return [
        pick(here, [got[(i - owner) % count] for i in range(count)]) for owner in range(count)
    ]


def pair_swap(values, bit):
    count = lax.axis_size("dp")
    return lax.ppermute(values, "dp", [(i, i ^ bit) for i in range(count)])


def gather_gains(gains):
    tensor_count, count = lax.axis_size("tensor"), lax.axis_size("dp")
    here = lax.axis_index("tensor")
    got = [gains] + [lax.ppermute(gains, "tensor", pairs) for pairs in shifts(tensor_count)]
    block = jnp.concatenate(
        [pick(here, [got[(i - owner) % tensor_count] for i in range(tensor_count)])
         for owner in range(tensor_count)],
        axis=1,
    )
    if count & (count - 1):
        return lax.all_gather(block, "dp", axis=1, tiled=True)
    whole = block[None]
    bit = 1
    while bit < count:
        whole = jnp.concatenate([whole, pair_swap(whole, bit)], axis=0)
        bit = bit * 2
    order = jnp.arange(count, dtype=jnp.int32) ^ lax.axis_index("dp")
    return jnp.moveaxis(whole[order], 0, 1).reshape(gains.shape[0], -1)


def scatter_gains(grads):
    count, tensor_count = lax.axis_size("dp"), lax.axis_size("tensor")
    here = lax.axis_index("tensor")
    if count & (count - 1):
        block = lax.psum_scatter(grads, "dp", scatter_dimension=1, tiled=True)
    else:
        order = jnp.arange(count, dtype=jnp.int32) ^ lax.axis_index("dp")
        live = jnp.moveaxis(grads.reshape(grads.shape[0], count, -1), 1, 0)[order]
        bit = count // 2
        while bit:
            live = live[:bit] + pair_swap(live[bit:], bit)
            bit = bit // 2
        block = live[0]
    parts = jnp.moveaxis(block.reshape(block.shape[0], tensor_count, -1), 1, 0)
    total = lax.dynamic_index_in_dim(parts, here, 0, keepdims=False)
    for k, pairs in enumerate(shifts(tensor_count), 1):
        part = lax.dynamic_index_in_dim(
            parts, lax.rem(here + k, tensor_count), 0, keepdims=False
        )
        total = total + lax.ppermute(part, "tensor", pairs)
    return total


def kernel(body, grid, in_specs, out_specs, out_shape, operands, scratch=(), order=None):
    spec = pltpu.PrefetchScalarGridSpec(
        num_scalar_prefetch=0 if order is None else 1,
        grid=grid,
        in_specs=in_specs,
        out_specs=out_specs,
        scratch_shapes=scratch,
    )
    return pl.pallas_call(
        body,
        grid_spec=spec,
        out_shape=out_shape,
        compiler_params=pltpu.CompilerParams(vmem_limit_bytes=52 * MIB),
        cost_estimate=pl.CostEstimate(flops=1, bytes_accessed=1, transcendentals=0),
    )(*(() if order is None else (order,)), *operands)


def place_body(order_ref, *refs):
    step = pl.program_id(0)
    out_ref = refs[-1]
    half = out_ref.shape[1] // 2
    for side in range(2):
        own, from_x, from_y, low, high = refs[5 * side : 5 * side + 5]
        for at, piece in enumerate((own, from_x, from_y)):

            @pl.when(step == 4 * side + at)
            def _():
                out_ref[0] = piece[...]

        @pl.when(step == 4 * side + 3)
        def _():
            out_ref[0, :half] = low[...]
            out_ref[0, half:] = high[...]


def plane_one(shard):
    count = lax.axis_size("dp")
    if count != 8 or shard.shape[0] % 32:
        return (lax.all_gather(shard, "dp", axis=0, tiled=True),)
    return shard, pair_swap(shard, 2), pair_swap(shard, 4)


def plane_two(given):
    if len(given) == 1:
        return given
    shard, from_x, from_y = given
    half = shard.shape[0] // 2
    return (*given, pair_swap(from_x[:half], 4), pair_swap(from_y[half:], 2))


def plane_three(near):
    if len(near) == 1:
        return near[0]
    rows, width = near[0].shape
    far = [pair_swap(piece, 1) for piece in near]
    order = jnp.array([0, 2, 4, 6, 1, 3, 5, 7], jnp.int32) ^ lax.axis_index("dp")
    whole = kernel(
        place_body,
        (8,),
        [whole_block(piece.shape) for piece in (*near, *far)],
        pl.BlockSpec((1, rows, width), lambda step, order_ref: (order_ref[step], 0, 0)),
        jax.ShapeDtypeStruct((8, rows, width), near[0].dtype),
        (*near, *far),
        order=order,
    )
    return whole.reshape(8 * rows, width)


def whole_block(shape):
    return pl.BlockSpec(shape, lambda *at: (0,) * len(shape))


def out_norm_body(mixed_ref, weight_ref, tokens_ref, gain_ref, hidden_ref, raw_ref, all_ref):
    step = pl.program_id(0)
    tile = weight_ref.shape[0]
    product = lax.dot_general(
        mixed_ref[...].reshape(hidden_ref.shape),
        weight_ref[...],
        COLUMN_CONTRACT,
        preferred_element_type=jnp.float32,
    )
    raw_ref[...] = product
    all_ref[step] = product

    @pl.when(step == pl.num_programs(0) - 1)
    def _():
        rows, width = hidden_ref.shape
        square = jnp.zeros((rows, 1), jnp.float32)
        for at in range(width // tile):
            square = square + jnp.sum(all_ref[at] * all_ref[at], axis=-1, keepdims=True)
        scale = lax.rsqrt(square / width + NORM_EPS)
        for at in range(width // tile):
            columns = slice(at * tile, (at + 1) * tile)
            place = tokens_ref[:, 0, :, columns].reshape(rows, tile).astype(jnp.float32)
            hidden_ref[:, columns] = (
                place + all_ref[at] * scale * gain_ref[:, columns]
            ).astype(jnp.bfloat16)


def out_norm(mixed, weight, tokens, chunk, gain):
    pieces, _, piece_rows, width = tokens.shape
    rows = pieces * piece_rows
    tile = min(512, width)
    part = pl.BlockSpec((pieces, 1, piece_rows, width), lambda n: (0, chunk, 0, 0))
    return kernel(
        out_norm_body,
        (width // tile,),
        [
            part,
            pl.BlockSpec((tile, width), lambda n: (n, 0)),
            part,
            whole_block((1, width)),
        ],
        [whole_block((rows, width)), pl.BlockSpec((rows, tile), lambda n: (0, n))],
        [
            jax.ShapeDtypeStruct((rows, width), jnp.bfloat16),
            jax.ShapeDtypeStruct((rows, width), jnp.float32),
        ],
        (mixed, weight, tokens, gain),
        [pltpu.VMEM((width // tile, rows, tile), jnp.float32)],
    )


def mlp_in_body(hidden_ref, weight_ref, inner_ref, gate_ref, upper_ref):
    gate = jnp.dot(hidden_ref[...], weight_ref[0], preferred_element_type=jnp.float32)
    upper = jnp.dot(hidden_ref[...], weight_ref[1], preferred_element_type=jnp.float32)
    gate_ref[...] = gate
    upper_ref[...] = upper
    inner_ref[...] = (gate * jax.nn.sigmoid(gate) * upper).astype(jnp.bfloat16)


def mlp_in(hidden, weights):
    rows, depth = hidden.shape
    width = weights.shape[2]
    tile = min(512, width)
    out_spec = pl.BlockSpec((rows, tile), lambda n: (0, n))
    return kernel(
        mlp_in_body,
        (width // tile,),
        [whole_block((rows, depth)), pl.BlockSpec((2, depth, tile), lambda n: (0, 0, n))],
        [out_spec] * 3,
        [
            jax.ShapeDtypeStruct((rows, width), kind)
            for kind in (jnp.bfloat16, jnp.float32, jnp.float32)
        ],
        (hidden, weights),
    )


def mlp_out_body(inner_ref, weight_ref, out_ref):
    out_ref[...] = lax.dot_general(
        inner_ref[...], weight_ref[...], COLUMN_CONTRACT, preferred_element_type=jnp.float32
    ).astype(jnp.bfloat16)


def mlp_out(inner, weight):
    rows, depth = inner.shape
    width = weight.shape[-2]
    tile = min(512, width)
    if weight.ndim == 3:
        weight_spec = pl.BlockSpec((None, tile, depth), lambda n: (2, n, 0))
    else:
        weight_spec = pl.BlockSpec((tile, depth), lambda n: (n, 0))
    return kernel(
        mlp_out_body,
        (width // tile,),
        [whole_block((rows, depth)), weight_spec],
        pl.BlockSpec((rows, tile), lambda n: (0, n)),
        jax.ShapeDtypeStruct((rows, width), jnp.bfloat16),
        (inner, weight),
    )


def mlp_back_body(back_ref, weight_ref, gate_ref, upper_ref, back_gate_ref, back_upper_ref):
    back = jnp.dot(back_ref[...], weight_ref[...], preferred_element_type=jnp.float32)
    gate = gate_ref[...]
    share = jax.nn.sigmoid(gate)
    slope = share * (1.0 + gate * (1.0 - share))
    back_gate_ref[...] = (back * upper_ref[...] * slope).astype(jnp.bfloat16)
    back_upper_ref[...] = (back * (gate * share)).astype(jnp.bfloat16)


def mlp_back(back, weight, gate, upper):
    rows, depth = back.shape
    width = weight.shape[2]
    tile = min(512, width)
    spec = pl.BlockSpec((rows, tile), lambda n: (0, n))
    return kernel(
        mlp_back_body,
        (width // tile,),
        [
            whole_block((rows, depth)),
            pl.BlockSpec((None, depth, tile), lambda n: (2, 0, n)),
            spec,
            spec,
        ],
        [spec] * 2,
        [jax.ShapeDtypeStruct((rows, width), jnp.bfloat16)] * 2,
        (back, weight, gate, upper),
    )


def hidden_back_body(gate_ref, upper_ref, weight_ref, out_ref):
    out_ref[...] = (
        lax.dot_general(
            gate_ref[...], weight_ref[0], COLUMN_CONTRACT, preferred_element_type=jnp.float32
        )
        + lax.dot_general(
            upper_ref[...], weight_ref[1], COLUMN_CONTRACT, preferred_element_type=jnp.float32
        )
    ).astype(jnp.bfloat16)


def hidden_back(back_gate, back_upper, weights):
    rows, depth = back_gate.shape
    width = weights.shape[1]
    tile = min(512, width)
    return kernel(
        hidden_back_body,
        (width // tile,),
        [
            whole_block((rows, depth)),
            whole_block((rows, depth)),
            pl.BlockSpec((2, tile, depth), lambda n: (0, n, 0)),
        ],
        pl.BlockSpec((rows, tile), lambda n: (0, n)),
        jax.ShapeDtypeStruct((rows, width), jnp.bfloat16),
        (back_gate, back_upper, weights),
    )


def project_body(tokens_ref, weight_ref, out_ref, sums_ref):
    step = pl.program_id(0)
    product = jnp.dot(tokens_ref[...], weight_ref[...], preferred_element_type=jnp.float32)
    out_ref[...] = product
    sums = jnp.sum(product * product, axis=-1, keepdims=True)
    lanes = lax.broadcasted_iota(jnp.int32, sums_ref.shape, 1)

    @pl.when(step == 0)
    def _():
        sums_ref[...] = jnp.where(lanes == 0, sums, 0.0)

    @pl.when(step == 1)
    def _():
        sums_ref[...] = jnp.where(lanes == 1, sums, sums_ref[...])


def project(tokens, weight):
    rows, depth = tokens.shape
    width = weight.shape[1]
    return kernel(
        project_body,
        (3,),
        [whole_block((rows, depth)), pl.BlockSpec((depth, width // 3), lambda n: (0, n))],
        [pl.BlockSpec((rows, width // 3), lambda n: (0, n)), whole_block((rows, HDIM))],
        [
            jax.ShapeDtypeStruct((rows, width), jnp.float32),
            jax.ShapeDtypeStruct((rows, HDIM), jnp.float32),
        ],
        (tokens, weight),
    )


def turned(values, cosine, sine):
    return values * cosine + pltpu.roll(values, HDIM // 2, 1) * sine


def softmax_rows(query, key, start):
    scores = lax.dot_general(query, key, COLUMN_CONTRACT, preferred_element_type=jnp.float32)
    scores = scores * HDIM ** (-0.5)
    rows = start + lax.broadcasted_iota(jnp.int32, scores.shape, 0)
    columns = lax.broadcasted_iota(jnp.int32, scores.shape, 1)
    scores = jnp.where(columns <= rows, scores, -jnp.inf)
    weights = jnp.exp(scores - jnp.max(scores, axis=-1, keepdims=True))
    return weights / jnp.sum(weights, axis=-1, keepdims=True)


def attend_body(
    query_ref, key_ref, value_ref, scale_ref, gain_ref, cos_ref, sin_ref, low_ref, out_ref
):
    cosine, sine = cos_ref[...], sin_ref[...]
    for at, source in enumerate((query_ref, key_ref)):
        normed = source[...] * scale_ref[:, at : at + 1] * gain_ref[at : at + 1, :]
        low_ref[at] = turned(normed, cosine, sine).astype(jnp.bfloat16)
    low_ref[2] = value_ref[...].astype(jnp.bfloat16)
    rows = out_ref.shape[0]
    block = min(256, rows)
    for start in range(0, rows, block):
        stop = start + block
        share = softmax_rows(low_ref[0, start:stop], low_ref[1, :stop], start)
        out_ref[start:stop] = jnp.dot(
            share.astype(jnp.bfloat16), low_ref[2, :stop], preferred_element_type=jnp.float32
        ).astype(jnp.bfloat16)


def head_specs(rows, heads):
    return [
        pl.BlockSpec((rows, HDIM), lambda h, part=part: (0, part * heads + h)) for part in range(3)
    ]


def attend(projected, scale, gains, cosine, sine):
    rows, width = projected.shape
    heads = width // (3 * HDIM)
    return kernel(
        attend_body,
        (heads,),
        head_specs(rows, heads)
        + [
            whole_block((rows, HDIM)),
            pl.BlockSpec((2, HDIM), lambda h: (0, h)),
            whole_block((rows, HDIM)),
            whole_block((rows, HDIM)),
        ],
        [
            pl.BlockSpec((3, rows, HDIM), lambda h: (0, 0, h)),
            pl.BlockSpec((rows, HDIM), lambda h: (0, h)),
        ],
        [
            jax.ShapeDtypeStruct((3, rows, width // 3), jnp.bfloat16),
            jax.ShapeDtypeStruct((rows, width // 3), jnp.bfloat16),
        ],
        (projected, projected, projected, scale, gains, cosine, sine),
    )


def attend_back_body(
    low_ref,
    back_ref,
    query_ref,
    key_ref,
    scale_ref,
    gain_ref,
    cos_ref,
    sin_ref,
    hats_ref,
    value_out_ref,
    cross_ref,
    gain_out_ref,
    query_sum,
    key_sum,
    value_sum,
):
    rows = value_out_ref.shape[0]
    block = min(256, rows)
    for start in reversed(range(0, rows, block)):
        stop = start + block
        query, key, value = low_ref[0, start:stop], low_ref[1, :stop], low_ref[2, :stop]
        back = back_ref[start:stop]
        share = softmax_rows(query, key, start)
        back_share = lax.dot_general(
            back, value, COLUMN_CONTRACT, preferred_element_type=jnp.float32
        )
        mean = jnp.sum(share * back_share, axis=-1, keepdims=True)
        back_scores = (share * (back_share - mean)).astype(jnp.bfloat16)
        value_part = lax.dot_general(
            share.astype(jnp.bfloat16), back, ROW_CONTRACT, preferred_element_type=jnp.float32
        )
        key_part = lax.dot_general(
            back_scores, query, ROW_CONTRACT, preferred_element_type=jnp.float32
        )
        query_sum[start:stop] = jnp.dot(back_scores, key, preferred_element_type=jnp.float32)
        if stop == rows:
            value_sum[...] = value_part
            key_sum[...] = key_part
        else:
            value_sum[:stop] += value_part
            key_sum[:stop] += key_part
    value_out_ref[...] = value_sum[...].astype(jnp.bfloat16)
    cosine, sine = cos_ref[...], sin_ref[...]
    lanes = lax.broadcasted_iota(jnp.int32, cross_ref.shape, 1)
    cross = jnp.zeros(cross_ref.shape, jnp.float32)
    for at, (source, total) in enumerate(((query_ref, query_sum), (key_ref, key_sum))):
        normed = turned(total[...] * HDIM ** (-0.5), cosine, -sine)
        hat = source[...] * scale_ref[:, at : at + 1]
        gain_out_ref[at : at + 1] = jnp.sum(normed * hat, axis=0, keepdims=True)
        back_hat = normed * gain_ref[at : at + 1, :]
        hats_ref[at] = back_hat
        cross = jnp.where(lanes == at, jnp.sum(back_hat * hat, axis=-1, keepdims=True), cross)

    @pl.when(pl.program_id(0) == 0)
    def _():
        cross_ref[...] = cross

    @pl.when(pl.program_id(0) > 0)
    def _():
        cross_ref[...] += cross


def attend_back(low, back, projected, scale, gains, cosine, sine):
    rows, width = back.shape
    heads = width // HDIM
    head = pl.BlockSpec((rows, HDIM), lambda h: (0, h))
    return kernel(
        attend_back_body,
        (heads,),
        [pl.BlockSpec((3, rows, HDIM), lambda h: (0, 0, h)), head]
        + head_specs(rows, heads)[:2]
        + [
            whole_block((rows, HDIM)),
            pl.BlockSpec((2, HDIM), lambda h: (0, h)),
            whole_block((rows, HDIM)),
            whole_block((rows, HDIM)),
        ],
        [
            pl.BlockSpec((2, rows, HDIM), lambda h: (0, 0, h)),
            head,
            whole_block((rows, HDIM)),
            pl.BlockSpec((2, HDIM), lambda h: (0, h)),
        ],
        [
            jax.ShapeDtypeStruct((2, rows, width), jnp.float32),
            jax.ShapeDtypeStruct((rows, width), jnp.bfloat16),
            jax.ShapeDtypeStruct((rows, HDIM), jnp.float32),
            jax.ShapeDtypeStruct((2, width), jnp.float32),
        ],
        (low, back, projected, projected, scale, gains, cosine, sine),
        [pltpu.VMEM((rows, HDIM), jnp.float32)] * 3,
    )


def tokens_back_body(
    hats_ref, query_ref, key_ref, value_ref, scale_ref, mean_ref, weight_ref, back_ref, out_ref
):
    width = value_ref.shape[1]

    @pl.when(pl.program_id(0) == 0)
    def _():
        for at, source in enumerate((query_ref, key_ref)):
            scale = scale_ref[:, at : at + 1]
            hat = source[...] * scale
            back_ref[:, at * width : (at + 1) * width] = (
                scale * (hats_ref[at] - hat * mean_ref[:, at : at + 1])
            ).astype(jnp.bfloat16)
        back_ref[:, 2 * width :] = value_ref[...]

    out_ref[...] = lax.dot_general(
        back_ref[...], weight_ref[...], COLUMN_CONTRACT, preferred_element_type=jnp.float32
    ).astype(jnp.bfloat16)


def tokens_back_part(hats, projected, value_back, scale, mean, weight):
    rows, width = value_back.shape
    model_width = weight.shape[0]
    tile = min(512, model_width)
    return kernel(
        tokens_back_body,
        (model_width // tile,),
        [
            whole_block((2, rows, width)),
            pl.BlockSpec((rows, width), lambda n: (0, 0)),
            pl.BlockSpec((rows, width), lambda n: (0, 1)),
            whole_block((rows, width)),
            whole_block((rows, HDIM)),
            whole_block((rows, HDIM)),
            pl.BlockSpec((tile, 3 * width), lambda n: (n, 0)),
        ],
        [
            whole_block((rows, 3 * width)),
            pl.BlockSpec((rows, tile), lambda n: (0, n)),
        ],
        [
            jax.ShapeDtypeStruct((rows, 3 * width), jnp.bfloat16),
            jax.ShapeDtypeStruct((rows, model_width), jnp.bfloat16),
        ],
        (hats, projected, projected, value_back, scale, mean, weight),
    )


def product_of(left_refs, right_refs):
    total = None
    for left_ref, right_ref in zip(left_refs, right_refs):
        product = lax.dot_general(
            left_ref[...], right_ref[...], ROW_CONTRACT, preferred_element_type=jnp.float32
        )
        total = product if total is None else total + product
    return total


def sent_body(order_ref, *refs):
    parts = len(refs) // 2
    refs[-1][...] = product_of(refs[:parts], refs[parts:-1]).astype(jnp.bfloat16)


def kept_body(order_ref, *refs):
    parts = (len(refs) - 5) // 2
    got_ref = refs[2 * parts]
    x_send, y_send, x_keep, y_keep = refs[2 * parts + 1 :]
    step = pl.program_id(0)
    total = product_of(refs[:parts], refs[parts : 2 * parts]) + got_ref[...].astype(jnp.float32)
    total = total.astype(jnp.bfloat16)
    half = total.shape[1] // 2
    left, right = total[:, :half], total[:, half:]

    @pl.when(step < 2)
    def _():
        x_send[0] = left

    @pl.when((step == 1) | (step == 2))
    def _():
        y_send[0] = right

    @pl.when(step >= 2)
    def _():
        x_keep[0] = left

    @pl.when((step == 0) | (step == 3))
    def _():
        y_keep[0] = right


def quick(lefts, rights):
    count = lax.axis_size("dp")
    size = lefts[0].shape[1] // count
    return count == 8 and size % 128 == 0 and rights[0].shape[1] % 256 == 0


def grad_specs(lefts, rights, size):
    return [
        pl.BlockSpec((left.shape[0], size), lambda m, order_ref: (0, order_ref[m]))
        for left in lefts
    ] + [pl.BlockSpec(right.shape, lambda m, order_ref: (0, 0)) for right in rights]


def grad_sent(lefts, rights):
    if not quick(lefts, rights):
        return jnp.zeros((16, 128), jnp.bfloat16)
    size = lefts[0].shape[1] // 8
    width = rights[0].shape[1]
    order = jnp.array([3, 7, 5, 1], jnp.int32) ^ lax.axis_index("dp")
    return kernel(
        sent_body,
        (4,),
        grad_specs(lefts, rights, size),
        pl.BlockSpec((size, width), lambda m, order_ref: (m, 0)),
        jax.ShapeDtypeStruct((4 * size, width), jnp.bfloat16),
        (*lefts, *rights),
        order=order,
    )


def grad_kept(lefts, rights, got):
    if not quick(lefts, rights):
        return [
            sum(
                lax.dot_general(left, right, ROW_CONTRACT, preferred_element_type=jnp.float32)
                for left, right in zip(lefts, rights)
            )
        ]
    size = lefts[0].shape[1] // 8
    width = rights[0].shape[1]
    order = jnp.array([2, 6, 4, 0], jnp.int32) ^ lax.axis_index("dp")
    block = (1, size, width // 2)
    return kernel(
        kept_body,
        (4,),
        grad_specs(lefts, rights, size)
        + [pl.BlockSpec((size, width), lambda m, order_ref: (m, 0))],
        [
            pl.BlockSpec(block, lambda m, order_ref: (jnp.minimum(m, 1), 0, 0)),
            pl.BlockSpec(block, lambda m, order_ref: (m // 2, 0, 0)),
            pl.BlockSpec(block, lambda m, order_ref: (m // 3, 0, 0)),
            pl.BlockSpec(block, lambda m, order_ref: (m // 3, 0, 0)),
        ],
        [jax.ShapeDtypeStruct((2, size, width // 2), jnp.bfloat16)] * 4,
        (*lefts, *rights, got),
        order=order,
    )


def exchange_one(kept):
    if len(kept) == 1:
        return kept
    return [pair_swap(kept[0], 2), pair_swap(kept[1], 4)]


def wide(values):
    return values.astype(jnp.float32)


def exchange_two(kept, first):
    if len(kept) == 1:
        return kept
    x_next = wide(kept[2][0]) + wide(first[0][1])
    y_next = wide(kept[3][0]) + wide(first[1][0])
    return [
        wide(kept[2][1]) + wide(first[0][0]),
        wide(kept[3][1]) + wide(first[1][1]),
        pair_swap(x_next.astype(jnp.bfloat16), 4),
        pair_swap(y_next.astype(jnp.bfloat16), 2),
    ]


def exchange_end(second):
    if len(second) == 1:
        return lax.psum_scatter(
            second[0].astype(jnp.bfloat16), "dp", scatter_dimension=0, tiled=True
        ).astype(jnp.float32)
    return jnp.concatenate(
        [second[half] + second[2 + half].astype(jnp.float32) for half in range(2)], axis=1
    )


def local(
    tokens,
    lengths,
    w_attn,
    w_mlp,
    norm_gains,
    moment_attn,
    square_attn,
    moment_mlp,
    square_mlp,
    moment_gains,
    square_gains,
    cotangent,
):
    rows_here, model_width = tokens.shape
    tensor_size = lax.axis_size("tensor")
    tensor_index = lax.axis_index("tensor")
    total_rows = rows_here * tensor_size
    seq_len = total_rows // lengths.shape[0]
    local_width = w_attn.shape[2]
    chunk_rows = rows_here // CHUNKS

    qkv_shard = jnp.concatenate([w_attn[k].astype(jnp.bfloat16) for k in range(3)], axis=1)
    mlp_low = w_mlp.astype(jnp.bfloat16)
    positions = doc_positions(lengths, seq_len).reshape(total_rows)

    def second_hop(given):
        mlp_shard = after(mlp_low, given)
        return plane_two(given), lax.all_gather(mlp_shard, "dp", axis=1, tiled=True), mlp_shard

    def third_hop(given):
        cos_table, sin_table = rope_tables(positions, HDIM)
        cosine = jnp.concatenate([cos_table, cos_table], axis=1)
        sine = jnp.concatenate([-sin_table, sin_table], axis=1)
        gains = gather_gains(after(norm_gains.astype(jnp.bfloat16), given))
        return plane_three(given), cosine, sine, gains

    hop, near = lax.optimization_barrier((line_hop(1, tokens, tokens), plane_one(qkv_shard)))
    hops = [hop]
    near, mlp_full, mlp_shard = second_hop(near)
    hop, near, mlp_shard = lax.optimization_barrier((line_hop(2, *hop), near, mlp_shard))
    hops.append(hop)
    hop, given = lax.optimization_barrier((line_hop(3, *hop), third_hop(near)))
    hops.append(hop)
    qkv_full, cosine, sine, gain_full = given
    whole_tokens = jnp.concatenate(line_pieces(tokens, hops), axis=0)
    gain_values = gain_full.astype(jnp.float32)
    column_start = tensor_index * local_width
    head_gains = lax.dynamic_slice_in_dim(gain_values[2:], column_start, local_width, 1)

    def summed_lanes(lanes):
        rows = lanes.shape[0]
        flat = lax.optimization_barrier(lanes[:, :2].T.reshape(-1, HDIM))
        return small_sum(flat).reshape(2, rows)

    def in_lanes(values):
        return jnp.pad(values.T, ((0, 0), (0, HDIM - 2)))

    projected, square_lanes = project(whole_tokens, qkv_full)
    inverse = lax.rsqrt(summed_lanes(square_lanes) / model_width + NORM_EPS)
    inverse_lanes = in_lanes(inverse)
    out_piece = after(w_attn[3].astype(jnp.bfloat16), inverse_lanes)
    out_shard = jnp.concatenate(shift_gather(out_piece), axis=1)
    low_heads, mixed_low = attend(projected, inverse_lanes, head_gains, cosine, sine)
    out_shard, mixed_low = lax.optimization_barrier((out_shard, mixed_low))
    pieces, out_full = line_gather(
        mixed_low, (lambda _: plane_one(out_shard), plane_two, plane_three)
    )
    whole_mixed = jnp.concatenate(pieces, axis=1)
    mixed_parted = whole_mixed.reshape(tensor_size, CHUNKS, chunk_rows, model_width)
    tokens_parted = whole_tokens.reshape(tensor_size, CHUNKS, chunk_rows, model_width)

    def own_part(values):
        parted = values.reshape((tensor_size, chunk_rows) + values.shape[1:])
        return lax.dynamic_index_in_dim(parted, tensor_index, 0, keepdims=False)

    def own_rows(values, chunk):
        return values[chunk * chunk_rows : (chunk + 1) * chunk_rows].astype(jnp.float32)

    chunks = range(CHUNKS)
    raw_attn, hidden_low, gate = ([None] * CHUNKS for _ in range(3))
    upper, inner_low, down_part, raw_mlp = ([None] * CHUNKS for _ in range(4))
    for chunk in chunks:
        mixed = mixed_parted
        if chunk:
            mixed = after(mixed, down_part[chunk - 1])
        hidden_low[chunk], raw_attn[chunk] = out_norm(
            mixed, out_full, tokens_parted, chunk, gain_values[:1]
        )
        inner_low[chunk], gate[chunk], upper[chunk] = mlp_in(hidden_low[chunk], mlp_full)
        down_part[chunk] = mlp_out(inner_low[chunk], mlp_full)
        raw_mlp[chunk] = chunk_scatter(down_part[chunk])

    own_mixed = [
        lax.dynamic_index_in_dim(mixed_parted[:, chunk], tensor_index, 0, keepdims=False)
        for chunk in chunks
    ]
    out_parts, back_raw_mlp, gains_mlp, attn_pulls = ([None] * CHUNKS for _ in range(4))
    gathered, gate_low, upper_low, hidden_part, back_sum = ([None] * CHUNKS for _ in range(5))

    def turn(chunk, raw):
        attn_normed, attn_pulls[chunk] = jax.vjp(
            post_norm, own_part(raw_attn[chunk]), gain_values[0]
        )
        mlp_normed, mlp_pull = jax.vjp(post_norm, raw, gain_values[1])
        hidden = own_rows(tokens, chunk) + attn_normed
        out_parts[chunk] = (hidden + mlp_normed).astype(jnp.bfloat16)
        back_raw, gains_mlp[chunk] = mlp_pull(own_rows(cotangent, chunk))
        back_raw_mlp[chunk] = back_raw.astype(jnp.bfloat16)

    def backward(chunk, gathered_rows):
        gate_low[chunk], upper_low[chunk] = mlp_back(
            gathered_rows, mlp_full, gate[chunk], upper[chunk]
        )
        hidden_part[chunk] = hidden_back(gate_low[chunk], upper_low[chunk], mlp_full)
        back_sum[chunk] = chunk_scatter(hidden_part[chunk])

    turn(0, raw_mlp[0])
    gathered[0] = jnp.concatenate(line_gather(back_raw_mlp[0]), axis=0)
    for chunk in chunks:
        rows = gathered[chunk]
        following = chunk + 1 < CHUNKS
        if following:
            turn(chunk + 1, after(raw_mlp[chunk + 1], rows))
            rows = after(rows, back_raw_mlp[chunk + 1])
        if following:
            gathered[chunk + 1] = jnp.concatenate(shift_gather(back_raw_mlp[chunk + 1]), axis=0)
        backward(chunk, rows)
    out_tokens = jnp.concatenate(out_parts, axis=0)

    down_left = after(gathered, hidden_part)
    down_sent = grad_sent(down_left, inner_low)
    gate_sent = grad_sent(after(hidden_low, down_sent), gate_low)
    down_kept = grad_kept(after(down_left, gate_sent), inner_low, pair_swap(down_sent, 1))
    down_one = exchange_one(down_kept)
    upper_sent = grad_sent(after(hidden_low, down_kept), upper_low)
    gate_kept = grad_kept(after(hidden_low, upper_sent), gate_low, pair_swap(gate_sent, 1))
    upper_kept = grad_kept(
        after(hidden_low, gate_kept, down_one), upper_low, pair_swap(upper_sent, 1)
    )
    gate_one = exchange_one(gate_kept)
    upper_one = exchange_one(upper_kept)

    back_hidden, gains_attn, back_raw_attn, back_rows = ([None] * CHUNKS for _ in range(4))
    back_heads = [None] * CHUNKS
    for chunk in chunks:
        rows = after(back_sum[chunk], upper_kept if chunk else gate_kept)
        back_hidden[chunk] = own_rows(cotangent, chunk) + rows
        back_raw, gains_attn[chunk] = attn_pulls[chunk](back_hidden[chunk])
        back_raw_attn[chunk] = back_raw.astype(jnp.bfloat16)
        if chunk:
            back_raw_attn[chunk] = after(back_raw_attn[chunk], gate_one)
        back_rows[chunk] = jnp.dot(
            back_raw_attn[chunk], out_full, preferred_element_type=jnp.float32
        ).astype(jnp.bfloat16)
        back_heads[chunk] = rows_to_heads(back_rows[chunk])
    back_mixed = jnp.stack([jnp.stack(parts) for parts in back_heads], axis=1)
    back_mixed = back_mixed.reshape(total_rows, local_width)
    out_sent = grad_sent(back_raw_attn, own_mixed)
    down_two = exchange_two(down_kept, after(down_one, upper_kept))
    out_kept = grad_kept(back_raw_attn, own_mixed, pair_swap(out_sent, 1))
    out_one = exchange_one(out_kept)
    back_mixed = after(back_mixed, out_kept, down_two, upper_one)

    back_hats, value_back, cross_lanes, head_gain_grads = attend_back(
        low_heads, back_mixed, projected, inverse_lanes, head_gains, cosine, sine
    )
    gate_two = exchange_two(gate_kept, after(gate_one, back_rows))
    cross_sums = summed_lanes(after(cross_lanes, gate_two))
    mean_lanes = in_lanes(cross_sums / model_width)
    upper_two = exchange_two(upper_kept, after(upper_one, value_back))
    mean_lanes = after(mean_lanes, out_one)
    qkv_back, tokens_part = tokens_back_part(
        back_hats, projected, value_back, inverse_lanes, mean_lanes, qkv_full
    )
    tokens_back = chunk_scatter(tokens_part)
    qkv_left = [after(whole_tokens, tokens_part)]
    qkv_sent = grad_sent(qkv_left, [qkv_back])
    out_two = exchange_two(out_kept, after(out_one, tokens_part))
    qkv_kept = grad_kept(
        after(qkv_left, upper_two, out_two), [qkv_back], pair_swap(qkv_sent, 1)
    )
    qkv_one = exchange_one(qkv_kept)

    gain_grad = jnp.zeros((4, model_width), jnp.float32)
    gain_grad = gain_grad.at[0].set(sum(gains_attn)).at[1].set(sum(gains_mlp))
    gain_grad = lax.dynamic_update_slice(
        gain_grad, head_gain_grads, (jnp.int32(2), column_start)
    )
    gain_final = scatter_gains(after(gain_grad, qkv_kept))
    gate_two, upper_two, down_two = after((gate_two, upper_two, down_two), qkv_kept)
    mlp_owned = jnp.stack([exchange_end(gate_two), exchange_end(upper_two), exchange_end(down_two)])
    new_mlp, new_moment_mlp, new_square_mlp = adamw(
        w_mlp, mlp_owned, moment_mlp, square_mlp, RATE_MATRIX, DECAY_MATRIX
    )
    qkv_two = exchange_two(qkv_kept, after(qkv_one, new_mlp))
    out_owned = shift_scatter(exchange_end(after(out_two, new_mlp)), local_width)
    qkv_owned = exchange_end(qkv_two)
    attn_owned = jnp.stack(
        [qkv_owned[:, k * local_width : (k + 1) * local_width] for k in range(3)] + [out_owned]
    )
    attn_owned = lax.optimization_barrier(attn_owned)
    new_attn, new_moment_attn, new_square_attn = adamw(
        w_attn, attn_owned, moment_attn, square_attn, RATE_MATRIX, DECAY_MATRIX
    )
    new_gains, new_moment_gains, new_square_gains = adamw(
        norm_gains, gain_final, moment_gains, square_gains, RATE_GAIN, 0.0
    )
    tokens_back = after(tokens_back, new_mlp, new_attn, new_gains)
    grad_tokens = (jnp.concatenate(back_hidden, axis=0) + tokens_back).astype(jnp.bfloat16)
    return (
        out_tokens,
        grad_tokens,
        new_attn,
        new_moment_attn,
        new_square_attn,
        new_mlp,
        new_moment_mlp,
        new_square_mlp,
        new_gains,
        new_moment_gains,
        new_square_gains,
    )


def solution(mesh):
    return jax.shard_map(
        local,
        mesh=mesh,
        in_specs=(
            P(("dp", "tensor"), None),
            P("dp", None),
            P(None, "dp", "tensor"),
            P(None, "dp", "tensor"),
            P(None, ("dp", "tensor")),
            P(None, "dp", "tensor"),
            P(None, "dp", "tensor"),
            P(None, "dp", "tensor"),
            P(None, "dp", "tensor"),
            P(None, ("dp", "tensor")),
            P(None, ("dp", "tensor")),
            P(("dp", "tensor"), None),
        ),
        out_specs=(
            P(("dp", "tensor"), None),
            P(("dp", "tensor"), None),
            P(None, "dp", "tensor"),
            P(None, "dp", "tensor"),
            P(None, "dp", "tensor"),
            P(None, "dp", "tensor"),
            P(None, "dp", "tensor"),
            P(None, "dp", "tensor"),
            P(None, ("dp", "tensor")),
            P(None, ("dp", "tensor")),
            P(None, ("dp", "tensor")),
        ),
        check_vma=False,
    )
```

time: 1090 us -> 865 us (0.79)
  Pallas kernels: 78 us -> 286 us
  matrix products: 179 us -> 9.36 us
  local copies, waits for them, and re-layouts: 113 us -> 18.5 us
  starting transfers between devices: 195 us -> 114 us
  other arithmetic: 154 us -> 92.9 us
  blocking collectives: 32.5 us -> 0 us
    pallas_call x10 -> x26, Pallas kernels: 78 us -> 286 us  [kernel(): pl.pallas_call(body, grid_spec=spec, out_shape=out_shape, compiler_params...]
    dot_general x30 -> x2, matrix products: 179 us -> 9.36 us  [local(): jnp.dot(back_raw_attn[chunk], out_full, preferred_element_type=jnp.float32)]
    ppermute x72 -> x33, starting transfers between devices: 150 us -> 57.7 us  [the longest x9 22.4 us: line_hop(): lax.ppermute(up, 'tensor', rising)]
    unnamed x315 -> x166, local copies, waits for them, and re-layouts: 53.3 us -> 8.2 us
    all_gather x2 -> x0, blocking collectives: 32.5 us -> none  [the longest x1 23.3 us: local(): lax.all_gather(norm_gains.astype(jnp.bfloat16), 'tensor', axis=1, tiled=T...]
    convert_element_type x34 -> x20, other arithmetic: 54.7 us -> 34.1 us  [the longest x5 10.5 us: exchange_two(): x_next.astype(jnp.bfloat16)]
    slice x20 -> x10, local copies, waits for them, and re-layouts: 21.4 us -> 4.94 us  [the longest x1 2.78 us: local(): mixed_parted[:, chunk]]
    ppermute x25 -> x49, starting transfers between devices: 23.9 us -> 38.8 us  [pair_swap(): return lax.ppermute(values, 'dp', [(i, i ^ bit) for i in range(count)])]
  transfers between devices with their start and end apart: 115 -> 100, of which waited for: 48 -> 51; matrix products, arithmetic and copies ran while one was open for 38% -> 12% of each run, Pallas kernels for 7% -> 28%
where the time goes in v2:
time: 865 us; the launch traced here: 851 us
  waiting for transfers between devices  314 us (36%)
  Pallas kernels  286 us (33%)
  starting transfers between devices  114 us (13%)
  other arithmetic  92.9 us (11%)
  local copies, waits for them, and re-layouts  18.5 us (2%)
  between operations  16.1 us (2%)
  matrix products  9.36 us (1%)
    pallas_call x26, Pallas kernels, kernel(): pl.pallas_call(body, grid_spec=spec, out_shape=out_shape, compiler_params...  286 us
    ppermute x9, waiting for transfers between devices, line_hop(): lax.ppermute(down, 'tensor', falling)  128 us
    ppermute x49, waiting for transfers between devices, pair_swap(): return lax.ppermute(values, 'dp', [(i, i ^ bit) for i in range(count)])  96.9 us
    ppermute x6, waiting for transfers between devices, shift_gather(): lax.ppermute(piece, 'tensor', pairs)  44.3 us
    ppermute x49, starting transfers between devices, pair_swap(): return lax.ppermute(values, 'dp', [(i, i ^ bit) for i in range(count)])  38.8 us
    ppermute x9, starting transfers between devices, line_hop(): lax.ppermute(up, 'tensor', rising)  22.4 us
    ppermute x3, waiting for transfers between devices, shift_scatter(): got = lax.ppermute(part.astype(jnp.bfloat16), 'tensor', pairs)  18 us
  transfers between devices with their start and end apart: 100, of which 51 were waited for; matrix products, arithmetic and copies ran while one was open for 12% of the time, Pallas kernels for 28%

profile of v2, /device:TPU:0, one launch (start us, length us, event | category | flops | bytes accessed | tf_op | source)
XLA Modules:
  0.0 850.9 jit_solution(6397636246256193122)
XLA Ops:
  21.6 13.9 %collective-permute-done.3.refs_2_ = bf16[256,1536]{1,0:T(8,128)(2,1)} collective-permute-done((bf16[256,1536]{1,0:T(8,128)(2,1)S(1)}, bf16[256,1536]{1,0:T(8,128)(2,1)}, u32[]{:S(2)}, u32[]{:S(2)}) %collective-permute-start.3) | collective-permute-done | bytes 786464 | tf_op jit(solution)/shard_map/ppermute | solution.py:175
  47.8 10.4 %collective-permute-done.7.refs_4_ = bf16[128,1536]{1,0:T(8,128)(2,1)S(1)} collective-permute-done((bf16[128,1536]{1,0:T(8,128)(2,1)S(1)}, bf16[128,1536]{1,0:T(8,128)(2,1)S(1)}, u32[]{:S(2)}, u32[]{:S(2)}) %collective-permute-start.7) | collective-permute-done | bytes 393248 | tf_op jit(solution)/shard_map/ppermute | solution.py:175
  99.4 10.1 %collective-permute-done.9 = bf16[256,2048]{1,0:T(8,128)(2,1)} collective-permute-done((bf16[256,2048]{1,0:T(8,128)(2,1)}, bf16[256,2048]{1,0:T(8,128)(2,1)}, u32[]{:S(2)}, u32[]{:S(2)}) %collective-permute-start.9) | collective-permute-done | bytes 1048608 | tf_op jit(solution)/shard_map/ppermute | solution.py:79
  114.3 11.5 %shard_map.312 = (f32[1024,1536]{1,0:T(8,128)}, f32[1024,128]{1,0:T(8,128)S(1)}) custom-call(bf16[1024,2048]{1,0:T(8,128)(2,1)} %pad_maximum_fusion.1.tokens_ref.refs_0_, bf16[2048,1536]{1,0:T(8,128)(2,1)} %bitcast.164), custom_call_target="tpu_custom_call" | custom-call | flops 1 | bytes 1 | tf_op jit(solution)/shard_map/pallas_call | solution.py:229
  135.2 14.5 %shard_map.313 = (bf16[3,1024,512]{2,1,0:T(8,128)(2,1)}, bf16[1024,512]{1,0:T(8,128)(2,1)}) custom-call(f32[1024,1536]{1,0:T(8,128)} %get-tuple-element.187.query_ref.key_ref.value_ref, f32[1024,1536]{1,0:T(8,128)} %get-tuple-element.187.query_ref.key_ref.value_ref, f32[1024,1536]{1,0:T(8,128)} %get-tuple-element.187.query_ref.key_ref.value_ref, ...), custom_call_target="tpu_custom_call" | custom-call | flops 1 | bytes 1 | tf_op jit(solution)/shard_map/pallas_call | solution.py:229
  163.5 16.7 %collective-permute-done.28 = bf16[1024,512]{1,0:T(8,128)(2,1)S(1)} collective-permute-done((bf16[1024,512]{1,0:T(8,128)(2,1)S(1)}, bf16[1024,512]{1,0:T(8,128)(2,1)S(1)}, u32[]{:S(2)}, u32[]{:S(2)}) %collective-permute-start.28) | collective-permute-done | bytes 1048608 | tf_op jit(solution)/shard_map/ppermute | solution.py:79
  194.9 10.7 %collective-permute-done.34.refs_4_ = bf16[128,2048]{1,0:T(8,128)(2,1)S(1)} collective-permute-done((bf16[128,2048]{1,0:T(8,128)(2,1)S(1)}, bf16[128,2048]{1,0:T(8,128)(2,1)S(1)}, u32[]{:S(2)}, u32[]{:S(2)}) %collective-permute-start.34) | collective-permute-done | bytes 524320 | tf_op jit(solution)/shard_map/ppermute | solution.py:175
  206.7 13.2 %collective-permute-done.32 = bf16[1024,512]{1,0:T(8,128)(2,1)S(1)} collective-permute-done((bf16[1024,512]{1,0:T(8,128)(2,1)S(1)}, bf16[1024,512]{1,0:T(8,128)(2,1)S(1)}, u32[]{:S(2)}, u32[]{:S(2)}) %collective-permute-start.32) | collective-permute-done | bytes 1048608 | tf_op jit(solution)/shard_map/ppermute | solution.py:79
  236.3 14.2 %collective-permute-done.36 = bf16[1024,512]{1,0:T(8,128)(2,1)S(1)} collective-permute-done((bf16[1024,512]{1,0:T(8,128)(2,1)S(1)}, bf16[1024,512]{1,0:T(8,128)(2,1)S(1)}, u32[]{:S(2)}, u32[]{:S(2)}) %collective-permute-start.36) | collective-permute-done | bytes 1048608 | tf_op jit(solution)/shard_map/ppermute | solution.py:79
  253.3 11.7 %shard_map.315 = (bf16[512,2048]{1,0:T(8,128)(2,1)}, f32[512,2048]{1,0:T(8,128)}) custom-call(bf16[4,2,128,2048]{3,2,1,0:T(8,128)(2,1)} %bitcast.161, bf16[2048,2048]{1,0:T(8,128)(2,1)} %bitcast.155, bf16[4,2,128,2048]{3,2,1,0:T(8,128)(2,1)} %bitcast.159, f32[1,2048]{1,0:T(1,128)S(1)} %get-tuple-element.392.gain_ref), custom_call_target="tpu_custom_call" | custom-call | flops 1 | bytes 1 | tf_op jit(solution)/shard_map/pallas_call | solution.py:229
  265.1 14.2 %shard_map.316 = (bf16[512,2048]{1,0:T(8,128)(2,1)}, f32[512,2048]{1,0:T(8,128)}, f32[512,2048]{1,0:T(8,128)}) custom-call(bf16[512,2048]{1,0:T(8,128)(2,1)} %get-tuple-element.245.hidden_ref.refs_0_, bf16[3,2048,2048]{2,1,0:T(8,128)(2,1)} %all-gather.2.cloned.1.call-done.weight_ref), custom_call_target="tpu_custom_call" | custom-call | flops 1 | bytes 1 | tf_op jit(solution)/shard_map/pallas_call | solution.py:229
  288.1 11.6 %shard_map.318 = (bf16[512,2048]{1,0:T(8,128)(2,1)}, f32[512,2048]{1,0:T(8,128)}) custom-call(bf16[4,2,128,2048]{3,2,1,0:T(8,128)(2,1)} %bitcast.162, bf16[2048,2048]{1,0:T(8,128)(2,1)} %bitcast.156, bf16[4,2,128,2048]{3,2,1,0:T(8,128)(2,1)} %bitcast.160, f32[1,2048]{1,0:T(1,128)S(1)} %get-tuple-element.392.gain_ref), custom_call_target="tpu_custom_call" | custom-call | flops 1 | bytes 1 | tf_op jit(solution)/shard_map/pallas_call | solution.py:229
  299.8 14.4 %shard_map.319 = (bf16[512,2048]{1,0:T(8,128)(2,1)}, f32[512,2048]{1,0:T(8,128)}, f32[512,2048]{1,0:T(8,128)}) custom-call(bf16[512,2048]{1,0:T(8,128)(2,1)} %get-tuple-element.246.hidden_ref.refs_1_, bf16[3,2048,2048]{2,1,0:T(8,128)(2,1)} %all-gather.2.cloned.1.call-done.weight_ref), custom_call_target="tpu_custom_call" | custom-call | flops 1 | bytes 1 | tf_op jit(solution)/shard_map/pallas_call | solution.py:229
  339.4 32.3 %collective-permute-done.45 = bf16[128,2048]{1,0:T(8,128)(2,1)S(1)} collective-permute-done((bf16[128,2048]{1,0:T(8,128)(2,1)S(1)}, bf16[128,2048]{1,0:T(8,128)(2,1)S(1)}, u32[]{:S(2)}, u32[]{:S(2)}) %collective-permute-start.45) | collective-permute-done | bytes 524320 | tf_op jit(solution)/shard_map/ppermute | solution.py:79
  374.4 19.4 %collective-permute-done.46 = bf16[128,2048]{1,0:T(8,128)(2,1)S(1)} collective-permute-done((bf16[128,2048]{1,0:T(8,128)(2,1)S(1)}, bf16[128,2048]{1,0:T(8,128)(2,1)S(1)}, u32[]{:S(2)}, u32[]{:S(2)}) %collective-permute-start.46) | collective-permute-done | bytes 524320 | tf_op jit(solution)/shard_map/ppermute | solution.py:79
  397.7 10.5 %collective-permute-done.47 = bf16[128,2048]{1,0:T(8,128)(2,1)} collective-permute-done((bf16[128,2048]{1,0:T(8,128)(2,1)S(1)}, bf16[128,2048]{1,0:T(8,128)(2,1)}, u32[]{:S(2)}, u32[]{:S(2)}) %collective-permute-start.47) | collective-permute-done | bytes 524320 | tf_op jit(solution)/shard_map/ppermute | solution.py:79
  418.1 11.6 %shard_map.321 = (bf16[512,2048]{1,0:T(8,128)(2,1)}, bf16[512,2048]{1,0:T(8,128)(2,1)}) custom-call(bf16[512,2048]{1,0:T(8,128)(2,1)} %pad_maximum_fusion.3.back_ref.refs_0_, bf16[3,2048,2048]{2,1,0:T(8,128)(2,1)} %all-gather.2.cloned.1.call-done.weight_ref, f32[512,2048]{1,0:T(8,128)} %get-tuple-element.218.gate_ref, f32[512,2048]{1,0:T(8,128)} %get-tuple-element.219.upper_ref), custom_call_target="tpu_custom_call" | custom-call | flops 1 | bytes 1 | tf_op jit(solution)/shard_map/pallas_call | solution.py:229
  429.7 13.8 %shard_map.322 = bf16[512,2048]{1,0:T(8,128)(2,1)} custom-call(bf16[512,2048]{1,0:T(8,128)(2,1)} %get-tuple-element.220.gate_ref.refs_2_, bf16[512,2048]{1,0:T(8,128)(2,1)} %get-tuple-element.221.upper_ref.refs_2_, bf16[3,2048,2048]{2,1,0:T(8,128)(2,1)} %all-gather.2.cloned.1.call-done.weight_ref), custom_call_target="tpu_custom_call" | custom-call | flops 1 | bytes 1 | tf_op jit(solution)/shard_map/pallas_call | solution.py:229
  443.7 38.9 %collective-permute-done.49 = bf16[128,2048]{1,0:T(8,128)(2,1)S(1)} collective-permute-done((bf16[128,2048]{1,0:T(8,128)(2,1)S(1)}, bf16[128,2048]{1,0:T(8,128)(2,1)S(1)}, u32[]{:S(2)}, u32[]{:S(2)}) %collective-permute-start.49) | collective-permute-done | bytes 524320 | tf_op jit(solution)/shard_map/ppermute | solution.py:109
  484.4 11.7 %shard_map.323 = (bf16[512,2048]{1,0:T(8,128)(2,1)}, bf16[512,2048]{1,0:T(8,128)(2,1)}) custom-call(bf16[512,2048]{1,0:T(8,128)(2,1)} %pad_maximum_fusion.4.back_ref.refs_1_, bf16[3,2048,2048]{2,1,0:T(8,128)(2,1)} %all-gather.2.cloned.1.call-done.weight_ref, f32[512,2048]{1,0:T(8,128)} %get-tuple-element.222.gate_ref, f32[512,2048]{1,0:T(8,128)} %get-tuple-element.223.upper_ref), custom_call_target="tpu_custom_call" | custom-call | flops 1 | bytes 1 | tf_op jit(solution)/shard_map/pallas_call | solution.py:229
  496.1 13.9 %shard_map.324 = bf16[512,2048]{1,0:T(8,128)(2,1)} custom-call(bf16[512,2048]{1,0:T(8,128)(2,1)} %get-tuple-element.224.gate_ref.refs_3_, bf16[512,2048]{1,0:T(8,128)(2,1)} %get-tuple-element.225.upper_ref.refs_3_, bf16[3,2048,2048]{2,1,0:T(8,128)(2,1)} %all-gather.2.cloned.1.call-done.weight_ref), custom_call_target="tpu_custom_call" | custom-call | flops 1 | bytes 1 | tf_op jit(solution)/shard_map/pallas_call | solution.py:229
  510.0 9.3 %shard_map.325 = bf16[1024,2048]{1,0:T(8,128)(2,1)} custom-call(s32[4]{0:T(128)S(1)} %broadcast_xor_fusion.order_ref, bf16[512,2048]{1,0:T(8,128)(2,1)} %pad_maximum_fusion.3.back_ref.refs_0_, bf16[512,2048]{1,0:T(8,128)(2,1)} %pad_maximum_fusion.4.back_ref.refs_1_, bf16[512,2048]{1,0:T(8,128)(2,1)} %get-tuple-element.211.inner_ref.refs_2_, ...), custom_call_target="tpu_custom_call" | custom-call | flops 1 | bytes 1 | tf_op jit(solution)/shard_map/pallas_call | solution.py:229
  519.2 9.3 %shard_map.326 = bf16[1024,2048]{1,0:T(8,128)(2,1)} custom-call(s32[4]{0:T(128)S(1)} %broadcast_xor_fusion.order_ref, bf16[512,2048]{1,0:T(8,128)(2,1)} %get-tuple-element.245.hidden_ref.refs_0_, bf16[512,2048]{1,0:T(8,128)(2,1)} %get-tuple-element.246.hidden_ref.refs_1_, bf16[512,2048]{1,0:T(8,128)(2,1)} %get-tuple-element.220.gate_ref.refs_2_, ...), custom_call_target="tpu_custom_call" | custom-call | flops 1 | bytes 1 | tf_op jit(solution)/shard_map/pallas_call | solution.py:229
  529.3 10.4 %shard_map.327 = (bf16[2,256,1024]{2,1,0:T(8,128)(2,1)S(1)}, bf16[2,256,1024]{2,1,0:T(8,128)(2,1)}, bf16[2,256,1024]{2,1,0:T(8,128)(2,1)}, bf16[2,256,1024]{2,1,0:T(8,128)(2,1)}) custom-call(s32[4]{0:T(128)S(1)} %broadcast_xor_fusion.1.order_ref, bf16[512,2048]{1,0:T(8,128)(2,1)} %pad_maximum_fusion.3.back_ref.refs_0_, ...), custom_call_target="tpu_custom_call" | custom-call | flops 1 | bytes 1 | tf_op jit(solution)/shard_map/pallas_call | solution.py:229
  539.7 9.3 %shard_map.328 = bf16[1024,2048]{1,0:T(8,128)(2,1)} custom-call(s32[4]{0:T(128)S(1)} %broadcast_xor_fusion.order_ref, bf16[512,2048]{1,0:T(8,128)(2,1)} %get-tuple-element.245.hidden_ref.refs_0_, bf16[512,2048]{1,0:T(8,128)(2,1)} %get-tuple-element.246.hidden_ref.refs_1_, bf16[512,2048]{1,0:T(8,128)(2,1)} %get-tuple-element.221.upper_ref.refs_2_, ...), custom_call_target="tpu_custom_call" | custom-call | flops 1 | bytes 1 | tf_op jit(solution)/shard_map/pallas_call | solution.py:229
  560.6 10.6 %shard_map.329 = (bf16[2,256,1024]{2,1,0:T(8,128)(2,1)}, bf16[2,256,1024]{2,1,0:T(8,128)(2,1)}, bf16[2,256,1024]{2,1,0:T(8,128)(2,1)}, bf16[2,256,1024]{2,1,0:T(8,128)(2,1)}) custom-call(s32[4]{0:T(128)S(1)} %broadcast_xor_fusion.1.order_ref, bf16[512,2048]{1,0:T(8,128)(2,1)} %get-tuple-element.245.hidden_ref.refs_0_, ...), custom_call_target="tpu_custom_call" | custom-call | flops 1 | bytes 1 | tf_op jit(solution)/shard_map/pallas_call | solution.py:229
  576.7 10.8 %shard_map.330 = (bf16[2,256,1024]{2,1,0:T(8,128)(2,1)S(1)}, bf16[2,256,1024]{2,1,0:T(8,128)(2,1)}, bf16[2,256,1024]{2,1,0:T(8,128)(2,1)}, bf16[2,256,1024]{2,1,0:T(8,128)(2,1)}) custom-call(s32[4]{0:T(128)S(1)} %broadcast_xor_fusion.1.order_ref, bf16[512,2048]{1,0:T(8,128)(2,1)} %get-tuple-element.245.hidden_ref.refs_0_, ...), custom_call_target="tpu_custom_call" | custom-call | flops 1 | bytes 1 | tf_op jit(solution)/shard_map/pallas_call | solution.py:229
  655.1 16.3 %collective-permute-done.65 = bf16[256,1024]{1,0:T(8,128)(2,1)S(1)} collective-permute-done((bf16[256,1024]{1,0:T(8,128)(2,1)S(1)}, bf16[256,1024]{1,0:T(8,128)(2,1)S(1)}, u32[]{:S(2)}, u32[]{:S(2)}) %collective-permute-start.65) | collective-permute-done | bytes 524320 | tf_op jit(solution)/shard_map/ppermute | solution.py:175
  675.9 20.3 %shard_map.333 = (f32[2,1024,512]{2,1,0:T(8,128)}, bf16[1024,512]{1,0:T(8,128)(2,1)}, f32[1024,128]{1,0:T(8,128)S(1)}, f32[2,512]{1,0:T(2,128)S(1)}) custom-call(bf16[3,1024,512]{2,1,0:T(8,128)(2,1)} %get-tuple-element.252.low_ref, bf16[1024,512]{1,0:T(8,128)(2,1)} %bitcast.168, f32[1024,1536]{1,0:T(8,128)} %get-tuple-element.187.query_ref.key_ref.value_ref, ...), custom_call_target="tpu_custom_call" | custom-call | flops 1 | bytes 1 | tf_op jit(solution)/shard_map/pallas_call | solution.py:229
  704.5 14.4 %shard_map.334 = (bf16[1024,1536]{1,0:T(8,128)(2,1)}, bf16[1024,2048]{1,0:T(8,128)(2,1)}) custom-call(f32[2,1024,512]{2,1,0:T(8,128)} %get-tuple-element.261.hats_ref, f32[1024,1536]{1,0:T(8,128)} %get-tuple-element.187.query_ref.key_ref.value_ref, f32[1024,1536]{1,0:T(8,128)} %get-tuple-element.187.query_ref.key_ref.value_ref, ...), custom_call_target="tpu_custom_call" | custom-call | flops 1 | bytes 1 | tf_op jit(solution)/shard_map/pallas_call | solution.py:229
  778.3 12.9 %multiply_subtract_fusion = (f32[3,256,2048]{2,1,0:T(8,128)}, f32[3,256,2048]{2,1,0:T(8,128)}, f32[3,256,2048]{2,1,0:T(8,128)}) fusion(f32[3,256,2048]{2,1,0:T(8,128)S(1)} %bitcast.167, f32[1,256,2048]{2,1,0:T(8,128)} %maximum_bitcast_fusion.2, f32[1,256,2048]{2,1,0:T(8,128)} %maximum_bitcast_fusion.1, f32[1,256,2048]{2,1,0:T(8,128)S(1)} %maximum_bitcast_fusion, ...), kind=kLoop, calls=%fused_computation.5 | loop fusion | flops 25165824 | bytes 44040192 | tf_op jit(solution)/shard_map/sub | solution.py:56
  818.2 13.0 %collective-permute-done.86 = bf16[256,512]{1,0:T(8,128)(2,1)S(1)} collective-permute-done((bf16[256,512]{1,0:T(8,128)(2,1)S(1)}, bf16[256,512]{1,0:T(8,128)(2,1)S(1)}, u32[]{:S(2)}, u32[]{:S(2)}) %collective-permute-start.86) | collective-permute-done | bytes 262176 | tf_op jit(solution)/shard_map/ppermute | solution.py:143
  (502 shorter events, 379.3 us)
Async XLA Ops:
  7.2 257.9 %all-gather.2.cloned.1.call-start = ((), (), s32[]{:S(2)}) async-start(), calls=%async_computation.5 | async-start | bytes 28311552 | tf_op jit(solution)/shard_map/all_gather | solution.py:852
  7.2 29.6 %collective-permute-start = (bf16[256,2048]{1,0:T(8,128)(2,1)}, bf16[256,2048]{1,0:T(8,128)(2,1)S(1)}, u32[]{:S(2)}, u32[]{:S(2)}) collective-permute-start(bf16[256,2048]{1,0:T(8,128)(2,1)} %param.28), channel_id=1, source_target_pairs={{0,1},{1,2},{2,3},{4,5},{5,6},{6,7},{8,9},{9,10},{10,11},{12,13},{... | collective-permute-start | bytes 3145736 | tf_op jit(solution)/shard_map/ppermute | solution.py:79
  39.4 289.9 %reduce-scatter.6.cloned.1.call-start = ((), (), s32[]{:S(2)}) async-start(), calls=%async_computation.6 | async-start | bytes 2621440 | tf_op jit(solution)/shard_map/reduce_scatter | solution.py:70
  41.1 28.2 %collective-permute-start.5 = (bf16[256,2048]{1,0:T(8,128)(2,1)}, bf16[256,2048]{1,0:T(8,128)(2,1)}, u32[]{:S(2)}, u32[]{:S(2)}) collective-permute-start(bf16[256,2048]{1,0:T(8,128)(2,1)} %collective-permute-done.1), channel_id=1, source_target_pairs={{1,0},{2,1},{5,4},{6,5},{9,8},{10,9},{13,12},{14,13},{17,16},{18,1... | collective-permute-start | bytes 3145736 | tf_op jit(solution)/shard_map/ppermute | solution.py:79
  82.4 27.1 %collective-permute-start.9 = (bf16[256,2048]{1,0:T(8,128)(2,1)}, bf16[256,2048]{1,0:T(8,128)(2,1)}, u32[]{:S(2)}, u32[]{:S(2)}) collective-permute-start(bf16[256,2048]{1,0:T(8,128)(2,1)} %collective-permute-done.5), channel_id=1, source_target_pairs={{1,0},{5,4},{9,8},{13,12},{17,16},{21,20},{25,24},{29,28}} | collective-permute-start | bytes 3145736 | tf_op jit(solution)/shard_map/ppermute | solution.py:79
  161.4 29.1 %collective-permute-start.30 = (bf16[256,2048]{1,0:T(8,128)(2,1)S(1)}, bf16[256,2048]{1,0:T(8,128)(2,1)S(1)}, u32[]{:S(2)}, u32[]{:S(2)}) collective-permute-start(bf16[256,2048]{1,0:T(8,128)(2,1)S(1)} %pad_maximum_fusion.6.refs_0_), channel_id=1, source_target_pairs={{0,16},{4,20},{8,24},{12,28},{16,0},{20,4},{24,8},{28,12},{1,17},{... | collective-permute-start | bytes 3145736 | tf_op jit(solution)/shard_map/ppermute | solution.py:175
  162.9 27.6 %collective-permute-start.29 = (bf16[256,2048]{1,0:T(8,128)(2,1)S(1)}, bf16[256,2048]{1,0:T(8,128)(2,1)S(1)}, u32[]{:S(2)}, u32[]{:S(2)}) collective-permute-start(bf16[256,2048]{1,0:T(8,128)(2,1)S(1)} %pad_maximum_fusion.6.refs_0_), channel_id=1, source_target_pairs={{0,8},{4,12},{8,0},{12,4},{16,24},{20,28},{24,16},{28,20},{1,9},{5... | collective-permute-start | bytes 3145736 | tf_op jit(solution)/shard_map/ppermute | solution.py:175
  191.4 28.5 %collective-permute-start.32 = (bf16[1024,512]{1,0:T(8,128)(2,1)S(1)}, bf16[1024,512]{1,0:T(8,128)(2,1)S(1)}, u32[]{:S(2)}, u32[]{:S(2)}) collective-permute-start(bf16[1024,512]{1,0:T(8,128)(2,1)S(1)} %collective-permute-done.28), channel_id=1, source_target_pairs={{1,0},{2,1},{5,4},{6,5},{9,8},{10,9},{13,12},{14,13},{17,16},{18,1... | collective-permute-start | bytes 3145736 | tf_op jit(solution)/shard_map/ppermute | solution.py:79
  223.4 27.1 %collective-permute-start.36 = (bf16[1024,512]{1,0:T(8,128)(2,1)S(1)}, bf16[1024,512]{1,0:T(8,128)(2,1)S(1)}, u32[]{:S(2)}, u32[]{:S(2)}) collective-permute-start(bf16[1024,512]{1,0:T(8,128)(2,1)S(1)} %collective-permute-done.32), channel_id=1, source_target_pairs={{1,0},{5,4},{9,8},{13,12},{17,16},{21,20},{25,24},{29,28}} | collective-permute-start | bytes 3145736 | tf_op jit(solution)/shard_map/ppermute | solution.py:79
  288.1 108.4 %reduce-scatter.8.cloned.1.call-start = ((), (), s32[]{:S(2)}) async-start(), calls=%async_computation.7 | async-start | bytes 2621440 | tf_op jit(solution)/shard_map/reduce_scatter | solution.py:70
  323.2 235.2 %reduce-scatter.10.cloned.1.call-start = ((), (), s32[]{:S(2)}) async-start(), calls=%async_computation.8 | async-start | bytes 2621440 | tf_op jit(solution)/shard_map/reduce_scatter | solution.py:70
  333.5 38.1 %collective-permute-start.45 = (bf16[128,2048]{1,0:T(8,128)(2,1)S(1)}, bf16[128,2048]{1,0:T(8,128)(2,1)S(1)}, u32[]{:S(2)}, u32[]{:S(2)}) collective-permute-start(bf16[128,2048]{1,0:T(8,128)(2,1)S(1)} %fusion.11), channel_id=1, source_target_pairs={{1,0},{2,1},{3,2},{5,4},{6,5},{7,6},{9,8},{10,9},{11,10},{13,12},{... | collective-permute-start | bytes 1572872 | tf_op jit(solution)/shard_map/ppermute | solution.py:79
  334.8 38.1 %collective-permute-start.42 = (bf16[128,2048]{1,0:T(8,128)(2,1)S(1)}, bf16[128,2048]{1,0:T(8,128)(2,1)S(1)}, u32[]{:S(2)}, u32[]{:S(2)}) collective-permute-start(bf16[128,2048]{1,0:T(8,128)(2,1)S(1)} %fusion.11), channel_id=1, source_target_pairs={{0,1},{1,2},{2,3},{4,5},{5,6},{6,7},{8,9},{9,10},{10,11},{12,13},{... | collective-permute-start | bytes 1572872 | tf_op jit(solution)/shard_map/ppermute | solution.py:79
  412.1 31.6 %collective-permute-start.50 = (bf16[128,2048]{1,0:T(8,128)(2,1)S(1)}, bf16[128,2048]{1,0:T(8,128)(2,1)S(1)}, u32[]{:S(2)}, u32[]{:S(2)}) collective-permute-start(bf16[128,2048]{1,0:T(8,128)(2,1)S(1)} %fusion.13), channel_id=1, source_target_pairs={{0,3},{1,0},{2,1},{3,2},{4,7},{5,4},{6,5},{7,6},{8,11},{9,8},{10,9... | collective-permute-start | bytes 1572872 | tf_op jit(solution)/shard_map/ppermute | solution.py:109
  417.5 65.1 %collective-permute-start.49 = (bf16[128,2048]{1,0:T(8,128)(2,1)S(1)}, bf16[128,2048]{1,0:T(8,128)(2,1)S(1)}, u32[]{:S(2)}, u32[]{:S(2)}) collective-permute-start(bf16[128,2048]{1,0:T(8,128)(2,1)S(1)} %fusion.13), channel_id=1, source_target_pairs={{0,2},{1,3},{2,0},{3,1},{4,6},{5,7},{6,4},{7,5},{8,10},{9,11},{10,... | collective-permute-start | bytes 1572872 | tf_op jit(solution)/shard_map/ppermute | solution.py:109
  417.5 65.1 %collective-permute-start.48 = (bf16[128,2048]{1,0:T(8,128)(2,1)S(1)}, bf16[128,2048]{1,0:T(8,128)(2,1)S(1)}, u32[]{:S(2)}, u32[]{:S(2)}) collective-permute-start(bf16[128,2048]{1,0:T(8,128)(2,1)S(1)} %fusion.13), channel_id=1, source_target_pairs={{0,1},{1,2},{2,3},{3,0},{4,5},{5,6},{6,7},{7,4},{8,9},{9,10},{10,1... | collective-permute-start | bytes 1572872 | tf_op jit(solution)/shard_map/ppermute | solution.py:109
  443.6 131.7 %reduce-scatter.12.cloned.1.call-start = ((), (), s32[]{:S(2)}) async-start(), calls=%async_computation.9 | async-start | bytes 2621440 | tf_op jit(solution)/shard_map/reduce_scatter | solution.py:70
  528.5 32.1 %collective-permute-start.52 = (bf16[1024,2048]{1,0:T(8,128)(2,1)}, bf16[1024,2048]{1,0:T(8,128)(2,1)}, u32[]{:S(2)}, u32[]{:S(2)}) collective-permute-start(bf16[1024,2048]{1,0:T(8,128)(2,1)} %shard_map.326), channel_id=1, source_target_pairs={{0,4},{4,0},{8,12},{12,8},{16,20},{20,16},{24,28},{28,24},{1,5},{5... | collective-permute-start | bytes 12582920 | tf_op jit(solution)/shard_map/ppermute | solution.py:175
  529.0 311.4 %reduce-scatter.14.cloned.1.call-start = ((), (), s32[]{:S(2)}) async-start(), calls=%async_computation.10 | async-start | bytes 5242880 | tf_op jit(solution)/shard_map/reduce_scatter | solution.py:70
  548.9 27.8 %collective-permute-start.55 = (bf16[1024,2048]{1,0:T(8,128)(2,1)}, bf16[1024,2048]{1,0:T(8,128)(2,1)}, u32[]{:S(2)}, u32[]{:S(2)}) collective-permute-start(bf16[1024,2048]{1,0:T(8,128)(2,1)} %shard_map.328), channel_id=1, source_target_pairs={{0,4},{4,0},{8,12},{12,8},{16,20},{20,16},{24,28},{28,24},{1,5},{5... | collective-permute-start | bytes 12582920 | tf_op jit(solution)/shard_map/ppermute | solution.py:175
  549.0 27.5 %collective-permute-start.53 = (bf16[2,256,1024]{2,1,0:T(8,128)(2,1)S(1)}, bf16[2,256,1024]{2,1,0:T(8,128)(2,1)}, u32[]{:S(2)}, u32[]{:S(2)}) collective-permute-start(bf16[2,256,1024]{2,1,0:T(8,128)(2,1)S(1)} %get-tuple-element.232), channel_id=1, source_target_pairs={{0,8},{4,12},{8,0},{12,4},{16,24},{20,28},{24,16},{28,20},{1,9},{5... | collective-permute-start | bytes 3145736 | tf_op jit(solution)/shard_map/ppermute | solution.py:175
  604.4 39.3 %collective-permute-start.64 = (bf16[1024,2048]{1,0:T(8,128)(2,1)}, bf16[1024,2048]{1,0:T(8,128)(2,1)}, u32[]{:S(2)}, u32[]{:S(2)}) collective-permute-start(bf16[1024,2048]{1,0:T(8,128)(2,1)} %shard_map.331), channel_id=1, source_target_pairs={{0,4},{4,0},{8,12},{12,8},{16,20},{20,16},{24,28},{28,24},{1,5},{5... | collective-permute-start | bytes 12582920 | tf_op jit(solution)/shard_map/ppermute | solution.py:175
  604.4 68.5 %collective-permute-start.67 = (bf16[2,256,1024]{2,1,0:T(8,128)(2,1)S(1)}, bf16[2,256,1024]{2,1,0:T(8,128)(2,1)S(1)}, u32[]{:S(2)}, u32[]{:S(2)}) collective-permute-start(bf16[2,256,1024]{2,1,0:T(8,128)(2,1)S(1)} %get-tuple-element.247), channel_id=1, source_target_pairs={{0,8},{4,12},{8,0},{12,4},{16,24},{20,28},{24,16},{28,20},{1,9},{5... | collective-permute-start | bytes 3145736 | tf_op jit(solution)/shard_map/ppermute | solution.py:175
  633.9 41.9 %collective-permute-start.68 = (bf16[2,256,1024]{2,1,0:T(8,128)(2,1)}, bf16[2,256,1024]{2,1,0:T(8,128)(2,1)S(1)}, u32[]{:S(2)}, u32[]{:S(2)}) collective-permute-start(bf16[2,256,1024]{2,1,0:T(8,128)(2,1)} %get-tuple-element.248), channel_id=1, source_target_pairs={{0,16},{4,20},{8,24},{12,28},{16,0},{20,4},{24,8},{28,12},{1,17},{... | collective-permute-start | bytes 3145736 | tf_op jit(solution)/shard_map/ppermute | solution.py:175
  639.6 31.8 %collective-permute-start.65 = (bf16[256,1024]{1,0:T(8,128)(2,1)S(1)}, bf16[256,1024]{1,0:T(8,128)(2,1)S(1)}, u32[]{:S(2)}, u32[]{:S(2)}) collective-permute-start(bf16[256,1024]{1,0:T(8,128)(2,1)S(1)} %get-tuple-element.351), channel_id=1, source_target_pairs={{0,16},{4,20},{8,24},{12,28},{16,0},{20,4},{24,8},{28,12},{1,17},{... | collective-permute-start | bytes 1572872 | tf_op jit(solution)/shard_map/ppermute | solution.py:175
  653.1 43.1 %collective-permute-start.70 = (bf16[256,1024]{1,0:T(8,128)(2,1)S(1)}, bf16[256,1024]{1,0:T(8,128)(2,1)S(1)}, u32[]{:S(2)}, u32[]{:S(2)}) collective-permute-start(bf16[256,1024]{1,0:T(8,128)(2,1)S(1)} %get-tuple-element.345), channel_id=1, source_target_pairs={{0,8},{4,12},{8,0},{12,4},{16,24},{20,28},{24,16},{28,20},{1,9},{5... | collective-permute-start | bytes 1572872 | tf_op jit(solution)/shard_map/ppermute | solution.py:175
  654.6 41.7 %collective-permute-start.69 = (bf16[256,1024]{1,0:T(8,128)(2,1)S(1)}, bf16[256,1024]{1,0:T(8,128)(2,1)S(1)}, u32[]{:S(2)}, u32[]{:S(2)}) collective-permute-start(bf16[256,1024]{1,0:T(8,128)(2,1)S(1)} %get-tuple-element.347), channel_id=1, source_target_pairs={{0,16},{4,20},{8,24},{12,28},{16,0},{20,4},{24,8},{28,12},{1,17},{... | collective-permute-start | bytes 1572872 | tf_op jit(solution)/shard_map/ppermute | solution.py:175
  671.4 33.0 %collective-permute-start.74 = (bf16[2,256,1024]{2,1,0:T(8,128)(2,1)}, bf16[2,256,1024]{2,1,0:T(8,128)(2,1)}, u32[]{:S(2)}, u32[]{:S(2)}) collective-permute-start(bf16[2,256,1024]{2,1,0:T(8,128)(2,1)} %get-tuple-element.254), channel_id=1, source_target_pairs={{0,8},{4,12},{8,0},{12,4},{16,24},{20,28},{24,16},{28,20},{1,9},{5... | collective-permute-start | bytes 3145736 | tf_op jit(solution)/shard_map/ppermute | solution.py:175
  672.9 31.6 %collective-permute-start.75 = (bf16[2,256,1024]{2,1,0:T(8,128)(2,1)}, bf16[2,256,1024]{2,1,0:T(8,128)(2,1)S(1)}, u32[]{:S(2)}, u32[]{:S(2)}) collective-permute-start(bf16[2,256,1024]{2,1,0:T(8,128)(2,1)} %get-tuple-element.255), channel_id=1, source_target_pairs={{0,16},{4,20},{8,24},{12,28},{16,0},{20,4},{24,8},{28,12},{1,17},{... | collective-permute-start | bytes 3145736 | tf_op jit(solution)/shard_map/ppermute | solution.py:175
  726.8 30.1 %collective-permute-start.80 = (bf16[1024,1536]{1,0:T(8,128)(2,1)}, bf16[1024,1536]{1,0:T(8,128)(2,1)}, u32[]{:S(2)}, u32[]{:S(2)}) collective-permute-start(bf16[1024,1536]{1,0:T(8,128)(2,1)} %shard_map.335), channel_id=1, source_target_pairs={{0,4},{4,0},{8,12},{12,8},{16,20},{20,16},{24,28},{28,24},{1,5},{5... | collective-permute-start | bytes 9437192 | tf_op jit(solution)/shard_map/ppermute | solution.py:175
  765.5 45.2 %collective-permute-start.81 = (bf16[2,256,768]{2,1,0:T(8,128)(2,1)S(1)}, bf16[2,256,768]{2,1,0:T(8,128)(2,1)}, u32[]{:S(2)}, u32[]{:S(2)}) collective-permute-start(bf16[2,256,768]{2,1,0:T(8,128)(2,1)S(1)} %get-tuple-element.276), channel_id=1, source_target_pairs={{0,8},{4,12},{8,0},{12,4},{16,24},{20,28},{24,16},{28,20},{1,9},{5... | collective-permute-start | bytes 2359304 | tf_op jit(solution)/shard_map/ppermute | solution.py:175
  766.9 43.8 %collective-permute-start.82 = (bf16[2,256,768]{2,1,0:T(8,128)(2,1)S(1)}, bf16[2,256,768]{2,1,0:T(8,128)(2,1)}, u32[]{:S(2)}, u32[]{:S(2)}) collective-permute-start(bf16[2,256,768]{2,1,0:T(8,128)(2,1)S(1)} %get-tuple-element.277), channel_id=1, source_target_pairs={{0,16},{4,20},{8,24},{12,28},{16,0},{20,4},{24,8},{28,12},{1,17},{... | collective-permute-start | bytes 2359304 | tf_op jit(solution)/shard_map/ppermute | solution.py:175
  (151 other events, 1923.5 us)
Sparse Core Ops, SparseCore 0:
  39.5 137.3 all-gather.1
  288.2 41.0 reduce-scatter.5
  331.7 56.9 reduce-scatter.7
  443.7 51.1 reduce-scatter.9
  529.2 46.1 reduce-scatter.11
  739.7 85.9 reduce-scatter.13

commit v3 on v2

--- a/solution.py
+++ b/solution.py
@@ -39,14 +39,6 @@
     return (jnp.cos(angles), jnp.sin(angles))
 
 
-def post_norm(raw_rows, gain_row):
-    return (
-        raw_rows
-        * lax.rsqrt(jnp.mean(raw_rows * raw_rows, axis=-1, keepdims=True) + NORM_EPS)
-        * gain_row
-    )
-
-
 def adamw(weight, gradient, moment_one, moment_two, rate, decay):
     moment_one = BETA_ONE * moment_one + (1.0 - BETA_ONE) * gradient
     moment_two = BETA_TWO * moment_two + (1.0 - BETA_TWO) * gradient * gradient
@@ -67,9 +59,7 @@
 
 
 def chunk_scatter(part):
-    return lax.psum_scatter(
-        part.astype(jnp.bfloat16), "tensor", scatter_dimension=0, tiled=True
-    ).astype(jnp.float32)
+    return lax.psum_scatter(part, "tensor", scatter_dimension=0, tiled=True)
 
 
 def line_hop(step, up, down):
@@ -90,17 +80,15 @@
     ]
 
 
-def line_gather(piece, work=None):
-    hops, given = [], ()
-    pair = (piece, piece)
+def line_gather(piece, work=()):
+    hops, given, pair = [], (), (piece, piece)
     for step in range(1, lax.axis_size("tensor")):
         pair = line_hop(step, *pair)
-        if work is not None and step - 1 < len(work):
+        if step - 1 < len(work):
             given = work[step - 1](given)
             pair, given = lax.optimization_barrier((pair, given))
         hops.append(pair)
-    pieces = line_pieces(piece, hops)
-    return pieces if work is None else (pieces, given)
+    return line_pieces(piece, hops), given
 
 
 def shift_gather(piece):
@@ -112,26 +100,8 @@
     ]
 
 
-def line_scatter(parts):
-    count = lax.axis_size("tensor")
-    here = lax.axis_index("tensor")
-    rising_sum = falling_sum = None
-    for step in range(1, count):
-        up_part = lax.dynamic_index_in_dim(
-            parts, jnp.minimum(here + count - step, count - 1), 0, keepdims=False
-        )
-        down_part = lax.dynamic_index_in_dim(
-            parts, jnp.maximum(here - count + step, 0), 0, keepdims=False
-        )
-        if rising_sum is not None:
-            up_part = up_part + rising_sum.astype(jnp.float32)
-            down_part = down_part + falling_sum.astype(jnp.float32)
-        rising = [(i, i + 1) for i in range(step)]
-        falling = [(i, i - 1) for i in range(count - step, count)]
-        rising_sum = lax.ppermute(up_part.astype(jnp.bfloat16), "tensor", rising)
-        falling_sum = lax.ppermute(down_part.astype(jnp.bfloat16), "tensor", falling)
-    own = lax.dynamic_index_in_dim(parts, here, 0, keepdims=False)
-    return own + rising_sum.astype(jnp.float32) + falling_sum.astype(jnp.float32)
+def together(*values):
+    return lax.optimization_barrier(values)
 
 
 def shift_scatter(values, width):
@@ -149,14 +119,13 @@
     return [[(i, (i + k) % count) for i in range(count)] for k in range(1, count)]
 
 
-def small_sum(values):
-    total = values
-    for pairs in shifts(lax.axis_size("tensor")):
-        total = total + lax.ppermute(values, "tensor", pairs)
-    return total
-
-
-def rows_to_heads(values):
+def small_sum(values, work=lambda: ()):
+    got = [lax.ppermute(values, "tensor", pairs) for pairs in shifts(lax.axis_size("tensor"))]
+    got, given = together(got, work())
+    return sum(got, values), given
+
+
+def rows_to_heads(values, work):
     count = lax.axis_size("tensor")
     here = lax.axis_index("tensor")
     rows, columns = values.shape
@@ -165,9 +134,11 @@
     for k, pairs in enumerate(shifts(count), 1):
         block = lax.dynamic_slice_in_dim(values, lax.rem(here + k, count) * width, width, 1)
         got.append(lax.ppermute(block, "tensor", pairs))
-    return [
+    got, given = together(got, work())
+    parts = [
         pick(here, [got[(i - owner) % count] for i in range(count)]) for owner in range(count)
     ]
+    return jnp.concatenate(parts, axis=0), given
 
 
 def pair_swap(values, bit):
@@ -175,45 +146,50 @@
     return lax.ppermute(values, "dp", [(i, i ^ bit) for i in range(count)])
 
 
-def gather_gains(gains):
-    tensor_count, count = lax.axis_size("tensor"), lax.axis_size("dp")
+def gains_over_tensor(gains):
+    count = lax.axis_size("tensor")
     here = lax.axis_index("tensor")
-    got = [gains] + [lax.ppermute(gains, "tensor", pairs) for pairs in shifts(tensor_count)]
-    block = jnp.concatenate(
-        [pick(here, [got[(i - owner) % tensor_count] for i in range(tensor_count)])
-         for owner in range(tensor_count)],
+    got = [gains] + [lax.ppermute(gains, "tensor", pairs) for pairs in shifts(count)]
+    return jnp.concatenate(
+        [pick(here, [got[(i - owner) % count] for i in range(count)]) for owner in range(count)],
         axis=1,
-    )
+    )[None]
+
+
+def gains_over_dp(blocks, bit):
+    if lax.axis_size("dp") & (lax.axis_size("dp") - 1):
+        return blocks
+    return jnp.concatenate([blocks, pair_swap(blocks, bit)], axis=0)
+
+
+def gains_end(blocks):
+    count = lax.axis_size("dp")
+    if blocks.shape[0] != count:
+        return lax.all_gather(blocks[0], "dp", axis=1, tiled=True)
+    order = jnp.arange(count, dtype=jnp.int32) ^ lax.axis_index("dp")
+    return jnp.moveaxis(blocks[order], 0, 1).reshape(blocks.shape[1], -1)
+
+
+def gains_blocks(grads):
+    count = lax.axis_size("dp")
     if count & (count - 1):
-        return lax.all_gather(block, "dp", axis=1, tiled=True)
-    whole = block[None]
-    bit = 1
-    while bit < count:
-        whole = jnp.concatenate([whole, pair_swap(whole, bit)], axis=0)
-        bit = bit * 2
+        return lax.psum_scatter(grads, "dp", scatter_dimension=1, tiled=True)[None]
     order = jnp.arange(count, dtype=jnp.int32) ^ lax.axis_index("dp")
-    return jnp.moveaxis(whole[order], 0, 1).reshape(gains.shape[0], -1)
-
-
-def scatter_gains(grads):
-    count, tensor_count = lax.axis_size("dp"), lax.axis_size("tensor")
+    return jnp.moveaxis(grads.reshape(grads.shape[0], count, -1), 1, 0)[order]
+
+
+def gains_fold(blocks):
+    bit = blocks.shape[0] // 2
+    return blocks[:bit] + pair_swap(blocks[bit:], bit) if bit else blocks
+
+
+def gains_owned(block):
+    count = lax.axis_size("tensor")
     here = lax.axis_index("tensor")
-    if count & (count - 1):
-        block = lax.psum_scatter(grads, "dp", scatter_dimension=1, tiled=True)
-    else:
-        order = jnp.arange(count, dtype=jnp.int32) ^ lax.axis_index("dp")
-        live = jnp.moveaxis(grads.reshape(grads.shape[0], count, -1), 1, 0)[order]
-        bit = count // 2
-        while bit:
-            live = live[:bit] + pair_swap(live[bit:], bit)
-            bit = bit // 2
-        block = live[0]
-    parts = jnp.moveaxis(block.reshape(block.shape[0], tensor_count, -1), 1, 0)
+    parts = jnp.moveaxis(block.reshape(block.shape[0], count, -1), 1, 0)
     total = lax.dynamic_index_in_dim(parts, here, 0, keepdims=False)
-    for k, pairs in enumerate(shifts(tensor_count), 1):
-        part = lax.dynamic_index_in_dim(
-            parts, lax.rem(here + k, tensor_count), 0, keepdims=False
-        )
+    for k, pairs in enumerate(shifts(count), 1):
+        part = lax.dynamic_index_in_dim(parts, lax.rem(here + k, count), 0, keepdims=False)
         total = total + lax.ppermute(part, "tensor", pairs)
     return total
 
@@ -265,14 +241,16 @@
         return given
     shard, from_x, from_y = given
     half = shard.shape[0] // 2
-    return (*given, pair_swap(from_x[:half], 4), pair_swap(from_y[half:], 2))
-
-
-def plane_three(near):
-    if len(near) == 1:
-        return near[0]
+    near = (*given, pair_swap(from_x[:half], 4), pair_swap(from_y[half:], 2))
+    return (*near, *(pair_swap(piece, 1) for piece in given))
+
+
+def plane_three(given):
+    if len(given) == 1:
+        return given[0]
+    near, far = given[:5], given[5:]
+    far = (*far, pair_swap(near[3], 1), pair_swap(near[4], 1))
     rows, width = near[0].shape
-    far = [pair_swap(piece, 1) for piece in near]
     order = jnp.array([0, 2, 4, 6, 1, 3, 5, 7], jnp.int32) ^ lax.axis_index("dp")
     whole = kernel(
         place_body,
@@ -294,7 +272,7 @@
     step = pl.program_id(0)
     tile = weight_ref.shape[0]
     product = lax.dot_general(
-        mixed_ref[...].reshape(hidden_ref.shape),
+        mixed_ref[...],
         weight_ref[...],
         COLUMN_CONTRACT,
         preferred_element_type=jnp.float32,
@@ -326,7 +304,7 @@
         out_norm_body,
         (width // tile,),
         [
-            part,
+            whole_block((rows, width)),
             pl.BlockSpec((tile, width), lambda n: (n, 0)),
             part,
             whole_block((1, width)),
@@ -687,6 +665,109 @@
     )
 
 
+def norm_parts(raw):
+    scale = lax.rsqrt(jnp.mean(raw * raw, axis=-1, keepdims=True) + NORM_EPS)
+    return scale, raw * scale
+
+
+def norm_back(scale, hat, back, gain):
+    back_hat = back * gain
+    return scale * (back_hat - hat * jnp.mean(back_hat * hat, axis=-1, keepdims=True))
+
+
+def turn_body(
+    place_ref, raw_mlp_ref, raw_ref, tokens_ref, back_ref, gains_ref, out_ref, low_ref, gain_out_ref
+):
+    _, attn_hat = norm_parts(raw_ref[...])
+    scale, hat = norm_parts(raw_mlp_ref[...].astype(jnp.float32))
+    hidden = tokens_ref[...].astype(jnp.float32) + attn_hat * gains_ref[0:1]
+    out_ref[...] = (hidden + hat * gains_ref[1:2]).astype(jnp.bfloat16)
+    back = back_ref[...].astype(jnp.float32)
+    low_ref[...] = norm_back(scale, hat, back, gains_ref[1:2]).astype(jnp.bfloat16)
+    gain_out_ref[...] = jnp.sum(back * hat, axis=0, keepdims=True)
+
+
+def turn_rows(raw_mlp, raw_attn, tokens, back, chunk, gains):
+    rows, width = raw_mlp.shape
+    chunk_spec = pl.BlockSpec((rows, width), lambda n, place_ref: (chunk, 0))
+    first = pl.BlockSpec((rows, width), lambda n, place_ref: (0, 0))
+    return kernel(
+        turn_body,
+        (1,),
+        [
+            first,
+            pl.BlockSpec((rows, width), lambda n, place_ref: (place_ref[0], 0)),
+            chunk_spec,
+            chunk_spec,
+            whole_block(gains.shape),
+        ],
+        [first, first, whole_block((1, width))],
+        [
+            jax.ShapeDtypeStruct((rows, width), jnp.bfloat16),
+            jax.ShapeDtypeStruct((rows, width), jnp.bfloat16),
+            jax.ShapeDtypeStruct((1, width), jnp.float32),
+        ],
+        (raw_mlp, raw_attn, tokens, back, gains),
+        order=lax.axis_index("tensor")[None],
+    )
+
+
+def output_back_body(
+    place_ref,
+    sum_ref,
+    raw_ref,
+    back_ref,
+    gains_ref,
+    weight_ref,
+    hidden_ref,
+    low_ref,
+    gain_out_ref,
+    rows_ref,
+):
+    @pl.when(pl.program_id(0) == 0)
+    def _():
+        scale, hat = norm_parts(raw_ref[...])
+        back = back_ref[...].astype(jnp.float32) + sum_ref[...].astype(jnp.float32)
+        hidden_ref[...] = back
+        gain_out_ref[...] = jnp.sum(back * hat, axis=0, keepdims=True)
+        low_ref[...] = norm_back(scale, hat, back, gains_ref[0:1]).astype(jnp.bfloat16)
+
+    rows_ref[...] = jnp.dot(
+        low_ref[...], weight_ref[...], preferred_element_type=jnp.float32
+    ).astype(jnp.bfloat16)
+
+
+def output_back_rows(summed, raw_attn, back, chunk, gains, weight):
+    rows, width = summed.shape
+    tile = min(512, width)
+    first = pl.BlockSpec((rows, width), lambda n, place_ref: (0, 0))
+    return kernel(
+        output_back_body,
+        (width // tile,),
+        [
+            first,
+            pl.BlockSpec((rows, width), lambda n, place_ref: (place_ref[0], 0)),
+            pl.BlockSpec((rows, width), lambda n, place_ref: (chunk, 0)),
+            whole_block(gains.shape),
+            pl.BlockSpec((width, tile), lambda n, place_ref: (0, n)),
+        ],
+        [
+            first,
+            first,
+            whole_block((1, width)),
+            pl.BlockSpec((rows, tile), lambda n, place_ref: (0, n)),
+        ],
+        [
+            jax.ShapeDtypeStruct((rows, width), jnp.float32),
+            jax.ShapeDtypeStruct((rows, width), jnp.bfloat16),
+            jax.ShapeDtypeStruct((1, width), jnp.float32),
+            jax.ShapeDtypeStruct((rows, width), jnp.bfloat16),
+        ],
+        (summed, raw_attn, back, gains, weight),
+        order=lax.axis_index("tensor")[None],
+    )
+
+
 def product_of(left_refs, right_refs):
     total = None
     for left_ref, right_ref in zip(left_refs, right_refs):
@@ -804,21 +885,21 @@
     x_next = wide(kept[2][0]) + wide(first[0][1])
     y_next = wide(kept[3][0]) + wide(first[1][0])
     return [
-        wide(kept[2][1]) + wide(first[0][0]),
-        wide(kept[3][1]) + wide(first[1][1]),
         pair_swap(x_next.astype(jnp.bfloat16), 4),
         pair_swap(y_next.astype(jnp.bfloat16), 2),
     ]
 
 
-def exchange_end(second):
-    if len(second) == 1:
+def exchange_end(kept, first, second):
+    if len(kept) == 1:
         return lax.psum_scatter(
-            second[0].astype(jnp.bfloat16), "dp", scatter_dimension=0, tiled=True
+            kept[0].astype(jnp.bfloat16), "dp", scatter_dimension=0, tiled=True
         ).astype(jnp.float32)
-    return jnp.concatenate(
-        [second[half] + second[2 + half].astype(jnp.float32) for half in range(2)], axis=1
-    )
+    halves = [
+        wide(kept[2][1]) + wide(first[0][0]) + wide(second[0]),
+        wide(kept[3][1]) + wide(first[1][1]) + wide(second[1]),
+    ]
+    return jnp.concatenate(halves, axis=1)
 
 
 def local(
@@ -847,178 +928,221 @@
     mlp_low = w_mlp.astype(jnp.bfloat16)
     positions = doc_positions(lengths, seq_len).reshape(total_rows)
 
-    def second_hop(given):
-        mlp_shard = after(mlp_low, given)
-        return plane_two(given), lax.all_gather(mlp_shard, "dp", axis=1, tiled=True), mlp_shard
-
-    def third_hop(given):
-        cos_table, sin_table = rope_tables(positions, HDIM)
-        cosine = jnp.concatenate([cos_table, cos_table], axis=1)
-        sine = jnp.concatenate([-sin_table, sin_table], axis=1)
-        gains = gather_gains(after(norm_gains.astype(jnp.bfloat16), given))
-        return plane_three(given), cosine, sine, gains
-
-    hop, near = lax.optimization_barrier((line_hop(1, tokens, tokens), plane_one(qkv_shard)))
+    gains_low = norm_gains.astype(jnp.bfloat16)
+    hop, near, gains, mlp_low = lax.optimization_barrier(
+        (line_hop(1, tokens, tokens), plane_one(qkv_shard), gains_over_tensor(gains_low), mlp_low)
+    )
     hops = [hop]
-    near, mlp_full, mlp_shard = second_hop(near)
-    hop, near, mlp_shard = lax.optimization_barrier((line_hop(2, *hop), near, mlp_shard))
+    mlp_shard = after(mlp_low, near)
+    mlp_full = lax.all_gather(mlp_shard, "dp", axis=1, tiled=True)
+    hop, near, gains, mlp_shard = lax.optimization_barrier(
+        (line_hop(2, *hop), plane_two(near), gains_over_dp(gains, 1), mlp_shard)
+    )
     hops.append(hop)
-    hop, given = lax.optimization_barrier((line_hop(3, *hop), third_hop(near)))
+    cos_table, sin_table = rope_tables(positions, HDIM)
+    cosine = jnp.concatenate([cos_table, cos_table], axis=1)
+    sine = jnp.concatenate([-sin_table, sin_table], axis=1)
+    hop, qkv_full, gains, cosine, sine = lax.optimization_barrier(
+        (line_hop(3, *hop), plane_three(near), gains_over_dp(gains, 2), cosine, sine)
+    )
     hops.append(hop)
-    qkv_full, cosine, sine, gain_full = given
     whole_tokens = jnp.concatenate(line_pieces(tokens, hops), axis=0)
+    bit = 4
+    while bit < lax.axis_size("dp"):
+        gains = gains_over_dp(gains, bit)
+        bit = bit * 2
+    gain_full = gains_end(gains)
     gain_values = gain_full.astype(jnp.float32)
     column_start = tensor_index * local_width
     head_gains = lax.dynamic_slice_in_dim(gain_values[2:], column_start, local_width, 1)
 
-    def summed_lanes(lanes):
-        rows = lanes.shape[0]
+    def summed_lanes(lanes, work=lambda: ()):
         flat = lax.optimization_barrier(lanes[:, :2].T.reshape(-1, HDIM))
-        return small_sum(flat).reshape(2, rows)
+        total, given = small_sum(flat, work)
+        return total.reshape(2, lanes.shape[0]), given
 
     def in_lanes(values):
         return jnp.pad(values.T, ((0, 0), (0, HDIM - 2)))
 
     projected, square_lanes = project(whole_tokens, qkv_full)
-    inverse = lax.rsqrt(summed_lanes(square_lanes) / model_width + NORM_EPS)
+    inverse = lax.rsqrt(summed_lanes(square_lanes)[0] / model_width + NORM_EPS)
     inverse_lanes = in_lanes(inverse)
-    out_piece = after(w_attn[3].astype(jnp.bfloat16), inverse_lanes)
+    out_piece = after(w_attn[3].astype(jnp.bfloat16), whole_tokens)
     out_shard = jnp.concatenate(shift_gather(out_piece), axis=1)
+    inverse_lanes, out_shard = lax.optimization_barrier((inverse_lanes, out_shard))
     low_heads, mixed_low = attend(projected, inverse_lanes, head_gains, cosine, sine)
-    out_shard, mixed_low = lax.optimization_barrier((out_shard, mixed_low))
-    pieces, out_full = line_gather(
-        mixed_low, (lambda _: plane_one(out_shard), plane_two, plane_three)
-    )
-    whole_mixed = jnp.concatenate(pieces, axis=1)
-    mixed_parted = whole_mixed.reshape(tensor_size, CHUNKS, chunk_rows, model_width)
+    mixed_pieces = mixed_low.reshape(tensor_size, CHUNKS, chunk_rows, local_width)
+
+    def mixed_chunk(chunk):
+        return mixed_pieces[:, chunk].reshape(tensor_size * chunk_rows, local_width)
+
     tokens_parted = whole_tokens.reshape(tensor_size, CHUNKS, chunk_rows, model_width)
 
     def own_part(values):
         parted = values.reshape((tensor_size, chunk_rows) + values.shape[1:])
         return lax.dynamic_index_in_dim(parted, tensor_index, 0, keepdims=False)
 
-    def own_rows(values, chunk):
-        return values[chunk * chunk_rows : (chunk + 1) * chunk_rows].astype(jnp.float32)
-
     chunks = range(CHUNKS)
-    raw_attn, hidden_low, gate = ([None] * CHUNKS for _ in range(3))
+    mixed, raw_attn, hidden_low, gate = ([None] * CHUNKS for _ in range(4))
     upper, inner_low, down_part, raw_mlp = ([None] * CHUNKS for _ in range(4))
+
+    def forward(chunk):
+        def first(_):
+            hidden_low[chunk], raw_attn[chunk] = out_norm(
+                mixed[chunk], out_full, tokens_parted, chunk, gain_values[:1]
+            )
+            return hidden_low[chunk], raw_attn[chunk]
+
+        def second(given):
+            hidden_low[chunk], raw_attn[chunk] = given
+            outs = mlp_in(hidden_low[chunk], mlp_full)
+            inner_low[chunk], gate[chunk], upper[chunk] = outs
+            return outs
+
+        def third(given):
+            inner_low[chunk], gate[chunk], upper[chunk] = given
+            down_part[chunk] = mlp_out(inner_low[chunk], mlp_full)
+            return down_part[chunk]
+
+        return first, second, third
+
+    pieces, out_full = lax.optimization_barrier(
+        (line_gather(mixed_chunk(0))[0], plane_three(plane_two(plane_one(out_shard))))
+    )
     for chunk in chunks:
-        mixed = mixed_parted
-        if chunk:
-            mixed = after(mixed, down_part[chunk - 1])
-        hidden_low[chunk], raw_attn[chunk] = out_norm(
-            mixed, out_full, tokens_parted, chunk, gain_values[:1]
+        mixed[chunk] = jnp.concatenate(pieces, axis=1)
+        if chunk + 1 < CHUNKS:
+            piece = after(mixed_chunk(chunk + 1), out_full if chunk == 0 else mixed[chunk])
+            pieces, down_part[chunk] = line_gather(piece, forward(chunk))
+        else:
+            given = ()
+            for work in forward(chunk):
+                given = work(given)
+        raw_mlp[chunk] = chunk_scatter(down_part[chunk])
+
+    own_mixed = [own_part(mixed[chunk]) for chunk in chunks]
+    out_parts, back_raw_mlp, gains_mlp = ([None] * CHUNKS for _ in range(3))
+    gathered, gate_low, upper_low, hidden_part, back_sum = ([None] * CHUNKS for _ in range(5))
+
+    def turn(chunk, raw):
+        out_parts[chunk], back_raw_mlp[chunk], gains_mlp[chunk] = turn_rows(
+            raw, raw_attn[chunk], tokens, cotangent, chunk, gain_values
         )
-        inner_low[chunk], gate[chunk], upper[chunk] = mlp_in(hidden_low[chunk], mlp_full)
-        down_part[chunk] = mlp_out(inner_low[chunk], mlp_full)
-        raw_mlp[chunk] = chunk_scatter(down_part[chunk])
-
-    own_mixed = [
-        lax.dynamic_index_in_dim(mixed_parted[:, chunk], tensor_index, 0, keepdims=False)
-        for chunk in chunks
-    ]
-    out_parts, back_raw_mlp, gains_mlp, attn_pulls = ([None] * CHUNKS for _ in range(4))
-    gathered, gate_low, upper_low, hidden_part, back_sum = ([None] * CHUNKS for _ in range(5))
-
-    def turn(chunk, raw):
-        attn_normed, attn_pulls[chunk] = jax.vjp(
-            post_norm, own_part(raw_attn[chunk]), gain_values[0]
-        )
-        mlp_normed, mlp_pull = jax.vjp(post_norm, raw, gain_values[1])
-        hidden = own_rows(tokens, chunk) + attn_normed
-        out_parts[chunk] = (hidden + mlp_normed).astype(jnp.bfloat16)
-        back_raw, gains_mlp[chunk] = mlp_pull(own_rows(cotangent, chunk))
-        back_raw_mlp[chunk] = back_raw.astype(jnp.bfloat16)
-
-    def backward(chunk, gathered_rows):
-        gate_low[chunk], upper_low[chunk] = mlp_back(
-            gathered_rows, mlp_full, gate[chunk], upper[chunk]
-        )
-        hidden_part[chunk] = hidden_back(gate_low[chunk], upper_low[chunk], mlp_full)
-        back_sum[chunk] = chunk_scatter(hidden_part[chunk])
+
+    def gather_rows(chunk, hops):
+        pieces = line_pieces(back_raw_mlp[chunk], hops)
+        gathered[chunk] = jnp.concatenate(pieces, axis=0)
+
+    def back_inner(chunk):
+        return mlp_back(gathered[chunk], mlp_full, gate[chunk], upper[chunk])
+
+    def back_hidden_part(chunk):
+        return hidden_back(gate_low[chunk], upper_low[chunk], mlp_full)
 
     turn(0, raw_mlp[0])
-    gathered[0] = jnp.concatenate(line_gather(back_raw_mlp[0]), axis=0)
-    for chunk in chunks:
-        rows = gathered[chunk]
-        following = chunk + 1 < CHUNKS
-        if following:
-            turn(chunk + 1, after(raw_mlp[chunk + 1], rows))
-            rows = after(rows, back_raw_mlp[chunk + 1])
-        if following:
-            gathered[chunk + 1] = jnp.concatenate(shift_gather(back_raw_mlp[chunk + 1]), axis=0)
-        backward(chunk, rows)
+    early_one = line_hop(1, back_raw_mlp[0], back_raw_mlp[0])
+    early_two, late_raw = together(line_hop(2, *early_one), raw_mlp[1])
+    turn(1, late_raw)
+    early_three, late_one = together(
+        line_hop(3, *early_two), line_hop(1, back_raw_mlp[1], back_raw_mlp[1])
+    )
+    gather_rows(0, (early_one, early_two, early_three))
+    late_two, (gate_low[0], upper_low[0]) = together(line_hop(2, *late_one), back_inner(0))
+    late_three, hidden_part[0] = together(line_hop(3, *late_two), back_hidden_part(0))
+    back_sum[0] = chunk_scatter(hidden_part[0])
+    gather_rows(1, (late_one, late_two, late_three))
+    gate_low[1], upper_low[1] = back_inner(1)
+    hidden_part[1] = back_hidden_part(1)
+    back_sum[1] = chunk_scatter(hidden_part[1])
     out_tokens = jnp.concatenate(out_parts, axis=0)
+
+    back_hidden, gains_attn, back_raw_attn, back_rows = ([None] * CHUNKS for _ in range(4))
+
+    def output_back(chunk, rows):
+        outs = output_back_rows(rows, raw_attn[chunk], cotangent, chunk, gain_values, out_full)
+        back_hidden[chunk], back_raw_attn[chunk], gains_attn[chunk], back_rows[chunk] = outs
 
     down_left = after(gathered, hidden_part)
     down_sent = grad_sent(down_left, inner_low)
     gate_sent = grad_sent(after(hidden_low, down_sent), gate_low)
-    down_kept = grad_kept(after(down_left, gate_sent), inner_low, pair_swap(down_sent, 1))
+    for chunk in chunks[:-1]:
+        output_back(chunk, after(back_sum[chunk], gate_sent))
+    down_kept = grad_kept(
+        after(down_left, gate_sent, back_rows[:-1]), inner_low, pair_swap(down_sent, 1)
+    )
     down_one = exchange_one(down_kept)
     upper_sent = grad_sent(after(hidden_low, down_kept), upper_low)
     gate_kept = grad_kept(after(hidden_low, upper_sent), gate_low, pair_swap(gate_sent, 1))
-    upper_kept = grad_kept(
-        after(hidden_low, gate_kept, down_one), upper_low, pair_swap(upper_sent, 1)
-    )
-    gate_one = exchange_one(gate_kept)
+    output_back(CHUNKS - 1, after(back_sum[-1], gate_kept))
+    gate_one = exchange_one(after(gate_kept, back_rows))
+    back_mixed, (down_one, upper_kept, out_sent) = rows_to_heads(
+        jnp.concatenate(back_rows, axis=0),
+        lambda: (
+            down_one,
+            grad_kept(after(hidden_low, back_rows), upper_low, pair_swap(upper_sent, 1)),
+            grad_sent(back_raw_attn, own_mixed),
+        ),
+    )
     upper_one = exchange_one(upper_kept)
-
-    back_hidden, gains_attn, back_raw_attn, back_rows = ([None] * CHUNKS for _ in range(4))
-    back_heads = [None] * CHUNKS
-    for chunk in chunks:
-        rows = after(back_sum[chunk], upper_kept if chunk else gate_kept)
-        back_hidden[chunk] = own_rows(cotangent, chunk) + rows
-        back_raw, gains_attn[chunk] = attn_pulls[chunk](back_hidden[chunk])
-        back_raw_attn[chunk] = back_raw.astype(jnp.bfloat16)
-        if chunk:
-            back_raw_attn[chunk] = after(back_raw_attn[chunk], gate_one)
-        back_rows[chunk] = jnp.dot(
-            back_raw_attn[chunk], out_full, preferred_element_type=jnp.float32
-        ).astype(jnp.bfloat16)
-        back_heads[chunk] = rows_to_heads(back_rows[chunk])
-    back_mixed = jnp.stack([jnp.stack(parts) for parts in back_heads], axis=1)
-    back_mixed = back_mixed.reshape(total_rows, local_width)
-    out_sent = grad_sent(back_raw_attn, own_mixed)
-    down_two = exchange_two(down_kept, after(down_one, upper_kept))
-    out_kept = grad_kept(back_raw_attn, own_mixed, pair_swap(out_sent, 1))
-    out_one = exchange_one(out_kept)
-    back_mixed = after(back_mixed, out_kept, down_two, upper_one)
-
     back_hats, value_back, cross_lanes, head_gain_grads = attend_back(
         low_heads, back_mixed, projected, inverse_lanes, head_gains, cosine, sine
     )
-    gate_two = exchange_two(gate_kept, after(gate_one, back_rows))
-    cross_sums = summed_lanes(after(cross_lanes, gate_two))
+    cross_lanes = after(cross_lanes, gate_one)
+    down_two = exchange_two(down_kept, after(down_one, cross_lanes))
+    cross_sums, out_kept = summed_lanes(
+        cross_lanes,
+        lambda: grad_kept(
+            after(back_raw_attn, cross_lanes), own_mixed, pair_swap(out_sent, 1)
+        ),
+    )
+    out_one = exchange_one(out_kept)
     mean_lanes = in_lanes(cross_sums / model_width)
-    upper_two = exchange_two(upper_kept, after(upper_one, value_back))
-    mean_lanes = after(mean_lanes, out_one)
     qkv_back, tokens_part = tokens_back_part(
         back_hats, projected, value_back, inverse_lanes, mean_lanes, qkv_full
     )
     tokens_back = chunk_scatter(tokens_part)
-    qkv_left = [after(whole_tokens, tokens_part)]
-    qkv_sent = grad_sent(qkv_left, [qkv_back])
-    out_two = exchange_two(out_kept, after(out_one, tokens_part))
-    qkv_kept = grad_kept(
-        after(qkv_left, upper_two, out_two), [qkv_back], pair_swap(qkv_sent, 1)
-    )
-    qkv_one = exchange_one(qkv_kept)
-
     gain_grad = jnp.zeros((4, model_width), jnp.float32)
-    gain_grad = gain_grad.at[0].set(sum(gains_attn)).at[1].set(sum(gains_mlp))
+    gain_grad = gain_grad.at[0].set(sum(gains_attn)[0]).at[1].set(sum(gains_mlp)[0])
     gain_grad = lax.dynamic_update_slice(
         gain_grad, head_gain_grads, (jnp.int32(2), column_start)
     )
-    gain_final = scatter_gains(after(gain_grad, qkv_kept))
-    gate_two, upper_two, down_two = after((gate_two, upper_two, down_two), qkv_kept)
-    mlp_owned = jnp.stack([exchange_end(gate_two), exchange_end(upper_two), exchange_end(down_two)])
-    new_mlp, new_moment_mlp, new_square_mlp = adamw(
-        w_mlp, mlp_owned, moment_mlp, square_mlp, RATE_MATRIX, DECAY_MATRIX
-    )
-    qkv_two = exchange_two(qkv_kept, after(qkv_one, new_mlp))
-    out_owned = shift_scatter(exchange_end(after(out_two, new_mlp)), local_width)
-    qkv_owned = exchange_end(qkv_two)
+    gains = gains_blocks(gain_grad)
+    qkv_left, gains = after(([whole_tokens], gains), tokens_part)
+    while gains.shape[0] > 8:
+        gains = gains_fold(gains)
+
+    down_two, upper_one, qkv_sent, gains = together(
+        down_two,
+        upper_one,
+        grad_sent(qkv_left, [qkv_back]),
+        gains_fold(gains),
+    )
+    gate_two, upper_two, out_one, qkv_kept, gains = together(
+        exchange_two(gate_kept, after(gate_one, qkv_sent)),
+        exchange_two(upper_kept, upper_one),
+        out_one,
+        grad_kept(qkv_left, [qkv_back], pair_swap(qkv_sent, 1)),
+        gains_fold(gains),
+    )
+    mlp_owned = jnp.stack(
+        [
+            exchange_end(gate_kept, gate_one, gate_two),
+            exchange_end(upper_kept, upper_one, upper_two),
+            exchange_end(down_kept, down_one, down_two),
+        ]
+    )
+    out_two, qkv_one, (new_mlp, new_moment_mlp, new_square_mlp), gains = together(
+        exchange_two(out_kept, out_one),
+        exchange_one(qkv_kept),
+        adamw(w_mlp, mlp_owned, moment_mlp, square_mlp, RATE_MATRIX, DECAY_MATRIX),
+        gains_fold(gains),
+    )
+    qkv_two, out_owned, gain_final = together(
+        exchange_two(qkv_kept, qkv_one),
+        shift_scatter(exchange_end(out_kept, out_one, out_two), local_width),
+        gains_owned(gains[0]),
+    )
+    qkv_owned = exchange_end(qkv_kept, qkv_one, qkv_two)
     attn_owned = jnp.stack(
         [qkv_owned[:, k * local_width : (k + 1) * local_width] for k in range(3)] + [out_owned]
     )
@@ -1030,7 +1154,7 @@
         norm_gains, gain_final, moment_gains, square_gains, RATE_GAIN, 0.0
     )
     tokens_back = after(tokens_back, new_mlp, new_attn, new_gains)
-    grad_tokens = (jnp.concatenate(back_hidden, axis=0) + tokens_back).astype(jnp.bfloat16)
+    grad_tokens = (jnp.concatenate(back_hidden, axis=0) + tokens_back.astype(jnp.float32)).astype(jnp.bfloat16)
     return (
         out_tokens,
         grad_tokens,

time: 865 us -> 800 us (0.925)
  waiting for transfers between devices: 314 us -> 233 us
  Pallas kernels: 286 us -> 305 us
  starting transfers between devices: 114 us -> 127 us
  other arithmetic: 92.9 us -> 82.4 us
  matrix products: 9.36 us -> 0 us
    ppermute x6 -> x3, waiting for transfers between devices: 44.3 us -> 3.4 us  [shift_gather(): lax.ppermute(piece, 'tensor', pairs)]
    ppermute x49, waiting for transfers between devices: 96.9 us -> 59.9 us  [pair_swap(): return lax.ppermute(values, 'dp', [(i, i ^ bit) for i in range(count)])]
    pallas_call x26 -> x30, Pallas kernels: 286 us -> 305 us  [kernel(): pl.pallas_call(body, grid_spec=spec, out_shape=out_shape, compiler_params...]
    reduce_scatter x5, waiting for transfers between devices: 8.63 us -> 24 us  [chunk_scatter(): return lax.psum_scatter(part, 'tensor', scatter_dimension=0, tiled=True)]
    ppermute x9 -> x15, starting transfers between devices: 22.4 us -> 36 us  [line_hop(): lax.ppermute(up, 'tensor', rising)]
    convert_element_type x9 -> x3, other arithmetic: 12.7 us -> 2.49 us  [the longest x1 2.48 us: local(): (jnp.concatenate(back_hidden, axis=0) + tokens_back.astype(jnp.float32))....]
    ppermute x9 -> x15, waiting for transfers between devices: 128 us -> 118 us  [line_hop(): lax.ppermute(down, 'tensor', falling)]
    dot_general x2 -> x0, matrix products: 9.36 us -> none  [local(): jnp.dot(back_raw_attn[chunk], out_full, preferred_element_type=jnp.float32)]
  transfers between devices with their start and end apart: 100 -> 106, of which waited for: 51 -> 44; matrix products, arithmetic and copies ran while one was open for 12% -> 11% of each run, Pallas kernels for 28% -> 38%
where the time goes in v3:
time: 800 us; the launch traced here: 785 us
  Pallas kernels  305 us (38%)
  waiting for transfers between devices  233 us (29%)
  starting transfers between devices  127 us (16%)
  other arithmetic  82.4 us (10%)
  local copies, waits for them, and re-layouts  21.8 us (3%)
  between operations  16.1 us (2%)
    pallas_call x30, Pallas kernels, kernel(): pl.pallas_call(body, grid_spec=spec, out_shape=out_shape, compiler_params...  305 us
    ppermute x15, waiting for transfers between devices, line_hop(): lax.ppermute(down, 'tensor', falling)  118 us
    ppermute x49, waiting for transfers between devices, pair_swap(): return lax.ppermute(values, 'dp', [(i, i ^ bit) for i in range(count)])  59.9 us
    ppermute x49, starting transfers between devices, pair_swap(): return lax.ppermute(values, 'dp', [(i, i ^ bit) for i in range(count)])  36.9 us
    ppermute x15, starting transfers between devices, line_hop(): lax.ppermute(up, 'tensor', rising)  36 us
    reduce_scatter x5, waiting for transfers between devices, chunk_scatter(): return lax.psum_scatter(part, 'tensor', scatter_dimension=0, tiled=True)  24 us
    ppermute x15, starting transfers between devices, line_hop(): lax.ppermute(down, 'tensor', falling)  19.4 us
    sub x3, other arithmetic, adamw(): weight * (1.0 - rate * decay) - rate * update  16.9 us
  transfers between devices with their start and end apart: 106, of which 44 were waited for; matrix products, arithmetic and copies ran while one was open for 11% of the time, Pallas kernels for 38%

profile of v3, /device:TPU:0, one launch (start us, length us, event | category | flops | bytes accessed | tf_op | source)
XLA Modules:
  0.0 785.5 jit_solution(14276803952536873630)
XLA Ops:
  23.1 13.7 %collective-permute-done.5 = bf16[4,64]{1,0:T(4,128)(2,1)S(1)} collective-permute-done((bf16[4,64]{1,0:T(4,128)(2,1)S(1)}, bf16[4,64]{1,0:T(4,128)(2,1)S(1)}, u32[]{:S(2)}, u32[]{:S(2)}) %collective-permute-start.5) | collective-permute-done | bytes 544 | tf_op jit(solution)/shard_map/ppermute | solution.py:152
  62.4 19.9 %collective-permute-done.8 = bf16[256,2048]{1,0:T(8,128)(2,1)} collective-permute-done((bf16[256,2048]{1,0:T(8,128)(2,1)}, bf16[256,2048]{1,0:T(8,128)(2,1)}, u32[]{:S(2)}, u32[]{:S(2)}) %collective-permute-start.8) | collective-permute-done | bytes 1048608 | tf_op jit(solution)/shard_map/ppermute | solution.py:69
  114.2 11.6 %shard_map.312 = (f32[1024,1536]{1,0:T(8,128)}, f32[1024,128]{1,0:T(8,128)S(1)}) custom-call(bf16[1024,2048]{1,0:T(8,128)(2,1)} %pad_maximum_fusion.1.tokens_ref.refs_0_, bf16[2048,1536]{1,0:T(8,128)(2,1)} %bitcast.119), custom_call_target="tpu_custom_call" | custom-call | flops 1 | bytes 1 | tf_op jit(solution)/shard_map/pallas_call | solution.py:205
  140.5 14.6 %shard_map.313 = (bf16[3,1024,512]{2,1,0:T(8,128)(2,1)}, bf16[1024,512]{1,0:T(8,128)(2,1)}) custom-call(f32[1024,1536]{1,0:T(8,128)} %get-tuple-element.251.query_ref.key_ref.value_ref, f32[1024,1536]{1,0:T(8,128)} %get-tuple-element.251.query_ref.key_ref.value_ref, f32[1024,1536]{1,0:T(8,128)} %get-tuple-element.251.query_ref.key_ref.value_ref, ...), custom_call_target="tpu_custom_call" | custom-call | flops 1 | bytes 1 | tf_op jit(solution)/shard_map/pallas_call | solution.py:205
  173.7 14.0 %collective-permute-done.31 = bf16[512,512]{1,0:T(8,128)(2,1)S(1)} collective-permute-done((bf16[512,512]{1,0:T(8,128)(2,1)S(1)}, bf16[512,512]{1,0:T(8,128)(2,1)S(1)}, u32[]{:S(2)}, u32[]{:S(2)}) %collective-permute-start.31) | collective-permute-done | bytes 524320 | tf_op jit(solution)/shard_map/ppermute | solution.py:69
  225.6 11.6 %shard_map.315 = (bf16[512,2048]{1,0:T(8,128)(2,1)}, f32[512,2048]{1,0:T(8,128)}) custom-call(bf16[512,2048]{1,0:T(8,128)(2,1)} %copy-done.13, bf16[2048,2048]{1,0:T(8,128)(2,1)} %bitcast.113, bf16[4,2,128,2048]{3,2,1,0:T(8,128)(2,1)} %bitcast.117, f32[1,2048]{1,0:T(1,128)S(1)} %bitcast.111), custom_call_target="tpu_custom_call" | custom-call | flops 1 | bytes 1 | tf_op jit(solution)/shard_map/pallas_call | solution.py:205
  239.3 14.3 %shard_map.316 = (bf16[512,2048]{1,0:T(8,128)(2,1)}, f32[512,2048]{1,0:T(8,128)}, f32[512,2048]{1,0:T(8,128)}) custom-call(bf16[512,2048]{1,0:T(8,128)(2,1)} %get-tuple-element.338.hidden_ref.refs_0_, bf16[3,2048,2048]{2,1,0:T(8,128)(2,1)} %all-gather.2.cloned.1.call-done.weight_ref), custom_call_target="tpu_custom_call" | custom-call | flops 1 | bytes 1 | tf_op jit(solution)/shard_map/pallas_call | solution.py:205
  259.8 8.8 %shard_map.317 = bf16[512,2048]{1,0:T(8,128)(2,1)} custom-call(bf16[512,2048]{1,0:T(8,128)(2,1)} %get-tuple-element.279.inner_ref.refs_2_, bf16[3,2048,2048]{2,1,0:T(8,128)(2,1)} %all-gather.2.cloned.1.call-done.weight_ref), custom_call_target="tpu_custom_call" | custom-call | flops 1 | bytes 1 | tf_op jit(solution)/shard_map/pallas_call | solution.py:205
  277.6 12.0 %shard_map.319 = (bf16[512,2048]{1,0:T(8,128)(2,1)}, f32[512,2048]{1,0:T(8,128)}) custom-call(bf16[512,2048]{1,0:T(8,128)(2,1)} %pad_maximum_fusion.2.mixed_ref, bf16[2048,2048]{1,0:T(8,128)(2,1)} %bitcast.114, bf16[4,2,128,2048]{3,2,1,0:T(8,128)(2,1)} %bitcast.118, f32[1,2048]{1,0:T(1,128)S(1)} %bitcast.112), custom_call_target="tpu_custom_call" | custom-call | flops 1 | bytes 1 | tf_op jit(solution)/shard_map/pallas_call | solution.py:205
  289.6 14.3 %shard_map.320 = (bf16[512,2048]{1,0:T(8,128)(2,1)}, f32[512,2048]{1,0:T(8,128)}, f32[512,2048]{1,0:T(8,128)}) custom-call(bf16[512,2048]{1,0:T(8,128)(2,1)} %get-tuple-element.339.hidden_ref.refs_1_, bf16[3,2048,2048]{2,1,0:T(8,128)(2,1)} %all-gather.2.cloned.1.call-done.weight_ref), custom_call_target="tpu_custom_call" | custom-call | flops 1 | bytes 1 | tf_op jit(solution)/shard_map/pallas_call | solution.py:205
  303.9 8.9 %shard_map.321 = bf16[512,2048]{1,0:T(8,128)(2,1)} custom-call(bf16[512,2048]{1,0:T(8,128)(2,1)} %get-tuple-element.287.inner_ref.refs_3_, bf16[3,2048,2048]{2,1,0:T(8,128)(2,1)} %all-gather.2.cloned.1.call-done.weight_ref), custom_call_target="tpu_custom_call" | custom-call | flops 1 | bytes 1 | tf_op jit(solution)/shard_map/pallas_call | solution.py:205
  326.7 30.9 %collective-permute-done.50 = bf16[128,2048]{1,0:T(8,128)(2,1)S(1)} collective-permute-done((bf16[128,2048]{1,0:T(8,128)(2,1)S(1)}, bf16[128,2048]{1,0:T(8,128)(2,1)S(1)}, u32[]{:S(2)}, u32[]{:S(2)}) %collective-permute-start.50) | collective-permute-done | bytes 524320 | tf_op jit(solution)/shard_map/ppermute | solution.py:69
  360.4 15.5 %reduce-scatter.8.cloned.1.call-done.raw_mlp_ref = bf16[128,2048]{1,0:T(8,128)(2,1)} async-done(((bf16[512,2048]{1,0:T(8,128)(2,1)}), bf16[128,2048]{1,0:T(8,128)(2,1)}) %reduce-scatter.8.cloned.1.call-update) | async-done | bytes 524304 | tf_op jit(solution)/shard_map/reduce_scatter | solution.py:62
  393.1 8.9 %collective-permute-done.55 = bf16[128,2048]{1,0:T(8,128)(2,1)S(1)} collective-permute-done((bf16[128,2048]{1,0:T(8,128)(2,1)S(1)}, bf16[128,2048]{1,0:T(8,128)(2,1)S(1)}, u32[]{:S(2)}, u32[]{:S(2)}) %collective-permute-start.55) | collective-permute-done | bytes 524320 | tf_op jit(solution)/shard_map/ppermute | solution.py:69
  402.0 9.1 %collective-permute-done.53 = bf16[128,2048]{1,0:T(8,128)(2,1)S(1)} collective-permute-done((bf16[128,2048]{1,0:T(8,128)(2,1)}, bf16[128,2048]{1,0:T(8,128)(2,1)S(1)}, u32[]{:S(2)}, u32[]{:S(2)}) %collective-permute-start.53) | collective-permute-done | bytes 524320 | tf_op jit(solution)/shard_map/ppermute | solution.py:69
  417.1 11.7 %shard_map.323 = (bf16[512,2048]{1,0:T(8,128)(2,1)}, bf16[512,2048]{1,0:T(8,128)(2,1)}) custom-call(bf16[512,2048]{1,0:T(8,128)(2,1)} %pad_maximum_fusion.3.back_ref.refs_0_, bf16[3,2048,2048]{2,1,0:T(8,128)(2,1)} %all-gather.2.cloned.1.call-done.weight_ref, f32[512,2048]{1,0:T(8,128)} %get-tuple-element.298.gate_ref, f32[512,2048]{1,0:T(8,128)} %get-tuple-element.299.upper_ref), custom_call_target="tpu_custom_call" | custom-call | flops 1 | bytes 1 | tf_op jit(solution)/shard_map/pallas_call | solution.py:205
  433.5 13.9 %shard_map.324 = bf16[512,2048]{1,0:T(8,128)(2,1)} custom-call(bf16[512,2048]{1,0:T(8,128)(2,1)} %get-tuple-element.304.gate_ref.refs_2_, bf16[512,2048]{1,0:T(8,128)(2,1)} %get-tuple-element.305.upper_ref.refs_2_, bf16[3,2048,2048]{2,1,0:T(8,128)(2,1)} %all-gather.2.cloned.1.call-done.weight_ref), custom_call_target="tpu_custom_call" | custom-call | flops 1 | bytes 1 | tf_op jit(solution)/shard_map/pallas_call | solution.py:205
  452.4 11.9 %shard_map.325 = (bf16[512,2048]{1,0:T(8,128)(2,1)}, bf16[512,2048]{1,0:T(8,128)(2,1)}) custom-call(bf16[512,2048]{1,0:T(8,128)(2,1)} %pad_maximum_fusion.4.back_ref.refs_1_, bf16[3,2048,2048]{2,1,0:T(8,128)(2,1)} %all-gather.2.cloned.1.call-done.weight_ref, f32[512,2048]{1,0:T(8,128)} %get-tuple-element.309.gate_ref, f32[512,2048]{1,0:T(8,128)} %get-tuple-element.310.upper_ref), custom_call_target="tpu_custom_call" | custom-call | flops 1 | bytes 1 | tf_op jit(solution)/shard_map/pallas_call | solution.py:205
  464.3 13.9 %shard_map.326 = bf16[512,2048]{1,0:T(8,128)(2,1)} custom-call(bf16[512,2048]{1,0:T(8,128)(2,1)} %get-tuple-element.311.gate_ref.refs_3_, bf16[512,2048]{1,0:T(8,128)(2,1)} %get-tuple-element.312.upper_ref.refs_3_, bf16[3,2048,2048]{2,1,0:T(8,128)(2,1)} %all-gather.2.cloned.1.call-done.weight_ref), custom_call_target="tpu_custom_call" | custom-call | flops 1 | bytes 1 | tf_op jit(solution)/shard_map/pallas_call | solution.py:205
  478.2 9.3 %shard_map.327 = bf16[1024,2048]{1,0:T(8,128)(2,1)} custom-call(s32[4]{0:T(128)S(1)} %broadcast_xor_fusion.1.order_ref, bf16[512,2048]{1,0:T(8,128)(2,1)} %pad_maximum_fusion.3.back_ref.refs_0_, bf16[512,2048]{1,0:T(8,128)(2,1)} %pad_maximum_fusion.4.back_ref.refs_1_, bf16[512,2048]{1,0:T(8,128)(2,1)} %get-tuple-element.279.inner_ref.refs_2_, ...), custom_call_target="tpu_custom_call" | custom-call | flops 1 | bytes 1 | tf_op jit(solution)/shard_map/pallas_call | solution.py:205
  487.6 9.3 %shard_map.328 = bf16[1024,2048]{1,0:T(8,128)(2,1)} custom-call(s32[4]{0:T(128)S(1)} %broadcast_xor_fusion.1.order_ref, bf16[512,2048]{1,0:T(8,128)(2,1)} %get-tuple-element.338.hidden_ref.refs_0_, bf16[512,2048]{1,0:T(8,128)(2,1)} %get-tuple-element.339.hidden_ref.refs_1_, bf16[512,2048]{1,0:T(8,128)(2,1)} %get-tuple-element.304.gate_ref.refs_2_, ...), custom_call_target="tpu_custom_call" | custom-call | flops 1 | bytes 1 | tf_op jit(solution)/shard_map/pallas_call | solution.py:205
  505.2 10.8 %shard_map.330 = (bf16[2,256,1024]{2,1,0:T(8,128)(2,1)S(1)}, bf16[2,256,1024]{2,1,0:T(8,128)(2,1)}, bf16[2,256,1024]{2,1,0:T(8,128)(2,1)}, bf16[2,256,1024]{2,1,0:T(8,128)(2,1)}) custom-call(s32[4]{0:T(128)S(1)} %broadcast_xor_fusion.order_ref, bf16[512,2048]{1,0:T(8,128)(2,1)} %pad_maximum_fusion.3.back_ref.refs_0_, ...), custom_call_target="tpu_custom_call" | custom-call | flops 1 | bytes 1 | tf_op jit(solution)/shard_map/pallas_call | solution.py:205
  516.0 9.3 %shard_map.331 = bf16[1024,2048]{1,0:T(8,128)(2,1)} custom-call(s32[4]{0:T(128)S(1)} %broadcast_xor_fusion.1.order_ref, bf16[512,2048]{1,0:T(8,128)(2,1)} %get-tuple-element.338.hidden_ref.refs_0_, bf16[512,2048]{1,0:T(8,128)(2,1)} %get-tuple-element.339.hidden_ref.refs_1_, bf16[512,2048]{1,0:T(8,128)(2,1)} %get-tuple-element.305.upper_ref.refs_2_, ...), custom_call_target="tpu_custom_call" | custom-call | flops 1 | bytes 1 | tf_op jit(solution)/shard_map/pallas_call | solution.py:205
  528.7 10.7 %shard_map.332 = (bf16[2,256,1024]{2,1,0:T(8,128)(2,1)}, bf16[2,256,1024]{2,1,0:T(8,128)(2,1)}, bf16[2,256,1024]{2,1,0:T(8,128)(2,1)}, bf16[2,256,1024]{2,1,0:T(8,128)(2,1)}) custom-call(s32[4]{0:T(128)S(1)} %broadcast_xor_fusion.order_ref, bf16[512,2048]{1,0:T(8,128)(2,1)} %get-tuple-element.338.hidden_ref.refs_0_, ...), custom_call_target="tpu_custom_call" | custom-call | flops 1 | bytes 1 | tf_op jit(solution)/shard_map/pallas_call | solution.py:205
  565.5 10.4 %shard_map.334 = (bf16[2,256,1024]{2,1,0:T(8,128)(2,1)S(1)}, bf16[2,256,1024]{2,1,0:T(8,128)(2,1)}, bf16[2,256,1024]{2,1,0:T(8,128)(2,1)}, bf16[2,256,1024]{2,1,0:T(8,128)(2,1)}) custom-call(s32[4]{0:T(128)S(1)} %broadcast_xor_fusion.order_ref, bf16[512,2048]{1,0:T(8,128)(2,1)} %get-tuple-element.338.hidden_ref.refs_0_, ...), custom_call_target="tpu_custom_call" | custom-call | flops 1 | bytes 1 | tf_op jit(solution)/shard_map/pallas_call | solution.py:205
  583.0 19.9 %shard_map.336 = (f32[2,1024,512]{2,1,0:T(8,128)}, bf16[1024,512]{1,0:T(8,128)(2,1)}, f32[1024,128]{1,0:T(8,128)S(1)}, f32[2,512]{1,0:T(2,128)S(1)}) custom-call(bf16[3,1024,512]{2,1,0:T(8,128)(2,1)} %get-tuple-element.336.low_ref, bf16[1024,512]{1,0:T(8,128)(2,1)} %pad_maximum_fusion.8.back_ref, ...), custom_call_target="tpu_custom_call" | custom-call | flops 1 | bytes 1 | tf_op jit(solution)/shard_map/pallas_call | solution.py:205
  626.7 14.0 %shard_map.338 = (bf16[1024,1536]{1,0:T(8,128)(2,1)}, bf16[1024,2048]{1,0:T(8,128)(2,1)}) custom-call(f32[2,1024,512]{2,1,0:T(8,128)} %get-tuple-element.350.hats_ref, f32[1024,1536]{1,0:T(8,128)} %get-tuple-element.251.query_ref.key_ref.value_ref, f32[1024,1536]{1,0:T(8,128)} %get-tuple-element.251.query_ref.key_ref.value_ref, ...), custom_call_target="tpu_custom_call" | custom-call | flops 1 | bytes 1 | tf_op jit(solution)/shard_map/pallas_call | solution.py:205
  662.9 14.9 %collective-permute-done.86 = f32[2,4,256]{2,1,0:T(4,128)S(1)} collective-permute-done((f32[2,4,256]{2,1,0:T(4,128)S(1)}, f32[2,4,256]{2,1,0:T(4,128)S(1)}, u32[]{:S(2)}, u32[]{:S(2)}) %collective-permute-start.86) | collective-permute-done | bytes 8224 | tf_op jit(solution)/shard_map/ppermute | solution.py:146
  678.4 10.2 %collective-permute-done.82 = bf16[256,1024]{1,0:T(8,128)(2,1)S(1)} collective-permute-done((bf16[256,1024]{1,0:T(8,128)(2,1)S(1)}, bf16[256,1024]{1,0:T(8,128)(2,1)S(1)}, u32[]{:S(2)}, u32[]{:S(2)}) %collective-permute-start.82) | collective-permute-done | bytes 524320 | tf_op jit(solution)/shard_map/ppermute | solution.py:146
  691.3 8.5 %shard_map.340 = (bf16[2,256,768]{2,1,0:T(8,128)(2,1)S(1)}, bf16[2,256,768]{2,1,0:T(8,128)(2,1)S(1)}, bf16[2,256,768]{2,1,0:T(8,128)(2,1)}, bf16[2,256,768]{2,1,0:T(8,128)(2,1)}) custom-call(s32[4]{0:T(128)S(1)} %broadcast_xor_fusion.order_ref, bf16[1024,2048]{1,0:T(8,128)(2,1)} %pad_maximum_fusion.1.tokens_ref.refs_0_, ...), custom_call_target="tpu_custom_call" | custom-call | flops 1 | bytes 1 | tf_op jit(solution)/shard_map/pallas_call | solution.py:205
  719.8 12.5 %multiply_subtract_fusion = (f32[3,256,2048]{2,1,0:T(8,128)}, f32[3,256,2048]{2,1,0:T(8,128)}, f32[3,256,2048]{2,1,0:T(8,128)}) fusion(f32[3,256,2048]{2,1,0:T(8,128)S(1)} %bitcast.122, f32[1,256,2048]{2,1,0:T(8,128)S(1)} %maximum_bitcast_fusion.2, f32[1,256,2048]{2,1,0:T(8,128)S(1)} %maximum_bitcast_fusion.1, f32[1,256,2048]{2,1,0:T(8,128)} %maximum_bitcast_fusion, ...), kind=kLoop, calls=%fused_computation.5 | loop fusion | flops 25165824 | bytes 44040192 | tf_op jit(solution)/shard_map/sub | solution.py:48
  757.5 8.9 %collective-permute-done.95 = bf16[256,512]{1,0:T(8,128)(2,1)S(1)} collective-permute-done((bf16[256,512]{1,0:T(8,128)(2,1)S(1)}, bf16[256,512]{1,0:T(8,128)(2,1)S(1)}, u32[]{:S(2)}, u32[]{:S(2)}) %collective-permute-start.95) | collective-permute-done | bytes 262176 | tf_op jit(solution)/shard_map/ppermute | solution.py:113
  (456 shorter events, 361.3 us)
Async XLA Ops:
  7.2 232.1 %all-gather.2.cloned.1.call-start = ((), (), s32[]{:S(2)}) async-start(), calls=%async_computation.5 | async-start | bytes 28311552 | tf_op jit(solution)/shard_map/all_gather | solution.py:937
  7.2 41.1 %collective-permute-start.1 = (bf16[256,2048]{1,0:T(8,128)(2,1)}, bf16[256,2048]{1,0:T(8,128)(2,1)}, u32[]{:S(2)}, u32[]{:S(2)}) collective-permute-start(bf16[256,2048]{1,0:T(8,128)(2,1)} %tokens_ref.3), channel_id=1, source_target_pairs={{1,0},{2,1},{3,2},{5,4},{6,5},{7,6},{9,8},{10,9},{11,10},{13,12},{... | collective-permute-start | bytes 3145736 | tf_op jit(solution)/shard_map/ppermute | solution.py:69
  8.5 39.8 %collective-permute-start = (bf16[256,2048]{1,0:T(8,128)(2,1)}, bf16[256,2048]{1,0:T(8,128)(2,1)}, u32[]{:S(2)}, u32[]{:S(2)}) collective-permute-start(bf16[256,2048]{1,0:T(8,128)(2,1)} %tokens_ref.3), channel_id=1, source_target_pairs={{0,1},{1,2},{2,3},{4,5},{5,6},{6,7},{8,9},{9,10},{10,11},{12,13},{... | collective-permute-start | bytes 3145736 | tf_op jit(solution)/shard_map/ppermute | solution.py:69
  17.0 31.3 %collective-permute-start.3 = (bf16[256,1536]{1,0:T(8,128)(2,1)S(1)}, bf16[256,1536]{1,0:T(8,128)(2,1)S(1)}, u32[]{:S(2)}, u32[]{:S(2)}) collective-permute-start(bf16[256,1536]{1,0:T(8,128)(2,1)S(1)} %pad_maximum_fusion.9.refs_0_), channel_id=1, source_target_pairs={{0,16},{4,20},{8,24},{12,28},{16,0},{20,4},{24,8},{28,12},{1,17},{... | collective-permute-start | bytes 2359304 | tf_op jit(solution)/shard_map/ppermute | solution.py:146
  19.0 29.3 %collective-permute-start.2 = (bf16[256,1536]{1,0:T(8,128)(2,1)S(1)}, bf16[256,1536]{1,0:T(8,128)(2,1)S(1)}, u32[]{:S(2)}, u32[]{:S(2)}) collective-permute-start(bf16[256,1536]{1,0:T(8,128)(2,1)S(1)} %pad_maximum_fusion.9.refs_0_), channel_id=1, source_target_pairs={{0,8},{4,12},{8,0},{12,4},{16,24},{20,28},{24,16},{28,20},{1,9},{5... | collective-permute-start | bytes 2359304 | tf_op jit(solution)/shard_map/ppermute | solution.py:146
  48.4 267.8 %reduce-scatter.6.cloned.1.call-start = ((), (), s32[]{:S(2)}) async-start(), calls=%async_computation.6 | async-start | bytes 2621440 | tf_op jit(solution)/shard_map/reduce_scatter | solution.py:62
  55.1 27.3 %collective-permute-start.8 = (bf16[256,2048]{1,0:T(8,128)(2,1)}, bf16[256,2048]{1,0:T(8,128)(2,1)}, u32[]{:S(2)}, u32[]{:S(2)}) collective-permute-start(bf16[256,2048]{1,0:T(8,128)(2,1)} %collective-permute-done.1), channel_id=1, source_target_pairs={{1,0},{2,1},{5,4},{6,5},{9,8},{10,9},{13,12},{14,13},{17,16},{18,1... | collective-permute-start | bytes 3145736 | tf_op jit(solution)/shard_map/ppermute | solution.py:69
  162.3 32.7 %collective-permute-start.34 = (bf16[256,2048]{1,0:T(8,128)(2,1)S(1)}, bf16[256,2048]{1,0:T(8,128)(2,1)S(1)}, u32[]{:S(2)}, u32[]{:S(2)}) collective-permute-start(bf16[256,2048]{1,0:T(8,128)(2,1)S(1)} %pad_maximum_fusion.6.refs_0_), channel_id=1, source_target_pairs={{0,16},{4,20},{8,24},{12,28},{16,0},{20,4},{24,8},{28,12},{1,17},{... | collective-permute-start | bytes 3145736 | tf_op jit(solution)/shard_map/ppermute | solution.py:146
  163.1 33.4 %collective-permute-start.33 = (bf16[256,2048]{1,0:T(8,128)(2,1)S(1)}, bf16[256,2048]{1,0:T(8,128)(2,1)S(1)}, u32[]{:S(2)}, u32[]{:S(2)}) collective-permute-start(bf16[256,2048]{1,0:T(8,128)(2,1)S(1)} %pad_maximum_fusion.6.refs_0_), channel_id=1, source_target_pairs={{0,8},{4,12},{8,0},{12,4},{16,24},{20,28},{24,16},{28,20},{1,9},{5... | collective-permute-start | bytes 3145736 | tf_op jit(solution)/shard_map/ppermute | solution.py:146
  274.3 101.5 %reduce-scatter.8.cloned.1.call-start = ((), (), s32[]{:S(2)}) async-start(), calls=%async_computation.7 | async-start | bytes 2621440 | tf_op jit(solution)/shard_map/reduce_scatter | solution.py:62
  312.7 184.8 %reduce-scatter.10.cloned.1.call-start = ((), (), s32[]{:S(2)}) async-start(), calls=%async_computation.8 | async-start | bytes 2621440 | tf_op jit(solution)/shard_map/reduce_scatter | solution.py:62
  320.8 36.8 %collective-permute-start.50 = (bf16[128,2048]{1,0:T(8,128)(2,1)S(1)}, bf16[128,2048]{1,0:T(8,128)(2,1)S(1)}, u32[]{:S(2)}, u32[]{:S(2)}) collective-permute-start(bf16[128,2048]{1,0:T(8,128)(2,1)S(1)} %get-tuple-element.283), channel_id=1, source_target_pairs={{1,0},{2,1},{3,2},{5,4},{6,5},{7,6},{9,8},{10,9},{11,10},{13,12},{... | collective-permute-start | bytes 1572872 | tf_op jit(solution)/shard_map/ppermute | solution.py:69
  322.1 36.8 %collective-permute-start.48 = (bf16[128,2048]{1,0:T(8,128)(2,1)S(1)}, bf16[128,2048]{1,0:T(8,128)(2,1)S(1)}, u32[]{:S(2)}, u32[]{:S(2)}) collective-permute-start(bf16[128,2048]{1,0:T(8,128)(2,1)S(1)} %get-tuple-element.283), channel_id=1, source_target_pairs={{0,1},{1,2},{2,3},{4,5},{5,6},{6,7},{8,9},{9,10},{10,11},{12,13},{... | collective-permute-start | bytes 1572872 | tf_op jit(solution)/shard_map/ppermute | solution.py:69
  448.6 96.1 %reduce-scatter.12.cloned.1.call-start = ((), (), s32[]{:S(2)}) async-start(), calls=%async_computation.9 | async-start | bytes 2621440 | tf_op jit(solution)/shard_map/reduce_scatter | solution.py:62
  496.8 31.9 %collective-permute-start.61 = (bf16[1024,2048]{1,0:T(8,128)(2,1)}, bf16[1024,2048]{1,0:T(8,128)(2,1)}, u32[]{:S(2)}, u32[]{:S(2)}) collective-permute-start(bf16[1024,2048]{1,0:T(8,128)(2,1)} %shard_map.328), channel_id=1, source_target_pairs={{0,4},{4,0},{8,12},{12,8},{16,20},{20,16},{24,28},{28,24},{1,5},{5... | collective-permute-start | bytes 12582920 | tf_op jit(solution)/shard_map/ppermute | solution.py:146
  497.4 278.3 %reduce-scatter.14.cloned.1.call-start = ((), (), s32[]{:S(2)}) async-start(), calls=%async_computation.10 | async-start | bytes 5242880 | tf_op jit(solution)/shard_map/reduce_scatter | solution.py:62
  525.2 29.2 %collective-permute-start.67 = (bf16[1024,2048]{1,0:T(8,128)(2,1)}, bf16[1024,2048]{1,0:T(8,128)(2,1)}, u32[]{:S(2)}, u32[]{:S(2)}) collective-permute-start(bf16[1024,2048]{1,0:T(8,128)(2,1)} %shard_map.331), channel_id=1, source_target_pairs={{0,4},{4,0},{8,12},{12,8},{16,20},{20,16},{24,28},{28,24},{1,5},{5... | collective-permute-start | bytes 12582920 | tf_op jit(solution)/shard_map/ppermute | solution.py:146
  525.8 51.9 %collective-permute-start.65 = (bf16[2,256,1024]{2,1,0:T(8,128)(2,1)}, bf16[2,256,1024]{2,1,0:T(8,128)(2,1)}, u32[]{:S(2)}, u32[]{:S(2)}) collective-permute-start(bf16[2,256,1024]{2,1,0:T(8,128)(2,1)} %copy-done.10), channel_id=1, source_target_pairs={{0,8},{4,12},{8,0},{12,4},{16,24},{20,28},{24,16},{28,20},{1,9},{5... | collective-permute-start | bytes 3145736 | tf_op jit(solution)/shard_map/ppermute | solution.py:146
  527.2 50.4 %collective-permute-start.66 = (bf16[2,256,1024]{2,1,0:T(8,128)(2,1)}, bf16[2,256,1024]{2,1,0:T(8,128)(2,1)}, u32[]{:S(2)}, u32[]{:S(2)}) collective-permute-start(bf16[2,256,1024]{2,1,0:T(8,128)(2,1)} %get-tuple-element.323), channel_id=1, source_target_pairs={{0,16},{4,20},{8,24},{12,28},{16,0},{20,4},{24,8},{28,12},{1,17},{... | collective-permute-start | bytes 3145736 | tf_op jit(solution)/shard_map/ppermute | solution.py:146
  577.6 40.1 %collective-permute-start.73 = (bf16[1024,2048]{1,0:T(8,128)(2,1)}, bf16[1024,2048]{1,0:T(8,128)(2,1)}, u32[]{:S(2)}, u32[]{:S(2)}) collective-permute-start(bf16[1024,2048]{1,0:T(8,128)(2,1)} %shard_map.335), channel_id=1, source_target_pairs={{0,4},{4,0},{8,12},{12,8},{16,20},{20,16},{24,28},{28,24},{1,5},{5... | collective-permute-start | bytes 12582920 | tf_op jit(solution)/shard_map/ppermute | solution.py:146
  607.8 42.4 %collective-permute-start.76 = (bf16[2,256,1024]{2,1,0:T(8,128)(2,1)}, bf16[2,256,1024]{2,1,0:T(8,128)(2,1)}, u32[]{:S(2)}, u32[]{:S(2)}) collective-permute-start(bf16[2,256,1024]{2,1,0:T(8,128)(2,1)} %copy-done.9), channel_id=1, source_target_pairs={{0,8},{4,12},{8,0},{12,4},{16,24},{20,28},{24,16},{28,20},{1,9},{5... | collective-permute-start | bytes 3145736 | tf_op jit(solution)/shard_map/ppermute | solution.py:146
  608.3 41.9 %collective-permute-start.77 = (bf16[2,256,1024]{2,1,0:T(8,128)(2,1)}, bf16[2,256,1024]{2,1,0:T(8,128)(2,1)}, u32[]{:S(2)}, u32[]{:S(2)}) collective-permute-start(bf16[2,256,1024]{2,1,0:T(8,128)(2,1)} %get-tuple-element.373), channel_id=1, source_target_pairs={{0,16},{4,20},{8,24},{12,28},{16,0},{20,4},{24,8},{28,12},{1,17},{... | collective-permute-start | bytes 3145736 | tf_op jit(solution)/shard_map/ppermute | solution.py:146
  616.3 33.8 %collective-permute-start.75 = (bf16[256,1024]{1,0:T(8,128)(2,1)}, bf16[256,1024]{1,0:T(8,128)(2,1)}, u32[]{:S(2)}, u32[]{:S(2)}) collective-permute-start(bf16[256,1024]{1,0:T(8,128)(2,1)} %fusion.4), channel_id=1, source_target_pairs={{0,8},{4,12},{8,0},{12,4},{16,24},{20,28},{24,16},{28,20},{1,9},{5... | collective-permute-start | bytes 1572872 | tf_op jit(solution)/shard_map/ppermute | solution.py:146
  617.8 32.3 %collective-permute-start.74 = (bf16[256,1024]{1,0:T(8,128)(2,1)}, bf16[256,1024]{1,0:T(8,128)(2,1)S(1)}, u32[]{:S(2)}, u32[]{:S(2)}) collective-permute-start(bf16[256,1024]{1,0:T(8,128)(2,1)} %fusion.3), channel_id=1, source_target_pairs={{0,16},{4,20},{8,24},{12,28},{16,0},{20,4},{24,8},{28,12},{1,17},{... | collective-permute-start | bytes 1572872 | tf_op jit(solution)/shard_map/ppermute | solution.py:146
  650.2 39.0 %collective-permute-start.85 = (bf16[1024,1536]{1,0:T(8,128)(2,1)}, bf16[1024,1536]{1,0:T(8,128)(2,1)}, u32[]{:S(2)}, u32[]{:S(2)}) collective-permute-start(bf16[1024,1536]{1,0:T(8,128)(2,1)} %shard_map.339), channel_id=1, source_target_pairs={{0,4},{4,0},{8,12},{12,8},{16,20},{20,16},{24,28},{28,24},{1,5},{5... | collective-permute-start | bytes 9437192 | tf_op jit(solution)/shard_map/ppermute | solution.py:146
  651.4 51.3 %collective-permute-start.83 = (bf16[2,256,1024]{2,1,0:T(8,128)(2,1)}, bf16[2,256,1024]{2,1,0:T(8,128)(2,1)}, u32[]{:S(2)}, u32[]{:S(2)}) collective-permute-start(bf16[2,256,1024]{2,1,0:T(8,128)(2,1)} %get-tuple-element.389), channel_id=1, source_target_pairs={{0,8},{4,12},{8,0},{12,4},{16,24},{20,28},{24,16},{28,20},{1,9},{5... | collective-permute-start | bytes 3145736 | tf_op jit(solution)/shard_map/ppermute | solution.py:146
  652.1 50.7 %collective-permute-start.84 = (bf16[2,256,1024]{2,1,0:T(8,128)(2,1)}, bf16[2,256,1024]{2,1,0:T(8,128)(2,1)}, u32[]{:S(2)}, u32[]{:S(2)}) collective-permute-start(bf16[2,256,1024]{2,1,0:T(8,128)(2,1)} %get-tuple-element.390), channel_id=1, source_target_pairs={{0,16},{4,20},{8,24},{12,28},{16,0},{20,4},{24,8},{28,12},{1,17},{... | collective-permute-start | bytes 3145736 | tf_op jit(solution)/shard_map/ppermute | solution.py:146
  655.3 33.3 %collective-permute-start.82 = (bf16[256,1024]{1,0:T(8,128)(2,1)S(1)}, bf16[256,1024]{1,0:T(8,128)(2,1)S(1)}, u32[]{:S(2)}, u32[]{:S(2)}) collective-permute-start(bf16[256,1024]{1,0:T(8,128)(2,1)S(1)} %fusion.8), channel_id=1, source_target_pairs={{0,8},{4,12},{8,0},{12,4},{16,24},{20,28},{24,16},{28,20},{1,9},{5... | collective-permute-start | bytes 1572872 | tf_op jit(solution)/shard_map/ppermute | solution.py:146
  702.8 29.5 %collective-permute-start.91 = (f32[1,4,256]{2,1,0:T(4,128)S(1)}, f32[1,4,256]{2,1,0:T(4,128)S(1)}, u32[]{:S(2)}, u32[]{:S(2)}) collective-permute-start(f32[1,4,256]{2,1,0:T(4,128)S(1)} %slice.278), channel_id=1, source_target_pairs={{0,4},{4,0},{8,12},{12,8},{16,20},{20,16},{24,28},{28,24},{1,5},{5... | collective-permute-start | bytes 12296 | tf_op jit(solution)/shard_map/ppermute | solution.py:146
  705.0 27.3 %collective-permute-start.88 = (bf16[256,1024]{1,0:T(8,128)(2,1)}, bf16[256,1024]{1,0:T(8,128)(2,1)S(1)}, u32[]{:S(2)}, u32[]{:S(2)}) collective-permute-start(bf16[256,1024]{1,0:T(8,128)(2,1)} %fusion.10), channel_id=1, source_target_pairs={{0,8},{4,12},{8,0},{12,4},{16,24},{20,28},{24,16},{28,20},{1,9},{5... | collective-permute-start | bytes 1572872 | tf_op jit(solution)/shard_map/ppermute | solution.py:146
  709.2 27.2 %collective-permute-start.89 = (bf16[2,256,768]{2,1,0:T(8,128)(2,1)S(1)}, bf16[2,256,768]{2,1,0:T(8,128)(2,1)}, u32[]{:S(2)}, u32[]{:S(2)}) collective-permute-start(bf16[2,256,768]{2,1,0:T(8,128)(2,1)S(1)} %get-tuple-element.399), channel_id=1, source_target_pairs={{0,8},{4,12},{8,0},{12,4},{16,24},{20,28},{24,16},{28,20},{1,9},{5... | collective-permute-start | bytes 2359304 | tf_op jit(solution)/shard_map/ppermute | solution.py:146
  709.8 30.0 %collective-permute-start.90 = (bf16[2,256,768]{2,1,0:T(8,128)(2,1)S(1)}, bf16[2,256,768]{2,1,0:T(8,128)(2,1)}, u32[]{:S(2)}, u32[]{:S(2)}) collective-permute-start(bf16[2,256,768]{2,1,0:T(8,128)(2,1)S(1)} %get-tuple-element.400), channel_id=1, source_target_pairs={{0,16},{4,20},{8,24},{12,28},{16,0},{20,4},{24,8},{28,12},{1,17},{... | collective-permute-start | bytes 2359304 | tf_op jit(solution)/shard_map/ppermute | solution.py:146
  (136 other events, 1552.4 us)
Sparse Core Ops, SparseCore 0:
  48.5 140.2 all-gather.1
  274.5 41.6 reduce-scatter.5
  318.6 57.2 reduce-scatter.7
  448.8 47.4 reduce-scatter.9
  498.5 46.1 reduce-scatter.11
  651.5 74.5 reduce-scatter.13

commit v4 on v3

--- a/solution.py
+++ b/solution.py
@@ -179,8 +179,14 @@
 
 
 def gains_fold(blocks):
-    bit = blocks.shape[0] // 2
-    return blocks[:bit] + pair_swap(blocks[bit:], bit) if bit else blocks
+    if blocks.shape[0] % 2:
+        return blocks
+    return blocks[0::2] + pair_swap(blocks[1::2], 1)
+
+
+def gains_rest(blocks):
+    step = max(1, lax.axis_size("dp") // blocks.shape[0])
+    return [blocks[0]] + [pair_swap(blocks[d], step * d) for d in range(1, blocks.shape[0])]
 
 
 def gains_owned(block):
@@ -926,11 +932,12 @@
 
     qkv_shard = jnp.concatenate([w_attn[k].astype(jnp.bfloat16) for k in range(3)], axis=1)
     mlp_low = w_mlp.astype(jnp.bfloat16)
+    qkv_shard = after(qkv_shard, mlp_low)
     positions = doc_positions(lengths, seq_len).reshape(total_rows)
 
     gains_low = norm_gains.astype(jnp.bfloat16)
-    hop, near, gains, mlp_low = lax.optimization_barrier(
-        (line_hop(1, tokens, tokens), plane_one(qkv_shard), gains_over_tensor(gains_low), mlp_low)
+    hop, near, gains = lax.optimization_barrier(
+        (line_hop(1, tokens, tokens), plane_one(qkv_shard), gains_over_tensor(gains_low))
     )
     hops = [hop]
     mlp_shard = after(mlp_low, near)
@@ -1108,21 +1115,16 @@
     )
     gains = gains_blocks(gain_grad)
     qkv_left, gains = after(([whole_tokens], gains), tokens_part)
-    while gains.shape[0] > 8:
-        gains = gains_fold(gains)
-
-    down_two, upper_one, qkv_sent, gains = together(
+    qkv_sent = grad_sent(after(qkv_left, upper_one), [qkv_back])
+    down_two, qkv_kept, gains = together(
         down_two,
-        upper_one,
-        grad_sent(qkv_left, [qkv_back]),
-        gains_fold(gains),
-    )
-    gate_two, upper_two, out_one, qkv_kept, gains = together(
-        exchange_two(gate_kept, after(gate_one, qkv_sent)),
-        exchange_two(upper_kept, upper_one),
-        out_one,
         grad_kept(qkv_left, [qkv_back], pair_swap(qkv_sent, 1)),
         gains_fold(gains),
+    )
+    gate_two, upper_two, out_one = together(
+        exchange_two(gate_kept, after(gate_one, qkv_kept)),
+        exchange_two(upper_kept, after(upper_one, qkv_kept)),
+        out_one,
     )
     mlp_owned = jnp.stack(
         [
@@ -1135,12 +1137,12 @@
         exchange_two(out_kept, out_one),
         exchange_one(qkv_kept),
         adamw(w_mlp, mlp_owned, moment_mlp, square_mlp, RATE_MATRIX, DECAY_MATRIX),
-        gains_fold(gains),
+        gains_rest(gains),
     )
     qkv_two, out_owned, gain_final = together(
         exchange_two(qkv_kept, qkv_one),
         shift_scatter(exchange_end(out_kept, out_one, out_two), local_width),
-        gains_owned(gains[0]),
+        gains_owned(sum(gains[1:], gains[0])),
     )
     qkv_owned = exchange_end(qkv_kept, qkv_one, qkv_two)
     attn_owned = jnp.stack(

time: 800 us -> 794 us (level)
    ppermute x49 -> x50, starting transfers between devices: 36.9 us -> 40.7 us  [pair_swap(): return lax.ppermute(values, 'dp', [(i, i ^ bit) for i in range(count)])]
    ppermute x49 -> x50, waiting for transfers between devices: 59.9 us -> 61.4 us  [pair_swap(): return lax.ppermute(values, 'dp', [(i, i ^ bit) for i in range(count)])]
  transfers between devices with their start and end apart: 106 -> 107, of which waited for: 44 -> 44; matrix products, arithmetic and copies ran while one was open for 11% -> 11% of each run, Pallas kernels for 38% -> 38%
where the time goes in v4:
time: 794 us; the launch traced here: 779 us
  Pallas kernels  305 us (38%)
  waiting for transfers between devices  228 us (29%)
  starting transfers between devices  131 us (16%)
  other arithmetic  79.1 us (10%)
  local copies, waits for them, and re-layouts  20.2 us (3%)
  between operations  15.8 us (2%)
    pallas_call x30, Pallas kernels, kernel(): pl.pallas_call(body, grid_spec=spec, out_shape=out_shape, compiler_params...  305 us
    ppermute x15, waiting for transfers between devices, line_hop(): lax.ppermute(down, 'tensor', falling)  111 us
    ppermute x50, waiting for transfers between devices, pair_swap(): return lax.ppermute(values, 'dp', [(i, i ^ bit) for i in range(count)])  61.4 us
    ppermute x50, starting transfers between devices, pair_swap(): return lax.ppermute(values, 'dp', [(i, i ^ bit) for i in range(count)])  40.7 us
    ppermute x15, starting transfers between devices, line_hop(): lax.ppermute(up, 'tensor', rising)  36 us
    reduce_scatter x5, waiting for transfers between devices, chunk_scatter(): return lax.psum_scatter(part, 'tensor', scatter_dimension=0, tiled=True)  24.4 us
    ppermute x15, starting transfers between devices, line_hop(): lax.ppermute(down, 'tensor', falling)  19.7 us
    sub x3, other arithmetic, adamw(): weight * (1.0 - rate * decay) - rate * update  17 us
  transfers between devices with their start and end apart: 107, of which 44 were waited for; matrix products, arithmetic and copies ran while one was open for 11% of the time, Pallas kernels for 38%

profile of v4, /device:TPU:0, one launch (start us, length us, event | category | flops | bytes accessed | tf_op | source)
XLA Modules:
  0.0 779.3 jit_solution(14715428601403227013)
XLA Ops:
  28.0 8.8 %collective-permute-done.5 = bf16[4,64]{1,0:T(4,128)(2,1)S(1)} collective-permute-done((bf16[4,64]{1,0:T(4,128)(2,1)S(1)}, bf16[4,64]{1,0:T(4,128)(2,1)S(1)}, u32[]{:S(2)}, u32[]{:S(2)}) %collective-permute-start.5) | collective-permute-done | bytes 544 | tf_op jit(solution)/shard_map/ppermute | solution.py:152
  62.4 15.8 %collective-permute-done.8 = bf16[256,2048]{1,0:T(8,128)(2,1)} collective-permute-done((bf16[256,2048]{1,0:T(8,128)(2,1)}, bf16[256,2048]{1,0:T(8,128)(2,1)}, u32[]{:S(2)}, u32[]{:S(2)}) %collective-permute-start.8) | collective-permute-done | bytes 1048608 | tf_op jit(solution)/shard_map/ppermute | solution.py:69
  109.2 11.5 %shard_map.312 = (f32[1024,1536]{1,0:T(8,128)}, f32[1024,128]{1,0:T(8,128)S(1)}) custom-call(bf16[1024,2048]{1,0:T(8,128)(2,1)} %pad_maximum_fusion.1.tokens_ref.refs_0_, bf16[2048,1536]{1,0:T(8,128)(2,1)} %bitcast.127), custom_call_target="tpu_custom_call" | custom-call | flops 1 | bytes 1 | tf_op jit(solution)/shard_map/pallas_call | solution.py:211
  136.5 14.6 %shard_map.313 = (bf16[3,1024,512]{2,1,0:T(8,128)(2,1)}, bf16[1024,512]{1,0:T(8,128)(2,1)}) custom-call(f32[1024,1536]{1,0:T(8,128)} %get-tuple-element.253.query_ref.key_ref.value_ref, f32[1024,1536]{1,0:T(8,128)} %get-tuple-element.253.query_ref.key_ref.value_ref, f32[1024,1536]{1,0:T(8,128)} %get-tuple-element.253.query_ref.key_ref.value_ref, ...), custom_call_target="tpu_custom_call" | custom-call | flops 1 | bytes 1 | tf_op jit(solution)/shard_map/pallas_call | solution.py:211
  170.2 14.3 %collective-permute-done.31 = bf16[512,512]{1,0:T(8,128)(2,1)S(1)} collective-permute-done((bf16[512,512]{1,0:T(8,128)(2,1)S(1)}, bf16[512,512]{1,0:T(8,128)(2,1)S(1)}, u32[]{:S(2)}, u32[]{:S(2)}) %collective-permute-start.31) | collective-permute-done | bytes 524320 | tf_op jit(solution)/shard_map/ppermute | solution.py:69
  224.1 11.6 %shard_map.315 = (bf16[512,2048]{1,0:T(8,128)(2,1)}, f32[512,2048]{1,0:T(8,128)}) custom-call(bf16[512,2048]{1,0:T(8,128)(2,1)} %copy-done.12, bf16[2048,2048]{1,0:T(8,128)(2,1)} %bitcast.121, bf16[4,2,128,2048]{3,2,1,0:T(8,128)(2,1)} %bitcast.125, f32[1,2048]{1,0:T(1,128)S(1)} %bitcast.119), custom_call_target="tpu_custom_call" | custom-call | flops 1 | bytes 1 | tf_op jit(solution)/shard_map/pallas_call | solution.py:211
  237.7 14.3 %shard_map.316 = (bf16[512,2048]{1,0:T(8,128)(2,1)}, f32[512,2048]{1,0:T(8,128)}, f32[512,2048]{1,0:T(8,128)}) custom-call(bf16[512,2048]{1,0:T(8,128)(2,1)} %get-tuple-element.340.hidden_ref.refs_0_, bf16[3,2048,2048]{2,1,0:T(8,128)(2,1)} %all-gather.2.cloned.1.call-done.weight_ref), custom_call_target="tpu_custom_call" | custom-call | flops 1 | bytes 1 | tf_op jit(solution)/shard_map/pallas_call | solution.py:211
  256.4 8.9 %shard_map.317 = bf16[512,2048]{1,0:T(8,128)(2,1)} custom-call(bf16[512,2048]{1,0:T(8,128)(2,1)} %get-tuple-element.281.inner_ref.refs_2_, bf16[3,2048,2048]{2,1,0:T(8,128)(2,1)} %all-gather.2.cloned.1.call-done.weight_ref), custom_call_target="tpu_custom_call" | custom-call | flops 1 | bytes 1 | tf_op jit(solution)/shard_map/pallas_call | solution.py:211
  274.3 12.0 %shard_map.319 = (bf16[512,2048]{1,0:T(8,128)(2,1)}, f32[512,2048]{1,0:T(8,128)}) custom-call(bf16[512,2048]{1,0:T(8,128)(2,1)} %pad_maximum_fusion.2.mixed_ref, bf16[2048,2048]{1,0:T(8,128)(2,1)} %bitcast.122, bf16[4,2,128,2048]{3,2,1,0:T(8,128)(2,1)} %bitcast.126, f32[1,2048]{1,0:T(1,128)S(1)} %bitcast.120), custom_call_target="tpu_custom_call" | custom-call | flops 1 | bytes 1 | tf_op jit(solution)/shard_map/pallas_call | solution.py:211
  286.3 14.3 %shard_map.320 = (bf16[512,2048]{1,0:T(8,128)(2,1)}, f32[512,2048]{1,0:T(8,128)}, f32[512,2048]{1,0:T(8,128)}) custom-call(bf16[512,2048]{1,0:T(8,128)(2,1)} %get-tuple-element.341.hidden_ref.refs_1_, bf16[3,2048,2048]{2,1,0:T(8,128)(2,1)} %all-gather.2.cloned.1.call-done.weight_ref), custom_call_target="tpu_custom_call" | custom-call | flops 1 | bytes 1 | tf_op jit(solution)/shard_map/pallas_call | solution.py:211
  300.6 8.9 %shard_map.321 = bf16[512,2048]{1,0:T(8,128)(2,1)} custom-call(bf16[512,2048]{1,0:T(8,128)(2,1)} %get-tuple-element.289.inner_ref.refs_3_, bf16[3,2048,2048]{2,1,0:T(8,128)(2,1)} %all-gather.2.cloned.1.call-done.weight_ref), custom_call_target="tpu_custom_call" | custom-call | flops 1 | bytes 1 | tf_op jit(solution)/shard_map/pallas_call | solution.py:211
  323.7 30.8 %collective-permute-done.50 = bf16[128,2048]{1,0:T(8,128)(2,1)S(1)} collective-permute-done((bf16[128,2048]{1,0:T(8,128)(2,1)S(1)}, bf16[128,2048]{1,0:T(8,128)(2,1)S(1)}, u32[]{:S(2)}, u32[]{:S(2)}) %collective-permute-start.50) | collective-permute-done | bytes 524320 | tf_op jit(solution)/shard_map/ppermute | solution.py:69
  357.3 15.6 %reduce-scatter.8.cloned.1.call-done.raw_mlp_ref = bf16[128,2048]{1,0:T(8,128)(2,1)} async-done(((bf16[512,2048]{1,0:T(8,128)(2,1)}), bf16[128,2048]{1,0:T(8,128)(2,1)}) %reduce-scatter.8.cloned.1.call-update) | async-done | bytes 524304 | tf_op jit(solution)/shard_map/reduce_scatter | solution.py:62
  390.1 8.9 %collective-permute-done.55 = bf16[128,2048]{1,0:T(8,128)(2,1)S(1)} collective-permute-done((bf16[128,2048]{1,0:T(8,128)(2,1)S(1)}, bf16[128,2048]{1,0:T(8,128)(2,1)S(1)}, u32[]{:S(2)}, u32[]{:S(2)}) %collective-permute-start.55) | collective-permute-done | bytes 524320 | tf_op jit(solution)/shard_map/ppermute | solution.py:69
  399.0 9.2 %collective-permute-done.53 = bf16[128,2048]{1,0:T(8,128)(2,1)S(1)} collective-permute-done((bf16[128,2048]{1,0:T(8,128)(2,1)}, bf16[128,2048]{1,0:T(8,128)(2,1)S(1)}, u32[]{:S(2)}, u32[]{:S(2)}) %collective-permute-start.53) | collective-permute-done | bytes 524320 | tf_op jit(solution)/shard_map/ppermute | solution.py:69
  414.1 11.7 %shard_map.323 = (bf16[512,2048]{1,0:T(8,128)(2,1)}, bf16[512,2048]{1,0:T(8,128)(2,1)}) custom-call(bf16[512,2048]{1,0:T(8,128)(2,1)} %pad_maximum_fusion.3.back_ref.refs_0_, bf16[3,2048,2048]{2,1,0:T(8,128)(2,1)} %all-gather.2.cloned.1.call-done.weight_ref, f32[512,2048]{1,0:T(8,128)} %get-tuple-element.300.gate_ref, f32[512,2048]{1,0:T(8,128)} %get-tuple-element.301.upper_ref), custom_call_target="tpu_custom_call" | custom-call | flops 1 | bytes 1 | tf_op jit(solution)/shard_map/pallas_call | solution.py:211
  430.3 13.8 %shard_map.324 = bf16[512,2048]{1,0:T(8,128)(2,1)} custom-call(bf16[512,2048]{1,0:T(8,128)(2,1)} %get-tuple-element.306.gate_ref.refs_2_, bf16[512,2048]{1,0:T(8,128)(2,1)} %get-tuple-element.307.upper_ref.refs_2_, bf16[3,2048,2048]{2,1,0:T(8,128)(2,1)} %all-gather.2.cloned.1.call-done.weight_ref), custom_call_target="tpu_custom_call" | custom-call | flops 1 | bytes 1 | tf_op jit(solution)/shard_map/pallas_call | solution.py:211
  449.1 12.0 %shard_map.325 = (bf16[512,2048]{1,0:T(8,128)(2,1)}, bf16[512,2048]{1,0:T(8,128)(2,1)}) custom-call(bf16[512,2048]{1,0:T(8,128)(2,1)} %pad_maximum_fusion.4.back_ref.refs_1_, bf16[3,2048,2048]{2,1,0:T(8,128)(2,1)} %all-gather.2.cloned.1.call-done.weight_ref, f32[512,2048]{1,0:T(8,128)} %get-tuple-element.311.gate_ref, f32[512,2048]{1,0:T(8,128)} %get-tuple-element.312.upper_ref), custom_call_target="tpu_custom_call" | custom-call | flops 1 | bytes 1 | tf_op jit(solution)/shard_map/pallas_call | solution.py:211
  461.1 14.0 %shard_map.326 = bf16[512,2048]{1,0:T(8,128)(2,1)} custom-call(bf16[512,2048]{1,0:T(8,128)(2,1)} %get-tuple-element.313.gate_ref.refs_3_, bf16[512,2048]{1,0:T(8,128)(2,1)} %get-tuple-element.314.upper_ref.refs_3_, bf16[3,2048,2048]{2,1,0:T(8,128)(2,1)} %all-gather.2.cloned.1.call-done.weight_ref), custom_call_target="tpu_custom_call" | custom-call | flops 1 | bytes 1 | tf_op jit(solution)/shard_map/pallas_call | solution.py:211
  475.1 9.3 %shard_map.327 = bf16[1024,2048]{1,0:T(8,128)(2,1)} custom-call(s32[4]{0:T(128)S(1)} %broadcast_xor_fusion.1.order_ref, bf16[512,2048]{1,0:T(8,128)(2,1)} %pad_maximum_fusion.3.back_ref.refs_0_, bf16[512,2048]{1,0:T(8,128)(2,1)} %pad_maximum_fusion.4.back_ref.refs_1_, bf16[512,2048]{1,0:T(8,128)(2,1)} %get-tuple-element.281.inner_ref.refs_2_, ...), custom_call_target="tpu_custom_call" | custom-call | flops 1 | bytes 1 | tf_op jit(solution)/shard_map/pallas_call | solution.py:211
  484.4 9.3 %shard_map.328 = bf16[1024,2048]{1,0:T(8,128)(2,1)} custom-call(s32[4]{0:T(128)S(1)} %broadcast_xor_fusion.1.order_ref, bf16[512,2048]{1,0:T(8,128)(2,1)} %get-tuple-element.340.hidden_ref.refs_0_, bf16[512,2048]{1,0:T(8,128)(2,1)} %get-tuple-element.341.hidden_ref.refs_1_, bf16[512,2048]{1,0:T(8,128)(2,1)} %get-tuple-element.306.gate_ref.refs_2_, ...), custom_call_target="tpu_custom_call" | custom-call | flops 1 | bytes 1 | tf_op jit(solution)/shard_map/pallas_call | solution.py:211
  502.0 10.7 %shard_map.330 = (bf16[2,256,1024]{2,1,0:T(8,128)(2,1)S(1)}, bf16[2,256,1024]{2,1,0:T(8,128)(2,1)}, bf16[2,256,1024]{2,1,0:T(8,128)(2,1)}, bf16[2,256,1024]{2,1,0:T(8,128)(2,1)}) custom-call(s32[4]{0:T(128)S(1)} %broadcast_xor_fusion.order_ref, bf16[512,2048]{1,0:T(8,128)(2,1)} %pad_maximum_fusion.3.back_ref.refs_0_, ...), custom_call_target="tpu_custom_call" | custom-call | flops 1 | bytes 1 | tf_op jit(solution)/shard_map/pallas_call | solution.py:211
  512.8 9.3 %shard_map.331 = bf16[1024,2048]{1,0:T(8,128)(2,1)} custom-call(s32[4]{0:T(128)S(1)} %broadcast_xor_fusion.1.order_ref, bf16[512,2048]{1,0:T(8,128)(2,1)} %get-tuple-element.340.hidden_ref.refs_0_, bf16[512,2048]{1,0:T(8,128)(2,1)} %get-tuple-element.341.hidden_ref.refs_1_, bf16[512,2048]{1,0:T(8,128)(2,1)} %get-tuple-element.307.upper_ref.refs_2_, ...), custom_call_target="tpu_custom_call" | custom-call | flops 1 | bytes 1 | tf_op jit(solution)/shard_map/pallas_call | solution.py:211
  525.4 10.7 %shard_map.332 = (bf16[2,256,1024]{2,1,0:T(8,128)(2,1)}, bf16[2,256,1024]{2,1,0:T(8,128)(2,1)}, bf16[2,256,1024]{2,1,0:T(8,128)(2,1)}, bf16[2,256,1024]{2,1,0:T(8,128)(2,1)}) custom-call(s32[4]{0:T(128)S(1)} %broadcast_xor_fusion.order_ref, bf16[512,2048]{1,0:T(8,128)(2,1)} %get-tuple-element.340.hidden_ref.refs_0_, ...), custom_call_target="tpu_custom_call" | custom-call | flops 1 | bytes 1 | tf_op jit(solution)/shard_map/pallas_call | solution.py:211
  562.2 10.5 %shard_map.334 = (bf16[2,256,1024]{2,1,0:T(8,128)(2,1)}, bf16[2,256,1024]{2,1,0:T(8,128)(2,1)}, bf16[2,256,1024]{2,1,0:T(8,128)(2,1)}, bf16[2,256,1024]{2,1,0:T(8,128)(2,1)}) custom-call(s32[4]{0:T(128)S(1)} %broadcast_xor_fusion.order_ref, bf16[512,2048]{1,0:T(8,128)(2,1)} %get-tuple-element.340.hidden_ref.refs_0_, ...), custom_call_target="tpu_custom_call" | custom-call | flops 1 | bytes 1 | tf_op jit(solution)/shard_map/pallas_call | solution.py:211
  580.8 19.9 %shard_map.336 = (f32[2,1024,512]{2,1,0:T(8,128)}, bf16[1024,512]{1,0:T(8,128)(2,1)}, f32[1024,128]{1,0:T(8,128)S(1)}, f32[2,512]{1,0:T(2,128)S(1)}) custom-call(bf16[3,1024,512]{2,1,0:T(8,128)(2,1)} %get-tuple-element.338.low_ref, bf16[1024,512]{1,0:T(8,128)(2,1)} %pad_maximum_fusion.8.back_ref, ...), custom_call_target="tpu_custom_call" | custom-call | flops 1 | bytes 1 | tf_op jit(solution)/shard_map/pallas_call | solution.py:211
  616.0 14.0 %shard_map.338 = (bf16[1024,1536]{1,0:T(8,128)(2,1)}, bf16[1024,2048]{1,0:T(8,128)(2,1)}) custom-call(f32[2,1024,512]{2,1,0:T(8,128)} %get-tuple-element.352.hats_ref, f32[1024,1536]{1,0:T(8,128)} %get-tuple-element.253.query_ref.key_ref.value_ref, f32[1024,1536]{1,0:T(8,128)} %get-tuple-element.253.query_ref.key_ref.value_ref, ...), custom_call_target="tpu_custom_call" | custom-call | flops 1 | bytes 1 | tf_op jit(solution)/shard_map/pallas_call | solution.py:211
  647.4 8.8 %shard_map.340 = (bf16[2,256,768]{2,1,0:T(8,128)(2,1)S(1)}, bf16[2,256,768]{2,1,0:T(8,128)(2,1)S(1)}, bf16[2,256,768]{2,1,0:T(8,128)(2,1)}, bf16[2,256,768]{2,1,0:T(8,128)(2,1)}) custom-call(s32[4]{0:T(128)S(1)} %broadcast_xor_fusion.order_ref, bf16[1024,2048]{1,0:T(8,128)(2,1)} %pad_maximum_fusion.1.tokens_ref.refs_0_, ...), custom_call_target="tpu_custom_call" | custom-call | flops 1 | bytes 1 | tf_op jit(solution)/shard_map/pallas_call | solution.py:211
  667.9 11.6 %collective-permute-done.84 = bf16[2,256,1024]{2,1,0:T(8,128)(2,1)S(1)} collective-permute-done((bf16[2,256,1024]{2,1,0:T(8,128)(2,1)}, bf16[2,256,1024]{2,1,0:T(8,128)(2,1)S(1)}, u32[]{:S(2)}, u32[]{:S(2)}) %collective-permute-start.84) | collective-permute-done | bytes 1048608 | tf_op jit(solution)/shard_map/ppermute | solution.py:146
  693.8 8.3 %collective-permute-done.81 = bf16[256,1024]{1,0:T(8,128)(2,1)S(1)} collective-permute-done((bf16[256,1024]{1,0:T(8,128)(2,1)S(1)}, bf16[256,1024]{1,0:T(8,128)(2,1)S(1)}, u32[]{:S(2)}, u32[]{:S(2)}) %collective-permute-start.81) | collective-permute-done | bytes 524320 | tf_op jit(solution)/shard_map/ppermute | solution.py:146
  720.7 12.6 %multiply_subtract_fusion = (f32[3,256,2048]{2,1,0:T(8,128)}, f32[3,256,2048]{2,1,0:T(8,128)}, f32[3,256,2048]{2,1,0:T(8,128)}) fusion(f32[3,256,2048]{2,1,0:T(8,128)S(1)} %bitcast.130, f32[1,256,2048]{2,1,0:T(8,128)S(1)} %maximum_bitcast_fusion.2, f32[1,256,2048]{2,1,0:T(8,128)S(1)} %maximum_bitcast_fusion.1, f32[1,256,2048]{2,1,0:T(8,128)} %maximum_bitcast_fusion, ...), kind=kLoop, calls=%fused_computation.5 | loop fusion | flops 25165824 | bytes 44040192 | tf_op jit(solution)/shard_map/sub | solution.py:48
  751.9 8.5 %collective-permute-done.96 = bf16[256,512]{1,0:T(8,128)(2,1)S(1)} collective-permute-done((bf16[256,512]{1,0:T(8,128)(2,1)S(1)}, bf16[256,512]{1,0:T(8,128)(2,1)S(1)}, u32[]{:S(2)}, u32[]{:S(2)}) %collective-permute-start.96) | collective-permute-done | bytes 262176 | tf_op jit(solution)/shard_map/ppermute | solution.py:113
  (446 shorter events, 369.2 us)
Async XLA Ops:
  7.2 230.5 %all-gather.2.cloned.1.call-start = ((), (), s32[]{:S(2)}) async-start(), calls=%async_computation.5 | async-start | bytes 28311552 | tf_op jit(solution)/shard_map/all_gather | solution.py:944
  7.2 41.1 %collective-permute-start.1 = (bf16[256,2048]{1,0:T(8,128)(2,1)}, bf16[256,2048]{1,0:T(8,128)(2,1)}, u32[]{:S(2)}, u32[]{:S(2)}) collective-permute-start(bf16[256,2048]{1,0:T(8,128)(2,1)} %tokens_ref.3), channel_id=1, source_target_pairs={{1,0},{2,1},{3,2},{5,4},{6,5},{7,6},{9,8},{10,9},{11,10},{13,12},{... | collective-permute-start | bytes 3145736 | tf_op jit(solution)/shard_map/ppermute | solution.py:69
  8.5 39.8 %collective-permute-start = (bf16[256,2048]{1,0:T(8,128)(2,1)}, bf16[256,2048]{1,0:T(8,128)(2,1)}, u32[]{:S(2)}, u32[]{:S(2)}) collective-permute-start(bf16[256,2048]{1,0:T(8,128)(2,1)} %tokens_ref.3), channel_id=1, source_target_pairs={{0,1},{1,2},{2,3},{4,5},{5,6},{6,7},{8,9},{9,10},{10,11},{12,13},{... | collective-permute-start | bytes 3145736 | tf_op jit(solution)/shard_map/ppermute | solution.py:69
  21.9 26.4 %collective-permute-start.3 = (bf16[256,1536]{1,0:T(8,128)(2,1)S(1)}, bf16[256,1536]{1,0:T(8,128)(2,1)S(1)}, u32[]{:S(2)}, u32[]{:S(2)}) collective-permute-start(bf16[256,1536]{1,0:T(8,128)(2,1)S(1)} %pad_maximum_fusion.9.refs_0_), channel_id=1, source_target_pairs={{0,16},{4,20},{8,24},{12,28},{16,0},{20,4},{24,8},{28,12},{1,17},{... | collective-permute-start | bytes 2359304 | tf_op jit(solution)/shard_map/ppermute | solution.py:146
  23.9 24.4 %collective-permute-start.2 = (bf16[256,1536]{1,0:T(8,128)(2,1)S(1)}, bf16[256,1536]{1,0:T(8,128)(2,1)S(1)}, u32[]{:S(2)}, u32[]{:S(2)}) collective-permute-start(bf16[256,1536]{1,0:T(8,128)(2,1)S(1)} %pad_maximum_fusion.9.refs_0_), channel_id=1, source_target_pairs={{0,8},{4,12},{8,0},{12,4},{16,24},{20,28},{24,16},{28,20},{1,9},{5... | collective-permute-start | bytes 2359304 | tf_op jit(solution)/shard_map/ppermute | solution.py:146
  48.4 264.8 %reduce-scatter.6.cloned.1.call-start = ((), (), s32[]{:S(2)}) async-start(), calls=%async_computation.6 | async-start | bytes 2621440 | tf_op jit(solution)/shard_map/reduce_scatter | solution.py:62
  158.2 34.8 %collective-permute-start.34 = (bf16[256,2048]{1,0:T(8,128)(2,1)S(1)}, bf16[256,2048]{1,0:T(8,128)(2,1)S(1)}, u32[]{:S(2)}, u32[]{:S(2)}) collective-permute-start(bf16[256,2048]{1,0:T(8,128)(2,1)S(1)} %pad_maximum_fusion.6.refs_0_), channel_id=1, source_target_pairs={{0,16},{4,20},{8,24},{12,28},{16,0},{20,4},{24,8},{28,12},{1,17},{... | collective-permute-start | bytes 3145736 | tf_op jit(solution)/shard_map/ppermute | solution.py:146
  160.0 34.6 %collective-permute-start.33 = (bf16[256,2048]{1,0:T(8,128)(2,1)S(1)}, bf16[256,2048]{1,0:T(8,128)(2,1)S(1)}, u32[]{:S(2)}, u32[]{:S(2)}) collective-permute-start(bf16[256,2048]{1,0:T(8,128)(2,1)S(1)} %pad_maximum_fusion.6.refs_0_), channel_id=1, source_target_pairs={{0,8},{4,12},{8,0},{12,4},{16,24},{20,28},{24,16},{28,20},{1,9},{5... | collective-permute-start | bytes 3145736 | tf_op jit(solution)/shard_map/ppermute | solution.py:146
  271.0 101.9 %reduce-scatter.8.cloned.1.call-start = ((), (), s32[]{:S(2)}) async-start(), calls=%async_computation.7 | async-start | bytes 2621440 | tf_op jit(solution)/shard_map/reduce_scatter | solution.py:62
  309.4 184.9 %reduce-scatter.10.cloned.1.call-start = ((), (), s32[]{:S(2)}) async-start(), calls=%async_computation.8 | async-start | bytes 2621440 | tf_op jit(solution)/shard_map/reduce_scatter | solution.py:62
  317.8 36.7 %collective-permute-start.50 = (bf16[128,2048]{1,0:T(8,128)(2,1)S(1)}, bf16[128,2048]{1,0:T(8,128)(2,1)S(1)}, u32[]{:S(2)}, u32[]{:S(2)}) collective-permute-start(bf16[128,2048]{1,0:T(8,128)(2,1)S(1)} %get-tuple-element.285), channel_id=1, source_target_pairs={{1,0},{2,1},{3,2},{5,4},{6,5},{7,6},{9,8},{10,9},{11,10},{13,12},{... | collective-permute-start | bytes 1572872 | tf_op jit(solution)/shard_map/ppermute | solution.py:69
  319.1 36.7 %collective-permute-start.48 = (bf16[128,2048]{1,0:T(8,128)(2,1)S(1)}, bf16[128,2048]{1,0:T(8,128)(2,1)S(1)}, u32[]{:S(2)}, u32[]{:S(2)}) collective-permute-start(bf16[128,2048]{1,0:T(8,128)(2,1)S(1)} %get-tuple-element.285), channel_id=1, source_target_pairs={{0,1},{1,2},{2,3},{4,5},{5,6},{6,7},{8,9},{9,10},{10,11},{12,13},{... | collective-permute-start | bytes 1572872 | tf_op jit(solution)/shard_map/ppermute | solution.py:69
  445.5 95.9 %reduce-scatter.12.cloned.1.call-start = ((), (), s32[]{:S(2)}) async-start(), calls=%async_computation.9 | async-start | bytes 2621440 | tf_op jit(solution)/shard_map/reduce_scatter | solution.py:62
  493.7 31.7 %collective-permute-start.61 = (bf16[1024,2048]{1,0:T(8,128)(2,1)}, bf16[1024,2048]{1,0:T(8,128)(2,1)}, u32[]{:S(2)}, u32[]{:S(2)}) collective-permute-start(bf16[1024,2048]{1,0:T(8,128)(2,1)} %shard_map.328), channel_id=1, source_target_pairs={{0,4},{4,0},{8,12},{12,8},{16,20},{20,16},{24,28},{28,24},{1,5},{5... | collective-permute-start | bytes 12582920 | tf_op jit(solution)/shard_map/ppermute | solution.py:146
  494.2 275.5 %reduce-scatter.14.cloned.1.call-start = ((), (), s32[]{:S(2)}) async-start(), calls=%async_computation.10 | async-start | bytes 5242880 | tf_op jit(solution)/shard_map/reduce_scatter | solution.py:62
  522.1 29.1 %collective-permute-start.67 = (bf16[1024,2048]{1,0:T(8,128)(2,1)}, bf16[1024,2048]{1,0:T(8,128)(2,1)}, u32[]{:S(2)}, u32[]{:S(2)}) collective-permute-start(bf16[1024,2048]{1,0:T(8,128)(2,1)} %shard_map.331), channel_id=1, source_target_pairs={{0,4},{4,0},{8,12},{12,8},{16,20},{20,16},{24,28},{28,24},{1,5},{5... | collective-permute-start | bytes 12582920 | tf_op jit(solution)/shard_map/ppermute | solution.py:146
  522.6 51.7 %collective-permute-start.65 = (bf16[2,256,1024]{2,1,0:T(8,128)(2,1)}, bf16[2,256,1024]{2,1,0:T(8,128)(2,1)}, u32[]{:S(2)}, u32[]{:S(2)}) collective-permute-start(bf16[2,256,1024]{2,1,0:T(8,128)(2,1)} %copy-done.9), channel_id=1, source_target_pairs={{0,8},{4,12},{8,0},{12,4},{16,24},{20,28},{24,16},{28,20},{1,9},{5... | collective-permute-start | bytes 3145736 | tf_op jit(solution)/shard_map/ppermute | solution.py:146
  524.0 50.3 %collective-permute-start.66 = (bf16[2,256,1024]{2,1,0:T(8,128)(2,1)}, bf16[2,256,1024]{2,1,0:T(8,128)(2,1)}, u32[]{:S(2)}, u32[]{:S(2)}) collective-permute-start(bf16[2,256,1024]{2,1,0:T(8,128)(2,1)} %get-tuple-element.325), channel_id=1, source_target_pairs={{0,16},{4,20},{8,24},{12,28},{16,0},{20,4},{24,8},{28,12},{1,17},{... | collective-permute-start | bytes 3145736 | tf_op jit(solution)/shard_map/ppermute | solution.py:146
  574.3 30.9 %collective-permute-start.73 = (bf16[1024,2048]{1,0:T(8,128)(2,1)}, bf16[1024,2048]{1,0:T(8,128)(2,1)}, u32[]{:S(2)}, u32[]{:S(2)}) collective-permute-start(bf16[1024,2048]{1,0:T(8,128)(2,1)} %shard_map.335), channel_id=1, source_target_pairs={{0,4},{4,0},{8,12},{12,8},{16,20},{20,16},{24,28},{28,24},{1,5},{5... | collective-permute-start | bytes 12582920 | tf_op jit(solution)/shard_map/ppermute | solution.py:146
  574.4 26.4 %collective-permute-start.68 = (bf16[2,256,1024]{2,1,0:T(8,128)(2,1)}, bf16[2,256,1024]{2,1,0:T(8,128)(2,1)}, u32[]{:S(2)}, u32[]{:S(2)}) collective-permute-start(bf16[2,256,1024]{2,1,0:T(8,128)(2,1)} %get-tuple-element.355), channel_id=1, source_target_pairs={{0,8},{4,12},{8,0},{12,4},{16,24},{20,28},{24,16},{28,20},{1,9},{5... | collective-permute-start | bytes 3145736 | tf_op jit(solution)/shard_map/ppermute | solution.py:146
  575.9 26.3 %collective-permute-start.69 = (bf16[2,256,1024]{2,1,0:T(8,128)(2,1)}, bf16[2,256,1024]{2,1,0:T(8,128)(2,1)}, u32[]{:S(2)}, u32[]{:S(2)}) collective-permute-start(bf16[2,256,1024]{2,1,0:T(8,128)(2,1)} %get-tuple-element.356), channel_id=1, source_target_pairs={{0,16},{4,20},{8,24},{12,28},{16,0},{20,4},{24,8},{28,12},{1,17},{... | collective-permute-start | bytes 3145736 | tf_op jit(solution)/shard_map/ppermute | solution.py:146
  577.4 52.6 %collective-permute-start.76 = (bf16[2,256,1024]{2,1,0:T(8,128)(2,1)}, bf16[2,256,1024]{2,1,0:T(8,128)(2,1)}, u32[]{:S(2)}, u32[]{:S(2)}) collective-permute-start(bf16[2,256,1024]{2,1,0:T(8,128)(2,1)} %get-tuple-element.381), channel_id=1, source_target_pairs={{0,8},{4,12},{8,0},{12,4},{16,24},{20,28},{24,16},{28,20},{1,9},{5... | collective-permute-start | bytes 3145736 | tf_op jit(solution)/shard_map/ppermute | solution.py:146
  577.9 52.0 %collective-permute-start.77 = (bf16[2,256,1024]{2,1,0:T(8,128)(2,1)}, bf16[2,256,1024]{2,1,0:T(8,128)(2,1)}, u32[]{:S(2)}, u32[]{:S(2)}) collective-permute-start(bf16[2,256,1024]{2,1,0:T(8,128)(2,1)} %get-tuple-element.382), channel_id=1, source_target_pairs={{0,16},{4,20},{8,24},{12,28},{16,0},{20,4},{24,8},{28,12},{1,17},{... | collective-permute-start | bytes 3145736 | tf_op jit(solution)/shard_map/ppermute | solution.py:146
  645.3 34.3 %collective-permute-start.84 = (bf16[2,256,1024]{2,1,0:T(8,128)(2,1)}, bf16[2,256,1024]{2,1,0:T(8,128)(2,1)S(1)}, u32[]{:S(2)}, u32[]{:S(2)}) collective-permute-start(bf16[2,256,1024]{2,1,0:T(8,128)(2,1)} %get-tuple-element.399), channel_id=1, source_target_pairs={{0,8},{4,12},{8,0},{12,4},{16,24},{20,28},{24,16},{28,20},{1,9},{5... | collective-permute-start | bytes 3145736 | tf_op jit(solution)/shard_map/ppermute | solution.py:146
  646.8 35.8 %collective-permute-start.85 = (bf16[2,256,1024]{2,1,0:T(8,128)(2,1)}, bf16[2,256,1024]{2,1,0:T(8,128)(2,1)S(1)}, u32[]{:S(2)}, u32[]{:S(2)}) collective-permute-start(bf16[2,256,1024]{2,1,0:T(8,128)(2,1)} %get-tuple-element.400), channel_id=1, source_target_pairs={{0,16},{4,20},{8,24},{12,28},{16,0},{20,4},{24,8},{28,12},{1,17},{... | collective-permute-start | bytes 3145736 | tf_op jit(solution)/shard_map/ppermute | solution.py:146
  659.0 31.8 %collective-permute-start.83 = (bf16[256,1024]{1,0:T(8,128)(2,1)S(1)}, bf16[256,1024]{1,0:T(8,128)(2,1)S(1)}, u32[]{:S(2)}, u32[]{:S(2)}) collective-permute-start(bf16[256,1024]{1,0:T(8,128)(2,1)S(1)} %fusion.8), channel_id=1, source_target_pairs={{0,8},{4,12},{8,0},{12,4},{16,24},{20,28},{24,16},{28,20},{1,9},{5... | collective-permute-start | bytes 1572872 | tf_op jit(solution)/shard_map/ppermute | solution.py:146
  661.8 30.4 %collective-permute-start.82 = (bf16[256,1024]{1,0:T(8,128)(2,1)S(1)}, bf16[256,1024]{1,0:T(8,128)(2,1)S(1)}, u32[]{:S(2)}, u32[]{:S(2)}) collective-permute-start(bf16[256,1024]{1,0:T(8,128)(2,1)S(1)} %fusion.7), channel_id=1, source_target_pairs={{0,16},{4,20},{8,24},{12,28},{16,0},{20,4},{24,8},{28,12},{1,17},{... | collective-permute-start | bytes 1572872 | tf_op jit(solution)/shard_map/ppermute | solution.py:146
  664.6 37.4 %collective-permute-start.81 = (bf16[256,1024]{1,0:T(8,128)(2,1)S(1)}, bf16[256,1024]{1,0:T(8,128)(2,1)S(1)}, u32[]{:S(2)}, u32[]{:S(2)}) collective-permute-start(bf16[256,1024]{1,0:T(8,128)(2,1)S(1)} %fusion.6), channel_id=1, source_target_pairs={{0,8},{4,12},{8,0},{12,4},{16,24},{20,28},{24,16},{28,20},{1,9},{5... | collective-permute-start | bytes 1572872 | tf_op jit(solution)/shard_map/ppermute | solution.py:146
  682.7 50.6 %collective-permute-start.88 = (bf16[2,256,768]{2,1,0:T(8,128)(2,1)S(1)}, bf16[2,256,768]{2,1,0:T(8,128)(2,1)}, u32[]{:S(2)}, u32[]{:S(2)}) collective-permute-start(bf16[2,256,768]{2,1,0:T(8,128)(2,1)S(1)} %get-tuple-element.389), channel_id=1, source_target_pairs={{0,8},{4,12},{8,0},{12,4},{16,24},{20,28},{24,16},{28,20},{1,9},{5... | collective-permute-start | bytes 2359304 | tf_op jit(solution)/shard_map/ppermute | solution.py:146
  690.8 42.5 %collective-permute-start.89 = (bf16[2,256,768]{2,1,0:T(8,128)(2,1)S(1)}, bf16[2,256,768]{2,1,0:T(8,128)(2,1)}, u32[]{:S(2)}, u32[]{:S(2)}) collective-permute-start(bf16[2,256,768]{2,1,0:T(8,128)(2,1)S(1)} %get-tuple-element.390), channel_id=1, source_target_pairs={{0,16},{4,20},{8,24},{12,28},{16,0},{20,4},{24,8},{28,12},{1,17},{... | collective-permute-start | bytes 2359304 | tf_op jit(solution)/shard_map/ppermute | solution.py:146
  692.3 27.2 %collective-permute-start.92 = (f32[4,256]{1,0:T(4,128)S(1)}, f32[4,256]{1,0:T(4,128)S(1)}, u32[]{:S(2)}, u32[]{:S(2)}) collective-permute-start(f32[4,256]{1,0:T(4,128)S(1)} %get-tuple-element.480), channel_id=1, source_target_pairs={{0,24},{4,28},{8,16},{12,20},{16,8},{20,12},{24,0},{28,4},{1,25},{... | collective-permute-start | bytes 12296 | tf_op jit(solution)/shard_map/ppermute | solution.py:146
  703.5 29.8 %collective-permute-start.90 = (f32[4,256]{1,0:T(4,128)S(1)}, f32[4,256]{1,0:T(4,128)S(1)}, u32[]{:S(2)}, u32[]{:S(2)}) collective-permute-start(f32[4,256]{1,0:T(4,128)S(1)} %get-tuple-element.482), channel_id=1, source_target_pairs={{0,8},{4,12},{8,0},{12,4},{16,24},{20,28},{24,16},{28,20},{1,9},{5... | collective-permute-start | bytes 12296 | tf_op jit(solution)/shard_map/ppermute | solution.py:146
  (132 other events, 1567.9 us)
Sparse Core Ops, SparseCore 0:
  48.5 141.2 all-gather.1
  271.1 41.9 reduce-scatter.5
  315.5 57.2 reduce-scatter.7
  445.6 47.5 reduce-scatter.9
  495.5 45.8 reduce-scatter.11
  645.4 75.4 reduce-scatter.13

commit v5 on v4

--- a/solution.py
+++ b/solution.py
@@ -1155,7 +1155,7 @@
     new_gains, new_moment_gains, new_square_gains = adamw(
         norm_gains, gain_final, moment_gains, square_gains, RATE_GAIN, 0.0
     )
-    tokens_back = after(tokens_back, new_mlp, new_attn, new_gains)
+    tokens_back = after(tokens_back, new_mlp)
     grad_tokens = (jnp.concatenate(back_hidden, axis=0) + tokens_back.astype(jnp.float32)).astype(jnp.bfloat16)
     return (
         out_tokens,

time: 794 us -> 794 us (level)
  no operation moved by 1% of the time
where the time goes in v5:
time: 794 us; the launch traced here: 779 us
  Pallas kernels  305 us (38%)
  waiting for transfers between devices  228 us (29%)
  starting transfers between devices  131 us (16%)
  other arithmetic  79.1 us (10%)
  local copies, waits for them, and re-layouts  20.2 us (3%)
  between operations  15.8 us (2%)
    pallas_call x30, Pallas kernels, kernel(): pl.pallas_call(body, grid_spec=spec, out_shape=out_shape, compiler_params...  305 us
    ppermute x15, waiting for transfers between devices, line_hop(): lax.ppermute(down, 'tensor', falling)  111 us
    ppermute x50, waiting for transfers between devices, pair_swap(): return lax.ppermute(values, 'dp', [(i, i ^ bit) for i in range(count)])  61.4 us
    ppermute x50, starting transfers between devices, pair_swap(): return lax.ppermute(values, 'dp', [(i, i ^ bit) for i in range(count)])  40.7 us
    ppermute x15, starting transfers between devices, line_hop(): lax.ppermute(up, 'tensor', rising)  36 us
    reduce_scatter x5, waiting for transfers between devices, chunk_scatter(): return lax.psum_scatter(part, 'tensor', scatter_dimension=0, tiled=True)  24.4 us
    ppermute x15, starting transfers between devices, line_hop(): lax.ppermute(down, 'tensor', falling)  19.7 us
    sub x3, other arithmetic, adamw(): weight * (1.0 - rate * decay) - rate * update  17 us
  transfers between devices with their start and end apart: 107, of which 44 were waited for; matrix products, arithmetic and copies ran while one was open for 11% of the time, Pallas kernels for 38%

profile of v5, /device:TPU:0, one launch (start us, length us, event | category | flops | bytes accessed | tf_op | source)
XLA Modules:
  0.0 779.3 jit_solution(14715428601403227013)
XLA Ops:
  28.0 8.8 %collective-permute-done.5 = bf16[4,64]{1,0:T(4,128)(2,1)S(1)} collective-permute-done((bf16[4,64]{1,0:T(4,128)(2,1)S(1)}, bf16[4,64]{1,0:T(4,128)(2,1)S(1)}, u32[]{:S(2)}, u32[]{:S(2)}) %collective-permute-start.5) | collective-permute-done | bytes 544 | tf_op jit(solution)/shard_map/ppermute | solution.py:152
  62.4 15.8 %collective-permute-done.8 = bf16[256,2048]{1,0:T(8,128)(2,1)} collective-permute-done((bf16[256,2048]{1,0:T(8,128)(2,1)}, bf16[256,2048]{1,0:T(8,128)(2,1)}, u32[]{:S(2)}, u32[]{:S(2)}) %collective-permute-start.8) | collective-permute-done | bytes 1048608 | tf_op jit(solution)/shard_map/ppermute | solution.py:69
  109.2 11.5 %shard_map.312 = (f32[1024,1536]{1,0:T(8,128)}, f32[1024,128]{1,0:T(8,128)S(1)}) custom-call(bf16[1024,2048]{1,0:T(8,128)(2,1)} %pad_maximum_fusion.1.tokens_ref.refs_0_, bf16[2048,1536]{1,0:T(8,128)(2,1)} %bitcast.127), custom_call_target="tpu_custom_call" | custom-call | flops 1 | bytes 1 | tf_op jit(solution)/shard_map/pallas_call | solution.py:211
  136.5 14.6 %shard_map.313 = (bf16[3,1024,512]{2,1,0:T(8,128)(2,1)}, bf16[1024,512]{1,0:T(8,128)(2,1)}) custom-call(f32[1024,1536]{1,0:T(8,128)} %get-tuple-element.253.query_ref.key_ref.value_ref, f32[1024,1536]{1,0:T(8,128)} %get-tuple-element.253.query_ref.key_ref.value_ref, f32[1024,1536]{1,0:T(8,128)} %get-tuple-element.253.query_ref.key_ref.value_ref, ...), custom_call_target="tpu_custom_call" | custom-call | flops 1 | bytes 1 | tf_op jit(solution)/shard_map/pallas_call | solution.py:211
  170.2 14.3 %collective-permute-done.31 = bf16[512,512]{1,0:T(8,128)(2,1)S(1)} collective-permute-done((bf16[512,512]{1,0:T(8,128)(2,1)S(1)}, bf16[512,512]{1,0:T(8,128)(2,1)S(1)}, u32[]{:S(2)}, u32[]{:S(2)}) %collective-permute-start.31) | collective-permute-done | bytes 524320 | tf_op jit(solution)/shard_map/ppermute | solution.py:69
  224.1 11.6 %shard_map.315 = (bf16[512,2048]{1,0:T(8,128)(2,1)}, f32[512,2048]{1,0:T(8,128)}) custom-call(bf16[512,2048]{1,0:T(8,128)(2,1)} %copy-done.12, bf16[2048,2048]{1,0:T(8,128)(2,1)} %bitcast.121, bf16[4,2,128,2048]{3,2,1,0:T(8,128)(2,1)} %bitcast.125, f32[1,2048]{1,0:T(1,128)S(1)} %bitcast.119), custom_call_target="tpu_custom_call" | custom-call | flops 1 | bytes 1 | tf_op jit(solution)/shard_map/pallas_call | solution.py:211
  237.7 14.3 %shard_map.316 = (bf16[512,2048]{1,0:T(8,128)(2,1)}, f32[512,2048]{1,0:T(8,128)}, f32[512,2048]{1,0:T(8,128)}) custom-call(bf16[512,2048]{1,0:T(8,128)(2,1)} %get-tuple-element.340.hidden_ref.refs_0_, bf16[3,2048,2048]{2,1,0:T(8,128)(2,1)} %all-gather.2.cloned.1.call-done.weight_ref), custom_call_target="tpu_custom_call" | custom-call | flops 1 | bytes 1 | tf_op jit(solution)/shard_map/pallas_call | solution.py:211
  256.4 8.9 %shard_map.317 = bf16[512,2048]{1,0:T(8,128)(2,1)} custom-call(bf16[512,2048]{1,0:T(8,128)(2,1)} %get-tuple-element.281.inner_ref.refs_2_, bf16[3,2048,2048]{2,1,0:T(8,128)(2,1)} %all-gather.2.cloned.1.call-done.weight_ref), custom_call_target="tpu_custom_call" | custom-call | flops 1 | bytes 1 | tf_op jit(solution)/shard_map/pallas_call | solution.py:211
  274.3 12.0 %shard_map.319 = (bf16[512,2048]{1,0:T(8,128)(2,1)}, f32[512,2048]{1,0:T(8,128)}) custom-call(bf16[512,2048]{1,0:T(8,128)(2,1)} %pad_maximum_fusion.2.mixed_ref, bf16[2048,2048]{1,0:T(8,128)(2,1)} %bitcast.122, bf16[4,2,128,2048]{3,2,1,0:T(8,128)(2,1)} %bitcast.126, f32[1,2048]{1,0:T(1,128)S(1)} %bitcast.120), custom_call_target="tpu_custom_call" | custom-call | flops 1 | bytes 1 | tf_op jit(solution)/shard_map/pallas_call | solution.py:211
  286.3 14.3 %shard_map.320 = (bf16[512,2048]{1,0:T(8,128)(2,1)}, f32[512,2048]{1,0:T(8,128)}, f32[512,2048]{1,0:T(8,128)}) custom-call(bf16[512,2048]{1,0:T(8,128)(2,1)} %get-tuple-element.341.hidden_ref.refs_1_, bf16[3,2048,2048]{2,1,0:T(8,128)(2,1)} %all-gather.2.cloned.1.call-done.weight_ref), custom_call_target="tpu_custom_call" | custom-call | flops 1 | bytes 1 | tf_op jit(solution)/shard_map/pallas_call | solution.py:211
  300.6 8.9 %shard_map.321 = bf16[512,2048]{1,0:T(8,128)(2,1)} custom-call(bf16[512,2048]{1,0:T(8,128)(2,1)} %get-tuple-element.289.inner_ref.refs_3_, bf16[3,2048,2048]{2,1,0:T(8,128)(2,1)} %all-gather.2.cloned.1.call-done.weight_ref), custom_call_target="tpu_custom_call" | custom-call | flops 1 | bytes 1 | tf_op jit(solution)/shard_map/pallas_call | solution.py:211
  323.7 30.8 %collective-permute-done.50 = bf16[128,2048]{1,0:T(8,128)(2,1)S(1)} collective-permute-done((bf16[128,2048]{1,0:T(8,128)(2,1)S(1)}, bf16[128,2048]{1,0:T(8,128)(2,1)S(1)}, u32[]{:S(2)}, u32[]{:S(2)}) %collective-permute-start.50) | collective-permute-done | bytes 524320 | tf_op jit(solution)/shard_map/ppermute | solution.py:69
  357.3 15.6 %reduce-scatter.8.cloned.1.call-done.raw_mlp_ref = bf16[128,2048]{1,0:T(8,128)(2,1)} async-done(((bf16[512,2048]{1,0:T(8,128)(2,1)}), bf16[128,2048]{1,0:T(8,128)(2,1)}) %reduce-scatter.8.cloned.1.call-update) | async-done | bytes 524304 | tf_op jit(solution)/shard_map/reduce_scatter | solution.py:62
  390.1 8.9 %collective-permute-done.55 = bf16[128,2048]{1,0:T(8,128)(2,1)S(1)} collective-permute-done((bf16[128,2048]{1,0:T(8,128)(2,1)S(1)}, bf16[128,2048]{1,0:T(8,128)(2,1)S(1)}, u32[]{:S(2)}, u32[]{:S(2)}) %collective-permute-start.55) | collective-permute-done | bytes 524320 | tf_op jit(solution)/shard_map/ppermute | solution.py:69
  399.0 9.2 %collective-permute-done.53 = bf16[128,2048]{1,0:T(8,128)(2,1)S(1)} collective-permute-done((bf16[128,2048]{1,0:T(8,128)(2,1)}, bf16[128,2048]{1,0:T(8,128)(2,1)S(1)}, u32[]{:S(2)}, u32[]{:S(2)}) %collective-permute-start.53) | collective-permute-done | bytes 524320 | tf_op jit(solution)/shard_map/ppermute | solution.py:69
  414.1 11.7 %shard_map.323 = (bf16[512,2048]{1,0:T(8,128)(2,1)}, bf16[512,2048]{1,0:T(8,128)(2,1)}) custom-call(bf16[512,2048]{1,0:T(8,128)(2,1)} %pad_maximum_fusion.3.back_ref.refs_0_, bf16[3,2048,2048]{2,1,0:T(8,128)(2,1)} %all-gather.2.cloned.1.call-done.weight_ref, f32[512,2048]{1,0:T(8,128)} %get-tuple-element.300.gate_ref, f32[512,2048]{1,0:T(8,128)} %get-tuple-element.301.upper_ref), custom_call_target="tpu_custom_call" | custom-call | flops 1 | bytes 1 | tf_op jit(solution)/shard_map/pallas_call | solution.py:211
  430.3 13.8 %shard_map.324 = bf16[512,2048]{1,0:T(8,128)(2,1)} custom-call(bf16[512,2048]{1,0:T(8,128)(2,1)} %get-tuple-element.306.gate_ref.refs_2_, bf16[512,2048]{1,0:T(8,128)(2,1)} %get-tuple-element.307.upper_ref.refs_2_, bf16[3,2048,2048]{2,1,0:T(8,128)(2,1)} %all-gather.2.cloned.1.call-done.weight_ref), custom_call_target="tpu_custom_call" | custom-call | flops 1 | bytes 1 | tf_op jit(solution)/shard_map/pallas_call | solution.py:211
  449.1 12.0 %shard_map.325 = (bf16[512,2048]{1,0:T(8,128)(2,1)}, bf16[512,2048]{1,0:T(8,128)(2,1)}) custom-call(bf16[512,2048]{1,0:T(8,128)(2,1)} %pad_maximum_fusion.4.back_ref.refs_1_, bf16[3,2048,2048]{2,1,0:T(8,128)(2,1)} %all-gather.2.cloned.1.call-done.weight_ref, f32[512,2048]{1,0:T(8,128)} %get-tuple-element.311.gate_ref, f32[512,2048]{1,0:T(8,128)} %get-tuple-element.312.upper_ref), custom_call_target="tpu_custom_call" | custom-call | flops 1 | bytes 1 | tf_op jit(solution)/shard_map/pallas_call | solution.py:211
  461.1 14.0 %shard_map.326 = bf16[512,2048]{1,0:T(8,128)(2,1)} custom-call(bf16[512,2048]{1,0:T(8,128)(2,1)} %get-tuple-element.313.gate_ref.refs_3_, bf16[512,2048]{1,0:T(8,128)(2,1)} %get-tuple-element.314.upper_ref.refs_3_, bf16[3,2048,2048]{2,1,0:T(8,128)(2,1)} %all-gather.2.cloned.1.call-done.weight_ref), custom_call_target="tpu_custom_call" | custom-call | flops 1 | bytes 1 | tf_op jit(solution)/shard_map/pallas_call | solution.py:211
  475.1 9.3 %shard_map.327 = bf16[1024,2048]{1,0:T(8,128)(2,1)} custom-call(s32[4]{0:T(128)S(1)} %broadcast_xor_fusion.1.order_ref, bf16[512,2048]{1,0:T(8,128)(2,1)} %pad_maximum_fusion.3.back_ref.refs_0_, bf16[512,2048]{1,0:T(8,128)(2,1)} %pad_maximum_fusion.4.back_ref.refs_1_, bf16[512,2048]{1,0:T(8,128)(2,1)} %get-tuple-element.281.inner_ref.refs_2_, ...), custom_call_target="tpu_custom_call" | custom-call | flops 1 | bytes 1 | tf_op jit(solution)/shard_map/pallas_call | solution.py:211
  484.4 9.3 %shard_map.328 = bf16[1024,2048]{1,0:T(8,128)(2,1)} custom-call(s32[4]{0:T(128)S(1)} %broadcast_xor_fusion.1.order_ref, bf16[512,2048]{1,0:T(8,128)(2,1)} %get-tuple-element.340.hidden_ref.refs_0_, bf16[512,2048]{1,0:T(8,128)(2,1)} %get-tuple-element.341.hidden_ref.refs_1_, bf16[512,2048]{1,0:T(8,128)(2,1)} %get-tuple-element.306.gate_ref.refs_2_, ...), custom_call_target="tpu_custom_call" | custom-call | flops 1 | bytes 1 | tf_op jit(solution)/shard_map/pallas_call | solution.py:211
  502.0 10.7 %shard_map.330 = (bf16[2,256,1024]{2,1,0:T(8,128)(2,1)S(1)}, bf16[2,256,1024]{2,1,0:T(8,128)(2,1)}, bf16[2,256,1024]{2,1,0:T(8,128)(2,1)}, bf16[2,256,1024]{2,1,0:T(8,128)(2,1)}) custom-call(s32[4]{0:T(128)S(1)} %broadcast_xor_fusion.order_ref, bf16[512,2048]{1,0:T(8,128)(2,1)} %pad_maximum_fusion.3.back_ref.refs_0_, ...), custom_call_target="tpu_custom_call" | custom-call | flops 1 | bytes 1 | tf_op jit(solution)/shard_map/pallas_call | solution.py:211
  512.8 9.3 %shard_map.331 = bf16[1024,2048]{1,0:T(8,128)(2,1)} custom-call(s32[4]{0:T(128)S(1)} %broadcast_xor_fusion.1.order_ref, bf16[512,2048]{1,0:T(8,128)(2,1)} %get-tuple-element.340.hidden_ref.refs_0_, bf16[512,2048]{1,0:T(8,128)(2,1)} %get-tuple-element.341.hidden_ref.refs_1_, bf16[512,2048]{1,0:T(8,128)(2,1)} %get-tuple-element.307.upper_ref.refs_2_, ...), custom_call_target="tpu_custom_call" | custom-call | flops 1 | bytes 1 | tf_op jit(solution)/shard_map/pallas_call | solution.py:211
  525.4 10.7 %shard_map.332 = (bf16[2,256,1024]{2,1,0:T(8,128)(2,1)}, bf16[2,256,1024]{2,1,0:T(8,128)(2,1)}, bf16[2,256,1024]{2,1,0:T(8,128)(2,1)}, bf16[2,256,1024]{2,1,0:T(8,128)(2,1)}) custom-call(s32[4]{0:T(128)S(1)} %broadcast_xor_fusion.order_ref, bf16[512,2048]{1,0:T(8,128)(2,1)} %get-tuple-element.340.hidden_ref.refs_0_, ...), custom_call_target="tpu_custom_call" | custom-call | flops 1 | bytes 1 | tf_op jit(solution)/shard_map/pallas_call | solution.py:211
  562.2 10.5 %shard_map.334 = (bf16[2,256,1024]{2,1,0:T(8,128)(2,1)}, bf16[2,256,1024]{2,1,0:T(8,128)(2,1)}, bf16[2,256,1024]{2,1,0:T(8,128)(2,1)}, bf16[2,256,1024]{2,1,0:T(8,128)(2,1)}) custom-call(s32[4]{0:T(128)S(1)} %broadcast_xor_fusion.order_ref, bf16[512,2048]{1,0:T(8,128)(2,1)} %get-tuple-element.340.hidden_ref.refs_0_, ...), custom_call_target="tpu_custom_call" | custom-call | flops 1 | bytes 1 | tf_op jit(solution)/shard_map/pallas_call | solution.py:211
  580.8 19.9 %shard_map.336 = (f32[2,1024,512]{2,1,0:T(8,128)}, bf16[1024,512]{1,0:T(8,128)(2,1)}, f32[1024,128]{1,0:T(8,128)S(1)}, f32[2,512]{1,0:T(2,128)S(1)}) custom-call(bf16[3,1024,512]{2,1,0:T(8,128)(2,1)} %get-tuple-element.338.low_ref, bf16[1024,512]{1,0:T(8,128)(2,1)} %pad_maximum_fusion.8.back_ref, ...), custom_call_target="tpu_custom_call" | custom-call | flops 1 | bytes 1 | tf_op jit(solution)/shard_map/pallas_call | solution.py:211
  616.0 14.0 %shard_map.338 = (bf16[1024,1536]{1,0:T(8,128)(2,1)}, bf16[1024,2048]{1,0:T(8,128)(2,1)}) custom-call(f32[2,1024,512]{2,1,0:T(8,128)} %get-tuple-element.352.hats_ref, f32[1024,1536]{1,0:T(8,128)} %get-tuple-element.253.query_ref.key_ref.value_ref, f32[1024,1536]{1,0:T(8,128)} %get-tuple-element.253.query_ref.key_ref.value_ref, ...), custom_call_target="tpu_custom_call" | custom-call | flops 1 | bytes 1 | tf_op jit(solution)/shard_map/pallas_call | solution.py:211
  647.4 8.8 %shard_map.340 = (bf16[2,256,768]{2,1,0:T(8,128)(2,1)S(1)}, bf16[2,256,768]{2,1,0:T(8,128)(2,1)S(1)}, bf16[2,256,768]{2,1,0:T(8,128)(2,1)}, bf16[2,256,768]{2,1,0:T(8,128)(2,1)}) custom-call(s32[4]{0:T(128)S(1)} %broadcast_xor_fusion.order_ref, bf16[1024,2048]{1,0:T(8,128)(2,1)} %pad_maximum_fusion.1.tokens_ref.refs_0_, ...), custom_call_target="tpu_custom_call" | custom-call | flops 1 | bytes 1 | tf_op jit(solution)/shard_map/pallas_call | solution.py:211
  667.9 11.6 %collective-permute-done.84 = bf16[2,256,1024]{2,1,0:T(8,128)(2,1)S(1)} collective-permute-done((bf16[2,256,1024]{2,1,0:T(8,128)(2,1)}, bf16[2,256,1024]{2,1,0:T(8,128)(2,1)S(1)}, u32[]{:S(2)}, u32[]{:S(2)}) %collective-permute-start.84) | collective-permute-done | bytes 1048608 | tf_op jit(solution)/shard_map/ppermute | solution.py:146
  693.8 8.3 %collective-permute-done.81 = bf16[256,1024]{1,0:T(8,128)(2,1)S(1)} collective-permute-done((bf16[256,1024]{1,0:T(8,128)(2,1)S(1)}, bf16[256,1024]{1,0:T(8,128)(2,1)S(1)}, u32[]{:S(2)}, u32[]{:S(2)}) %collective-permute-start.81) | collective-permute-done | bytes 524320 | tf_op jit(solution)/shard_map/ppermute | solution.py:146
  720.7 12.6 %multiply_subtract_fusion = (f32[3,256,2048]{2,1,0:T(8,128)}, f32[3,256,2048]{2,1,0:T(8,128)}, f32[3,256,2048]{2,1,0:T(8,128)}) fusion(f32[3,256,2048]{2,1,0:T(8,128)S(1)} %bitcast.130, f32[1,256,2048]{2,1,0:T(8,128)S(1)} %maximum_bitcast_fusion.2, f32[1,256,2048]{2,1,0:T(8,128)S(1)} %maximum_bitcast_fusion.1, f32[1,256,2048]{2,1,0:T(8,128)} %maximum_bitcast_fusion, ...), kind=kLoop, calls=%fused_computation.5 | loop fusion | flops 25165824 | bytes 44040192 | tf_op jit(solution)/shard_map/sub | solution.py:48
  751.9 8.5 %collective-permute-done.96 = bf16[256,512]{1,0:T(8,128)(2,1)S(1)} collective-permute-done((bf16[256,512]{1,0:T(8,128)(2,1)S(1)}, bf16[256,512]{1,0:T(8,128)(2,1)S(1)}, u32[]{:S(2)}, u32[]{:S(2)}) %collective-permute-start.96) | collective-permute-done | bytes 262176 | tf_op jit(solution)/shard_map/ppermute | solution.py:113
  (446 shorter events, 369.2 us)
Async XLA Ops:
  7.2 230.5 %all-gather.2.cloned.1.call-start = ((), (), s32[]{:S(2)}) async-start(), calls=%async_computation.5 | async-start | bytes 28311552 | tf_op jit(solution)/shard_map/all_gather | solution.py:944
  7.2 41.1 %collective-permute-start.1 = (bf16[256,2048]{1,0:T(8,128)(2,1)}, bf16[256,2048]{1,0:T(8,128)(2,1)}, u32[]{:S(2)}, u32[]{:S(2)}) collective-permute-start(bf16[256,2048]{1,0:T(8,128)(2,1)} %tokens_ref.3), channel_id=1, source_target_pairs={{1,0},{2,1},{3,2},{5,4},{6,5},{7,6},{9,8},{10,9},{11,10},{13,12},{... | collective-permute-start | bytes 3145736 | tf_op jit(solution)/shard_map/ppermute | solution.py:69
  8.5 39.8 %collective-permute-start = (bf16[256,2048]{1,0:T(8,128)(2,1)}, bf16[256,2048]{1,0:T(8,128)(2,1)}, u32[]{:S(2)}, u32[]{:S(2)}) collective-permute-start(bf16[256,2048]{1,0:T(8,128)(2,1)} %tokens_ref.3), channel_id=1, source_target_pairs={{0,1},{1,2},{2,3},{4,5},{5,6},{6,7},{8,9},{9,10},{10,11},{12,13},{... | collective-permute-start | bytes 3145736 | tf_op jit(solution)/shard_map/ppermute | solution.py:69
  21.9 26.4 %collective-permute-start.3 = (bf16[256,1536]{1,0:T(8,128)(2,1)S(1)}, bf16[256,1536]{1,0:T(8,128)(2,1)S(1)}, u32[]{:S(2)}, u32[]{:S(2)}) collective-permute-start(bf16[256,1536]{1,0:T(8,128)(2,1)S(1)} %pad_maximum_fusion.9.refs_0_), channel_id=1, source_target_pairs={{0,16},{4,20},{8,24},{12,28},{16,0},{20,4},{24,8},{28,12},{1,17},{... | collective-permute-start | bytes 2359304 | tf_op jit(solution)/shard_map/ppermute | solution.py:146
  23.9 24.4 %collective-permute-start.2 = (bf16[256,1536]{1,0:T(8,128)(2,1)S(1)}, bf16[256,1536]{1,0:T(8,128)(2,1)S(1)}, u32[]{:S(2)}, u32[]{:S(2)}) collective-permute-start(bf16[256,1536]{1,0:T(8,128)(2,1)S(1)} %pad_maximum_fusion.9.refs_0_), channel_id=1, source_target_pairs={{0,8},{4,12},{8,0},{12,4},{16,24},{20,28},{24,16},{28,20},{1,9},{5... | collective-permute-start | bytes 2359304 | tf_op jit(solution)/shard_map/ppermute | solution.py:146
  48.4 264.8 %reduce-scatter.6.cloned.1.call-start = ((), (), s32[]{:S(2)}) async-start(), calls=%async_computation.6 | async-start | bytes 2621440 | tf_op jit(solution)/shard_map/reduce_scatter | solution.py:62
  158.2 34.8 %collective-permute-start.34 = (bf16[256,2048]{1,0:T(8,128)(2,1)S(1)}, bf16[256,2048]{1,0:T(8,128)(2,1)S(1)}, u32[]{:S(2)}, u32[]{:S(2)}) collective-permute-start(bf16[256,2048]{1,0:T(8,128)(2,1)S(1)} %pad_maximum_fusion.6.refs_0_), channel_id=1, source_target_pairs={{0,16},{4,20},{8,24},{12,28},{16,0},{20,4},{24,8},{28,12},{1,17},{... | collective-permute-start | bytes 3145736 | tf_op jit(solution)/shard_map/ppermute | solution.py:146
  160.0 34.6 %collective-permute-start.33 = (bf16[256,2048]{1,0:T(8,128)(2,1)S(1)}, bf16[256,2048]{1,0:T(8,128)(2,1)S(1)}, u32[]{:S(2)}, u32[]{:S(2)}) collective-permute-start(bf16[256,2048]{1,0:T(8,128)(2,1)S(1)} %pad_maximum_fusion.6.refs_0_), channel_id=1, source_target_pairs={{0,8},{4,12},{8,0},{12,4},{16,24},{20,28},{24,16},{28,20},{1,9},{5... | collective-permute-start | bytes 3145736 | tf_op jit(solution)/shard_map/ppermute | solution.py:146
  271.0 101.9 %reduce-scatter.8.cloned.1.call-start = ((), (), s32[]{:S(2)}) async-start(), calls=%async_computation.7 | async-start | bytes 2621440 | tf_op jit(solution)/shard_map/reduce_scatter | solution.py:62
  309.4 184.9 %reduce-scatter.10.cloned.1.call-start = ((), (), s32[]{:S(2)}) async-start(), calls=%async_computation.8 | async-start | bytes 2621440 | tf_op jit(solution)/shard_map/reduce_scatter | solution.py:62
  317.8 36.7 %collective-permute-start.50 = (bf16[128,2048]{1,0:T(8,128)(2,1)S(1)}, bf16[128,2048]{1,0:T(8,128)(2,1)S(1)}, u32[]{:S(2)}, u32[]{:S(2)}) collective-permute-start(bf16[128,2048]{1,0:T(8,128)(2,1)S(1)} %get-tuple-element.285), channel_id=1, source_target_pairs={{1,0},{2,1},{3,2},{5,4},{6,5},{7,6},{9,8},{10,9},{11,10},{13,12},{... | collective-permute-start | bytes 1572872 | tf_op jit(solution)/shard_map/ppermute | solution.py:69
  319.1 36.7 %collective-permute-start.48 = (bf16[128,2048]{1,0:T(8,128)(2,1)S(1)}, bf16[128,2048]{1,0:T(8,128)(2,1)S(1)}, u32[]{:S(2)}, u32[]{:S(2)}) collective-permute-start(bf16[128,2048]{1,0:T(8,128)(2,1)S(1)} %get-tuple-element.285), channel_id=1, source_target_pairs={{0,1},{1,2},{2,3},{4,5},{5,6},{6,7},{8,9},{9,10},{10,11},{12,13},{... | collective-permute-start | bytes 1572872 | tf_op jit(solution)/shard_map/ppermute | solution.py:69
  445.5 95.9 %reduce-scatter.12.cloned.1.call-start = ((), (), s32[]{:S(2)}) async-start(), calls=%async_computation.9 | async-start | bytes 2621440 | tf_op jit(solution)/shard_map/reduce_scatter | solution.py:62
  493.7 31.7 %collective-permute-start.61 = (bf16[1024,2048]{1,0:T(8,128)(2,1)}, bf16[1024,2048]{1,0:T(8,128)(2,1)}, u32[]{:S(2)}, u32[]{:S(2)}) collective-permute-start(bf16[1024,2048]{1,0:T(8,128)(2,1)} %shard_map.328), channel_id=1, source_target_pairs={{0,4},{4,0},{8,12},{12,8},{16,20},{20,16},{24,28},{28,24},{1,5},{5... | collective-permute-start | bytes 12582920 | tf_op jit(solution)/shard_map/ppermute | solution.py:146
  494.2 275.5 %reduce-scatter.14.cloned.1.call-start = ((), (), s32[]{:S(2)}) async-start(), calls=%async_computation.10 | async-start | bytes 5242880 | tf_op jit(solution)/shard_map/reduce_scatter | solution.py:62
  522.1 29.1 %collective-permute-start.67 = (bf16[1024,2048]{1,0:T(8,128)(2,1)}, bf16[1024,2048]{1,0:T(8,128)(2,1)}, u32[]{:S(2)}, u32[]{:S(2)}) collective-permute-start(bf16[1024,2048]{1,0:T(8,128)(2,1)} %shard_map.331), channel_id=1, source_target_pairs={{0,4},{4,0},{8,12},{12,8},{16,20},{20,16},{24,28},{28,24},{1,5},{5... | collective-permute-start | bytes 12582920 | tf_op jit(solution)/shard_map/ppermute | solution.py:146
  522.6 51.7 %collective-permute-start.65 = (bf16[2,256,1024]{2,1,0:T(8,128)(2,1)}, bf16[2,256,1024]{2,1,0:T(8,128)(2,1)}, u32[]{:S(2)}, u32[]{:S(2)}) collective-permute-start(bf16[2,256,1024]{2,1,0:T(8,128)(2,1)} %copy-done.9), channel_id=1, source_target_pairs={{0,8},{4,12},{8,0},{12,4},{16,24},{20,28},{24,16},{28,20},{1,9},{5... | collective-permute-start | bytes 3145736 | tf_op jit(solution)/shard_map/ppermute | solution.py:146
  524.0 50.3 %collective-permute-start.66 = (bf16[2,256,1024]{2,1,0:T(8,128)(2,1)}, bf16[2,256,1024]{2,1,0:T(8,128)(2,1)}, u32[]{:S(2)}, u32[]{:S(2)}) collective-permute-start(bf16[2,256,1024]{2,1,0:T(8,128)(2,1)} %get-tuple-element.325), channel_id=1, source_target_pairs={{0,16},{4,20},{8,24},{12,28},{16,0},{20,4},{24,8},{28,12},{1,17},{... | collective-permute-start | bytes 3145736 | tf_op jit(solution)/shard_map/ppermute | solution.py:146
  574.3 30.9 %collective-permute-start.73 = (bf16[1024,2048]{1,0:T(8,128)(2,1)}, bf16[1024,2048]{1,0:T(8,128)(2,1)}, u32[]{:S(2)}, u32[]{:S(2)}) collective-permute-start(bf16[1024,2048]{1,0:T(8,128)(2,1)} %shard_map.335), channel_id=1, source_target_pairs={{0,4},{4,0},{8,12},{12,8},{16,20},{20,16},{24,28},{28,24},{1,5},{5... | collective-permute-start | bytes 12582920 | tf_op jit(solution)/shard_map/ppermute | solution.py:146
  574.4 26.4 %collective-permute-start.68 = (bf16[2,256,1024]{2,1,0:T(8,128)(2,1)}, bf16[2,256,1024]{2,1,0:T(8,128)(2,1)}, u32[]{:S(2)}, u32[]{:S(2)}) collective-permute-start(bf16[2,256,1024]{2,1,0:T(8,128)(2,1)} %get-tuple-element.355), channel_id=1, source_target_pairs={{0,8},{4,12},{8,0},{12,4},{16,24},{20,28},{24,16},{28,20},{1,9},{5... | collective-permute-start | bytes 3145736 | tf_op jit(solution)/shard_map/ppermute | solution.py:146
  575.9 26.3 %collective-permute-start.69 = (bf16[2,256,1024]{2,1,0:T(8,128)(2,1)}, bf16[2,256,1024]{2,1,0:T(8,128)(2,1)}, u32[]{:S(2)}, u32[]{:S(2)}) collective-permute-start(bf16[2,256,1024]{2,1,0:T(8,128)(2,1)} %get-tuple-element.356), channel_id=1, source_target_pairs={{0,16},{4,20},{8,24},{12,28},{16,0},{20,4},{24,8},{28,12},{1,17},{... | collective-permute-start | bytes 3145736 | tf_op jit(solution)/shard_map/ppermute | solution.py:146
  577.4 52.6 %collective-permute-start.76 = (bf16[2,256,1024]{2,1,0:T(8,128)(2,1)}, bf16[2,256,1024]{2,1,0:T(8,128)(2,1)}, u32[]{:S(2)}, u32[]{:S(2)}) collective-permute-start(bf16[2,256,1024]{2,1,0:T(8,128)(2,1)} %get-tuple-element.381), channel_id=1, source_target_pairs={{0,8},{4,12},{8,0},{12,4},{16,24},{20,28},{24,16},{28,20},{1,9},{5... | collective-permute-start | bytes 3145736 | tf_op jit(solution)/shard_map/ppermute | solution.py:146
  577.9 52.0 %collective-permute-start.77 = (bf16[2,256,1024]{2,1,0:T(8,128)(2,1)}, bf16[2,256,1024]{2,1,0:T(8,128)(2,1)}, u32[]{:S(2)}, u32[]{:S(2)}) collective-permute-start(bf16[2,256,1024]{2,1,0:T(8,128)(2,1)} %get-tuple-element.382), channel_id=1, source_target_pairs={{0,16},{4,20},{8,24},{12,28},{16,0},{20,4},{24,8},{28,12},{1,17},{... | collective-permute-start | bytes 3145736 | tf_op jit(solution)/shard_map/ppermute | solution.py:146
  645.3 34.3 %collective-permute-start.84 = (bf16[2,256,1024]{2,1,0:T(8,128)(2,1)}, bf16[2,256,1024]{2,1,0:T(8,128)(2,1)S(1)}, u32[]{:S(2)}, u32[]{:S(2)}) collective-permute-start(bf16[2,256,1024]{2,1,0:T(8,128)(2,1)} %get-tuple-element.399), channel_id=1, source_target_pairs={{0,8},{4,12},{8,0},{12,4},{16,24},{20,28},{24,16},{28,20},{1,9},{5... | collective-permute-start | bytes 3145736 | tf_op jit(solution)/shard_map/ppermute | solution.py:146
  646.8 35.8 %collective-permute-start.85 = (bf16[2,256,1024]{2,1,0:T(8,128)(2,1)}, bf16[2,256,1024]{2,1,0:T(8,128)(2,1)S(1)}, u32[]{:S(2)}, u32[]{:S(2)}) collective-permute-start(bf16[2,256,1024]{2,1,0:T(8,128)(2,1)} %get-tuple-element.400), channel_id=1, source_target_pairs={{0,16},{4,20},{8,24},{12,28},{16,0},{20,4},{24,8},{28,12},{1,17},{... | collective-permute-start | bytes 3145736 | tf_op jit(solution)/shard_map/ppermute | solution.py:146
  659.0 31.8 %collective-permute-start.83 = (bf16[256,1024]{1,0:T(8,128)(2,1)S(1)}, bf16[256,1024]{1,0:T(8,128)(2,1)S(1)}, u32[]{:S(2)}, u32[]{:S(2)}) collective-permute-start(bf16[256,1024]{1,0:T(8,128)(2,1)S(1)} %fusion.8), channel_id=1, source_target_pairs={{0,8},{4,12},{8,0},{12,4},{16,24},{20,28},{24,16},{28,20},{1,9},{5... | collective-permute-start | bytes 1572872 | tf_op jit(solution)/shard_map/ppermute | solution.py:146
  661.8 30.4 %collective-permute-start.82 = (bf16[256,1024]{1,0:T(8,128)(2,1)S(1)}, bf16[256,1024]{1,0:T(8,128)(2,1)S(1)}, u32[]{:S(2)}, u32[]{:S(2)}) collective-permute-start(bf16[256,1024]{1,0:T(8,128)(2,1)S(1)} %fusion.7), channel_id=1, source_target_pairs={{0,16},{4,20},{8,24},{12,28},{16,0},{20,4},{24,8},{28,12},{1,17},{... | collective-permute-start | bytes 1572872 | tf_op jit(solution)/shard_map/ppermute | solution.py:146
  664.6 37.4 %collective-permute-start.81 = (bf16[256,1024]{1,0:T(8,128)(2,1)S(1)}, bf16[256,1024]{1,0:T(8,128)(2,1)S(1)}, u32[]{:S(2)}, u32[]{:S(2)}) collective-permute-start(bf16[256,1024]{1,0:T(8,128)(2,1)S(1)} %fusion.6), channel_id=1, source_target_pairs={{0,8},{4,12},{8,0},{12,4},{16,24},{20,28},{24,16},{28,20},{1,9},{5... | collective-permute-start | bytes 1572872 | tf_op jit(solution)/shard_map/ppermute | solution.py:146
  682.7 50.6 %collective-permute-start.88 = (bf16[2,256,768]{2,1,0:T(8,128)(2,1)S(1)}, bf16[2,256,768]{2,1,0:T(8,128)(2,1)}, u32[]{:S(2)}, u32[]{:S(2)}) collective-permute-start(bf16[2,256,768]{2,1,0:T(8,128)(2,1)S(1)} %get-tuple-element.389), channel_id=1, source_target_pairs={{0,8},{4,12},{8,0},{12,4},{16,24},{20,28},{24,16},{28,20},{1,9},{5... | collective-permute-start | bytes 2359304 | tf_op jit(solution)/shard_map/ppermute | solution.py:146
  690.8 42.5 %collective-permute-start.89 = (bf16[2,256,768]{2,1,0:T(8,128)(2,1)S(1)}, bf16[2,256,768]{2,1,0:T(8,128)(2,1)}, u32[]{:S(2)}, u32[]{:S(2)}) collective-permute-start(bf16[2,256,768]{2,1,0:T(8,128)(2,1)S(1)} %get-tuple-element.390), channel_id=1, source_target_pairs={{0,16},{4,20},{8,24},{12,28},{16,0},{20,4},{24,8},{28,12},{1,17},{... | collective-permute-start | bytes 2359304 | tf_op jit(solution)/shard_map/ppermute | solution.py:146
  692.3 27.2 %collective-permute-start.92 = (f32[4,256]{1,0:T(4,128)S(1)}, f32[4,256]{1,0:T(4,128)S(1)}, u32[]{:S(2)}, u32[]{:S(2)}) collective-permute-start(f32[4,256]{1,0:T(4,128)S(1)} %get-tuple-element.480), channel_id=1, source_target_pairs={{0,24},{4,28},{8,16},{12,20},{16,8},{20,12},{24,0},{28,4},{1,25},{... | collective-permute-start | bytes 12296 | tf_op jit(solution)/shard_map/ppermute | solution.py:146
  703.5 29.8 %collective-permute-start.90 = (f32[4,256]{1,0:T(4,128)S(1)}, f32[4,256]{1,0:T(4,128)S(1)}, u32[]{:S(2)}, u32[]{:S(2)}) collective-permute-start(f32[4,256]{1,0:T(4,128)S(1)} %get-tuple-element.482), channel_id=1, source_target_pairs={{0,8},{4,12},{8,0},{12,4},{16,24},{20,28},{24,16},{28,20},{1,9},{5... | collective-permute-start | bytes 12296 | tf_op jit(solution)/shard_map/ppermute | solution.py:146
  (132 other events, 1567.9 us)
Sparse Core Ops, SparseCore 0:
  48.5 141.2 all-gather.1
  271.1 41.9 reduce-scatter.5
  315.5 57.2 reduce-scatter.7
  445.6 47.5 reduce-scatter.9
  495.5 45.8 reduce-scatter.11
  645.4 75.4 reduce-scatter.13
